TPU v7x, 32 devices: a whole 2x2x4 slice. The times are simulated.
32 devices in a mesh: rep: 4 (over y, x), mp: 8 (over z, core).
Axes of the slice: x: 2, y: 2, z: 4, core: 2. Of those that a mesh axis runs over, the one named last changes fastest.
Arguments:
- dense_feats: bfloat16 [4096, 13], P(('rep', 'mp')), may hold values from -6 to 6
- bag_counts: int32 [4096, 8, 64], P('rep', 'mp'), may hold values from 0 to 2
- emb_rows: bfloat16 [8, 64, 256], P('mp'), may hold values from -0.625 to 0.625
- v_emb: bfloat16 [2048, 256], P('mp'), may hold values from -0.125 to 0.125
- u_emb: bfloat16 [256, 2048], P(None, 'mp'), may hold values from -0.375 to 0.375
- b_emb: bfloat16 [2048], P('mp'), may hold values from -3 to 3
- v_bot: bfloat16 [256, 256], replicated, may hold values from -0.375 to 0.375
- u_bot: bfloat16 [256, 256], replicated, may hold values from -0.375 to 0.375
- b_bot: bfloat16 [256], replicated, may hold values from -3 to 3
- w_first: bfloat16 [13, 1024], replicated, may hold values from -1.75 to 1.75
- b_first: bfloat16 [1024], replicated, may hold values from -3 to 3
- w_second: bfloat16 [1024, 256], replicated, may hold values from -0.1875 to 0.1875
- b_second: bfloat16 [256], replicated, may hold values from -3 to 3
- cot_cross: bfloat16 [4096, 2048], P(('rep', 'mp')), may hold values from -12 to 12
- cot_bottom: bfloat16 [4096, 256], P(('rep', 'mp')), may hold values from -6 to 6
Outputs:
- cross_emb: bfloat16 [4096, 2048], P(('rep', 'mp'))
- cross_bot: bfloat16 [4096, 256], P(('rep', 'mp'))
- grad_table: bfloat16 [8, 64, 256], P('mp')
- grad_v_emb: bfloat16 [2048, 256], P('mp')
- grad_u_emb: bfloat16 [256, 2048], P(None, 'mp')
- grad_b_emb: bfloat16 [2048], P('mp')
- grad_v_bot: bfloat16 [256, 256], replicated
- grad_u_bot: bfloat16 [256, 256], replicated
- grad_b_bot: bfloat16 [256], replicated
- grad_w_first: bfloat16 [13, 1024], replicated
- grad_b_first: bfloat16 [1024], replicated
- grad_w_second: bfloat16 [1024, 256], replicated
- grad_b_second: bfloat16 [256], replicated
Inputs may be any that keep to these rules, and one draw needn't show every extreme that they name: bag_counts[s, t, j] is how often row j of table t occurs in the bag of sample s.
All inputs are finite; a program needn't handle non-finite values.
Results may differ from a plain program's by a relative error of at most 0.029.
Values may be sent and summed in bfloat16 or wider, within the bound.
No kernel may reach another device: no remote copies, remote signals or barrier semaphores. Data moves between devices by JAX's collectives and lax.ppermute only.
A program may use at most 64 MiB of HBM per device.

v0:
```python
import math

import jax
import jax.numpy as jnp
from jax import lax
from jax.sharding import PartitionSpec as P


def silu_slope(inputs):
    gate_value = jax.nn.sigmoid(inputs)
    return gate_value * (1.0 + inputs * (1.0 - gate_value))


def contract_rows(left_side, right_side):
    return lax.dot_general(
        left_side, right_side, (((0,), (0,)), ((), ())), preferred_element_type=jnp.float32
    )


def contract_cols(left_side, right_side):
    return lax.dot_general(
        left_side, right_side, (((1,), (1,)), ((), ())), preferred_element_type=jnp.float32
    )


def local(
    dense_feats,
    bag_counts,
    emb_rows,
    v_emb,
    u_emb,
    b_emb,
    v_bot,
    u_bot,
    b_bot,
    w_first,
    b_first,
    w_second,
    b_second,
    cot_cross,
    cot_bottom,
):
    group_size = lax.axis_size("mp")
    own_rows = dense_feats.shape[0]
    first_row = lax.axis_index("mp") * own_rows
    grad_scale = 1.0 / math.sqrt(own_rows * group_size * lax.axis_size("rep"))
    counts = bag_counts[:, 0, :].astype(jnp.bfloat16)
    pooled = jnp.dot(counts, emb_rows[0], preferred_element_type=jnp.float32).astype(jnp.bfloat16)
    partial_value = jnp.dot(pooled, v_emb, preferred_element_type=jnp.float32)
    first_pre = jnp.dot(dense_feats, w_first, preferred_element_type=jnp.float32) + b_first.astype(
        jnp.float32
    )
    first_act = jax.nn.silu(first_pre).astype(jnp.bfloat16)
    second_pre = jnp.dot(first_act, w_second, preferred_element_type=jnp.float32) + b_second.astype(
        jnp.float32
    )
    bottom = jax.nn.silu(second_pre).astype(jnp.bfloat16)
    own_part = lax.dynamic_slice_in_dim(partial_value, first_row, own_rows, 0) + jnp.dot(
        bottom, v_bot, preferred_element_type=jnp.float32
    )
    partial_value = lax.dynamic_update_slice_in_dim(partial_value, own_part, first_row, 0)
    low_rank = lax.psum(partial_value.astype(jnp.bfloat16), "mp")
    lift_emb = jnp.dot(low_rank, u_emb, preferred_element_type=jnp.float32) + b_emb.astype(
        jnp.float32
    )
    pooled_full = pooled.astype(jnp.float32)
    cross_local = (pooled_full * (lift_emb + 1.0)).astype(jnp.bfloat16)
    cross_emb = lax.all_to_all(cross_local, "mp", split_axis=0, concat_axis=1, tiled=True)
    own_low = lax.dynamic_slice_in_dim(low_rank, first_row, own_rows, 0)
    lift_bottom = jnp.dot(own_low, u_bot, preferred_element_type=jnp.float32) + b_bot.astype(
        jnp.float32
    )
    bottom_full = bottom.astype(jnp.float32)
    cross_bot = (bottom_full * (lift_bottom + 1.0)).astype(jnp.bfloat16)
    cot_rows = lax.all_to_all(cot_cross, "mp", split_axis=1, concat_axis=0, tiled=True).astype(
        jnp.float32
    )
    d_lift = cot_rows * pooled_full
    d_lift_round = d_lift.astype(jnp.bfloat16)
    own_back = lax.psum_scatter(
        contract_cols(d_lift_round, u_emb).astype(jnp.bfloat16),
        "mp",
        scatter_dimension=0,
        tiled=True,
    ).astype(jnp.float32)
    cot_low = cot_bottom.astype(jnp.float32)
    d_bottom_lift = cot_low * bottom_full
    d_bottom_round = d_bottom_lift.astype(jnp.bfloat16)
    own_d_low = (own_back + contract_cols(d_bottom_round, u_bot)).astype(jnp.bfloat16)
    d_low = lax.all_gather(own_d_low, "mp", axis=0, tiled=True)
    d_pooled = (cot_rows * (lift_emb + 1.0) + contract_cols(d_low, v_emb)).astype(jnp.bfloat16)
    grad_table = grad_scale * contract_rows(counts, d_pooled)
    grad_v = grad_scale * contract_rows(pooled, d_low)
    grad_u = grad_scale * contract_rows(low_rank, d_lift_round)
    grad_b = grad_scale * jnp.sum(d_lift, axis=0)
    d_bottom = cot_low * (lift_bottom + 1.0) + contract_cols(own_d_low, v_bot)
    grad_vb = grad_scale * contract_rows(bottom, own_d_low)
    grad_ub = grad_scale * contract_rows(own_low, d_bottom_round)
    grad_bb = grad_scale * jnp.sum(d_bottom_lift, axis=0)
    d_second = d_bottom * silu_slope(second_pre)
    d_second_round = d_second.astype(jnp.bfloat16)
    grad_ws = grad_scale * contract_rows(first_act, d_second_round)
    grad_bs = grad_scale * jnp.sum(d_second, axis=0)
    d_first = contract_cols(d_second_round, w_second) * silu_slope(first_pre)
    d_first_round = d_first.astype(jnp.bfloat16)
    grad_wf = grad_scale * contract_rows(dense_feats, d_first_round)
    grad_bf = grad_scale * jnp.sum(d_first, axis=0)
    dense_sums = lax.psum(
        (grad_wf, grad_bf, grad_ws, grad_bs, grad_vb, grad_ub, grad_bb), ("rep", "mp")
    )
    table_sums = (
        lax.psum(grad_table.astype(jnp.bfloat16), "rep").astype(jnp.float32),
        lax.psum(grad_v.astype(jnp.bfloat16), "rep").astype(jnp.float32),
        lax.psum(grad_u.astype(jnp.bfloat16), "rep").astype(jnp.float32),
        lax.psum(grad_b.astype(jnp.bfloat16), "rep").astype(jnp.float32),
    )
    return (
        cross_emb,
        cross_bot,
        table_sums[0][None].astype(jnp.bfloat16),
        table_sums[1].astype(jnp.bfloat16),
        table_sums[2].astype(jnp.bfloat16),
        table_sums[3].astype(jnp.bfloat16),
        dense_sums[4].astype(jnp.bfloat16),
        dense_sums[5].astype(jnp.bfloat16),
        dense_sums[6].astype(jnp.bfloat16),
        dense_sums[0].astype(jnp.bfloat16),
        dense_sums[1].astype(jnp.bfloat16),
        dense_sums[2].astype(jnp.bfloat16),
        dense_sums[3].astype(jnp.bfloat16),
    )


def solution(mesh):
    return jax.shard_map(
        local,
        mesh=mesh,
        in_specs=(
            P(("rep", "mp"), None),
            P("rep", "mp", None),
            P("mp", None, None),
            P("mp", None),
            P(None, "mp"),
            P("mp"),
            P(),
            P(),
            P(),
            P(),
            P(),
            P(),
            P(),
            P(("rep", "mp"), None),
            P(("rep", "mp"), None),
        ),
        out_specs=(
            P(("rep", "mp"), None),
            P(("rep", "mp"), None),
            P("mp", None, None),
            P("mp", None),
            P(None, "mp"),
            P("mp"),
            P(),
            P(),
            P(),
            P(),
            P(),
            P(),
            P(),
        ),
        check_vma=False,
    )
```

profile of v0, /device:TPU:0, one launch (start us, length us, event | category | flops | bytes accessed | tf_op | source)
XLA Modules:
  0.0 220.0 jit_solution(4229316802180316235)
XLA Ops:
  7.2 1.9 copy.33
  9.1 6.5 %all-to-all-start.1 = ((bf16[128,8,256]{2,0,1:T(8,128)(2,1)}), bf16[128,8,256]{2,0,1:T(8,128)(2,1)S(1)}, u32[]{:S(2)}, u32[]{:S(2)}) async-start(bf16[128,8,256]{2,0,1:T(8,128)(2,1)} %bitcast.58), calls=%async_computation.1 | async-start | bytes 1048576 | tf_op jit(solution)/shard_map/all_to_all | solution.py:75
  16.3 0.7 copy-done.16
  17.9 0.9 fusion.20
  20.9 0.8 convert_element_type.134
  22.4 57.1 %all-reduce.7.cloned.1.call-done = bf16[1024,256]{1,0:T(8,128)(2,1)} async-done(((bf16[1024,256]{1,0:T(8,128)(2,1)}), bf16[1024,256]{1,0:T(8,128)(2,1)}) %all-reduce.7.cloned.1.call-update) | async-done | bytes 524304 | tf_op jit(solution)/shard_map/psum | solution.py:62
  79.5 2.3 %bitcast_multiply_fusion = (f32[1024,256]{1,0:T(8,128)S(1)}, bf16[1024,256]{1,0:T(8,128)(2,1)}, bf16[1024,256]{1,0:T(8,128)(2,1)S(1)}, f32[256]{0:T(256)S(1)}) fusion(bf16[128,8,256]{2,0,1:T(8,128)(2,1)S(1)} %all-to-all-done.1, bf16[1024,256]{1,0:T(8,128)(2,1)S(1)} %convolution_convert_fusion.1, f32[256]{0:T(256)S(1)} %convert_element_type.135, ...), kind=kOutput, calls=%fused_computation.33 | convolution fusion | flops 136838912 | bytes 3803136 | tf_op jit(solution)/shard_map/dot_general | solution.py:63
  81.8 2.0 convolution_convert_fusion
  84.6 3.5 %all-to-all-start = ((bf16[8,128,256]{2,1,0:T(8,128)(2,1)}), bf16[8,128,256]{2,1,0:T(8,128)(2,1)S(1)}, u32[]{:S(2)}, u32[]{:S(2)}) async-start(bf16[8,128,256]{2,1,0:T(8,128)(2,1)} %bitcast.2), calls=%async_computation | async-start | bytes 1048576 | tf_op jit(solution)/shard_map/all_to_all | solution.py:68
  88.1 1.8 convolution_multiply_fusion.2
  89.9 1.8 fusion.17
  91.7 1.0 fusion.4
  92.7 13.7 %all-to-all-done = bf16[8,128,256]{2,1,0:T(8,128)(2,1)S(1)} async-done(((bf16[8,128,256]{2,1,0:T(8,128)(2,1)}), bf16[8,128,256]{2,1,0:T(8,128)(2,1)S(1)}, u32[]{:S(2)}, u32[]{:S(2)}) %all-to-all-start) | async-done | bytes 524320 | tf_op jit(solution)/shard_map/all_to_all | solution.py:68
  106.4 0.8 copy.31
  107.3 7.9 %reduce-scatter.2.cloned.1.call-done = bf16[128,256]{1,0:T(8,128)(2,1)} async-done(((bf16[1024,256]{1,0:T(8,128)(2,1)}), bf16[128,256]{1,0:T(8,128)(2,1)}) %reduce-scatter.2.cloned.1.call-update) | async-done | bytes 65552 | tf_op jit(solution)/shard_map/reduce_scatter | solution.py:80
  115.2 1.0 fusion.8
  116.3 15.0 %all_gather.3 = bf16[1024,256]{1,0:T(8,128)(2,1)S(1)} all-gather(bf16[128,256]{1,0:T(8,128)(2,1)S(1)} %fusion.8), channel_id=1, replica_groups=mesh['rep'=4,'mp'=8] {'mp'}, dimensions={0}, use_global_device_ids=true | all-gather | bytes 589824 | tf_op jit(solution)/shard_map/all_gather | solution.py:90
  131.5 0.7 copy-done.12
  133.0 1.4 convolution_multiply_fusion
  134.3 1.0 fusion.3
  135.5 0.9 copy-done.8
  137.0 17.4 %all-reduce.1 = (bf16[1,64,256]{2,1,0:T(8,128)(2,1)}, bf16[256]{0:T(256)(128)(2,1)}) all-reduce(bf16[1,64,256]{2,1,0:T(8,128)(2,1)S(1)} %fusion.12, bf16[256]{0:T(256)(128)(2,1)S(1)} %multiply_convert_fusion.2), channel_id=1, replica_groups=mesh['rep'=4,'mp'=8] {'rep'}, use_global_device_ids=true, to_apply=%region_2.3 | all-reduce | flops 16640 | bytes 66560 | tf_op jit(solution)/shard_map/psum | solution.py:112
  154.4 56.8 %all-reduce.10 = (bf16[256,256]{1,0:T(8,128)(2,1)}, bf16[256,256]{1,0:T(8,128)(2,1)}, bf16[256]{0:T(256)(128)(2,1)}, bf16[13,1024]{1,0:T(8,128)(2,1)}, bf16[1024...) all-reduce(f32[256,256]{1,0:T(8,128)S(1)} %convolution_multiply_fus, ...), channel_id=1, replica_groups=mesh['rep'=4,'mp'=8] {'rep','mp'}, use_global_device_ids=true, to_apply=%region_7.8 | all-reduce | flops 408064 | bytes 2448384 | tf_op jit(solution)/shard_map/psum | solution.py:108
  211.2 1.6 copy.52
  (67 shorter events, 7.4 us)
Async XLA Ops:
  7.2 10.1 %copy-start = (bf16[1024,256]{1,0:T(8,128)(2,1)S(1)}, bf16[1024,256]{1,0:T(8,128)(2,1)}, u32[]{:S(2)}) copy-start(bf16[1024,256]{1,0:T(8,128)(2,1)} %param.26) | copy-start | bytes 1572868
  9.1 6.5 %copy-start.18 = (bf16[256]{0:T(256)(128)(2,1)S(1)}, bf16[256]{0:T(256)(128)(2,1)}, u32[]{:S(2)}) copy-start(bf16[256]{0:T(256)(128)(2,1)} %param.27) | copy-start | bytes 1540
  9.1 7.2 %copy-start.14 = (bf16[13,1024]{1,0:T(8,128)(2,1)S(1)}, bf16[13,1024]{1,0:T(8,128)(2,1)}, u32[]{:S(2)}) copy-start(bf16[13,1024]{1,0:T(8,128)(2,1)} %param.24) | copy-start | bytes 79876
  9.1 70.4 %all-to-all-start.1 = ((bf16[128,8,256]{2,0,1:T(8,128)(2,1)}), bf16[128,8,256]{2,0,1:T(8,128)(2,1)S(1)}, u32[]{:S(2)}, u32[]{:S(2)}) async-start(bf16[128,8,256]{2,0,1:T(8,128)(2,1)} %bitcast.58), calls=%async_computation.1 | async-start | bytes 1048576 | tf_op jit(solution)/shard_map/all_to_all | solution.py:75
  15.6 64.0 %all-reduce.7.cloned.1.call-start = ((), (), s32[]{:S(2)}) async-start(), calls=%async_computation.3 | async-start | bytes 1048576 | tf_op jit(solution)/shard_map/psum | solution.py:62
  16.3 0.7 copy-start.16
  17.0 0.8 copy-start.9
  17.8 1.0 copy-start.4
  17.8 1.1 copy-start.1
  17.8 1.1 copy-start.15
  19.0 0.9 copy-start.7
  19.9 0.9 copy-start.11
  21.8 93.4 %reduce-scatter.2.cloned.1.call-start = ((), (), s32[]{:S(2)}) async-start(), calls=%async_computation.4 | async-start | bytes 589824 | tf_op jit(solution)/shard_map/reduce_scatter | solution.py:80
  84.6 21.9 %all-to-all-start = ((bf16[8,128,256]{2,1,0:T(8,128)(2,1)}), bf16[8,128,256]{2,1,0:T(8,128)(2,1)S(1)}, u32[]{:S(2)}, u32[]{:S(2)}) async-start(bf16[8,128,256]{2,1,0:T(8,128)(2,1)} %bitcast.2), calls=%async_computation | async-start | bytes 1048576 | tf_op jit(solution)/shard_map/all_to_all | solution.py:68
  88.1 123.2 %all-reduce.9.cloned.1.call-start = ((), (), s32[]{:S(2)}) async-start(), calls=%async_computation.5 | async-start | bytes 524288 | tf_op jit(solution)/shard_map/psum | solution.py:113
  88.1 3.6 %copy-start.3 = (bf16[1024,256]{1,0:T(8,128)(2,1)S(1)}, bf16[1024,256]{1,0:T(8,128)(2,1)}, u32[]{:S(2)}) copy-start(bf16[1024,256]{1,0:T(8,128)(2,1)} %all-reduce.7.cloned.1.call-done) | copy-start | bytes 1572868
  106.4 8.8 %copy-start.6 = (bf16[256,256]{1,0:T(8,128)(2,1)S(1)}, bf16[256,256]{1,0:T(8,128)(2,1)}, u32[]{:S(2)}) copy-start(bf16[256,256]{1,0:T(8,128)(2,1)} %param.22) | copy-start | bytes 393220
  131.3 0.9 copy-start.12
  131.3 1.0 copy-start.13
  131.3 1.0 copy-start.21
  131.5 1.1 copy-start.5
  135.5 0.9 copy-start.8
  136.4 18.0 %copy-start.2 = (f32[256,256]{1,0:T(8,128)S(1)}, f32[256,256]{1,0:T(8,128)}, u32[]{:S(2)}) copy-start(f32[256,256]{1,0:T(8,128)} %convolution_multiply_fusion.2) | copy-start | bytes 786436
  211.2 1.6 copy-start.10
  (3 other events, 2.0 us)
Sparse Core Ops, SparseCore 0:
  21.9 57.5 all-reduce.6
  84.0 31.1 reduce-scatter.1
  135.6 41.6 all-reduce.8
where the time goes:
time: 221 us; the launch traced here: 220 us
  blocking collectives  89.3 us (40%)
  waiting for transfers between devices  78.8 us (36%)
  matrix products  15.8 us (7%)
  between operations  13.9 us (6%)
  local copies, waits for them, and re-layouts  11.3 us (5%)
  starting transfers between devices  10.1 us (5%)
    psum x1, waiting for transfers between devices, local(): low_rank = lax.psum(partial_value.astype(jnp.bfloat16), 'mp')  57.1 us
    psum x1, blocking collectives, local(): lax.psum((grad_wf, grad_bf, grad_ws, grad_bs, grad_vb, grad_ub, grad_bb),...  56.8 us
    psum x1, blocking collectives, local(): lax.psum(grad_table.astype(jnp.bfloat16), 'rep').astype(jnp.float32)  17.4 us
    all_gather x1, blocking collectives, local(): d_low = lax.all_gather(own_d_low, 'mp', axis=0, tiled=True)  15 us
    all_to_all x1, waiting for transfers between devices, local(): lax.all_to_all(cross_local, 'mp', split_axis=0, concat_axis=1, tiled=True)  13.7 us
    unnamed x46, local copies, waits for them, and re-layouts  8.5 us
    reduce_scatter x1, waiting for transfers between devices, local(): lax.psum_scatter(contract_cols(d_lift_round, u_emb).astype(jnp.bfloat16),...  7.95 us
    all_to_all x1, starting transfers between devices, local(): lax.all_to_all(cot_cross, 'mp', split_axis=1, concat_axis=0, tiled=True)  6.46 us
  transfers between devices with their start and end apart: 5, of which 3 were waited for; matrix products, arithmetic and copies ran while one was open for 4% of the time, Pallas kernels for 0%

commit v1 on v0

v1 whole, which is shorter than its diff:
```python
import math

import jax
import jax.numpy as jnp
from jax import lax
from jax.experimental import pallas as pl
from jax.experimental.pallas import tpu as pltpu
from jax.sharding import Mesh
from jax.sharding import PartitionSpec as P

BF = jnp.bfloat16
F32 = jnp.float32
TILE = 16


def round_up(value, unit):
    return -(-value // unit) * unit


def silu_parts(inputs):
    gate_value = jax.nn.sigmoid(inputs)
    return inputs * gate_value, gate_value * (1.0 + inputs * (1.0 - gate_value))


def mul_nn(left, right):
    return lax.dot_general(left, right, (((1,), (0,)), ((), ())), preferred_element_type=F32)


def mul_tn(left, right):
    return lax.dot_general(left, right, (((0,), (0,)), ((), ())), preferred_element_type=F32)


def mul_nt(left, right):
    return lax.dot_general(left, right, (((1,), (1,)), ((), ())), preferred_element_type=F32)


def tree_sum(values):
    while len(values) > 1:
        values = [a + b for a, b in zip(values[::2], values[1::2])]
    return values[0]


def rows_of(index, count):
    return pl.ds(pl.multiple_of(index * count, TILE), count)


def cols_of(index, count):
    return pl.ds(pl.multiple_of(index * count, 128), count)


def run(body, out_shapes, args, name, scratch=(), flops=10**8, limit=6):
    in_vmem = pl.BlockSpec(memory_space=pltpu.VMEM)
    moved = sum(math.prod(a.shape) * a.dtype.itemsize for a in (*args, *out_shapes))

    def placed(spot_ref, *refs):
        body((spot_ref[0], spot_ref[1], spot_ref[2]), *refs)

    return pl.pallas_call(
        placed,
        out_shape=out_shapes,
        in_specs=[pl.BlockSpec(memory_space=pltpu.SMEM)] + [in_vmem] * (len(args) - 1),
        out_specs=[in_vmem] * len(out_shapes),
        scratch_shapes=list(scratch),
        compiler_params=pltpu.CompilerParams(vmem_limit_bytes=limit * 2**20),
        cost_estimate=pl.CostEstimate(flops=flops, bytes_accessed=moved, transcendentals=0),
        name=name,
    )(*args)


def shape(rows, cols, dtype=BF):
    return jax.ShapeDtypeStruct((rows, cols), dtype)


def local(
    dense_feats,
    bag_counts,
    emb_rows,
    v_emb,
    u_emb,
    b_emb,
    v_bot,
    u_bot,
    b_bot,
    w_first,
    b_first,
    w_second,
    b_second,
    cot_cross,
    cot_bottom,
):
    n_rep, n_z = lax.axis_size("rep"), lax.axis_size("z")
    own_rows, n_feat = dense_feats.shape
    hidden = w_first.shape[1]
    width = v_bot.shape[0]
    n_bag = bag_counts.shape[2]
    pair = 2 * own_rows
    grad_scale = 1.0 / math.sqrt(own_rows * 2 * n_z * n_rep)
    u_part = width // n_rep
    bag_part = round_up(-(-2 * n_bag // n_rep), TILE)
    bag_full = bag_part * n_rep
    dense_rows = hidden + 2 * width
    dense_part = round_up(-(-dense_rows // (2 * n_rep)), TILE)
    feat_rows = round_up(n_feat + 1, TILE)
    n_wide = hidden // width
    slots = [(q * feat_rows + i) for i in range(n_feat + 1, feat_rows) for q in range(n_wide)]
    small_rows = n_wide * feat_rows
    while len(slots) < 2 + n_z:
        slots += list(range(small_rows, small_rows + TILE))
        small_rows += TILE
    small_rows = round_up(small_rows, TILE * n_rep)
    small_part = small_rows // n_rep
    rep_part = dense_part + small_part
    half = rep_part * n_rep
    z_rows = rep_part + u_part + bag_part
    msg_rows = 3 * n_bag + TILE
    gb_rows = round_up(n_z, 8)

    def swap(value):
        return lax.ppermute(value, "core", [(0, 1), (1, 0)])

    def to_z(value, k):
        return lax.ppermute(value, "z", [(i, i ^ k) for i in range(n_z)])

    def to_rep(value, k):
        return lax.ppermute(value, "rep", [(i, i ^ k) for i in range(n_rep)])

    def call(body, out_shapes, args, name, scratch=()):
        return run(body, out_shapes, (spots, *args), name, scratch)

    spots = jnp.stack([lax.axis_index(name) for name in ("rep", "z", "core")]).astype(jnp.int32)

    bias_rows = jnp.concatenate(
        [b[None].astype(F32) for b in (b_emb, b_second, b_bot)] + [jnp.zeros((5, width), F32)]
    )

    def bags_body(spot, ct_ref, emb_ref, v_ref, b_ref, *outs):
        _, z, c = spot
        emb = emb_ref[...]
        emb_v = mul_nn(emb, v_ref[...]).astype(BF)
        bias = jnp.broadcast_to(b_ref[0:1, :], (TILE, width)).astype(BF)
        for k, out in enumerate(outs):
            first = (z ^ k) * 2
            out[:n_bag, :own_rows] = ct_ref[:, cols_of(first + c, own_rows)].astype(F32).astype(BF)
            out[:n_bag, own_rows:] = (
                ct_ref[:, cols_of(first + 1 - c, own_rows)].astype(F32).astype(BF)
            )
            out[n_bag : 2 * n_bag, :] = emb
            out[2 * n_bag : 3 * n_bag, :] = emb_v
            out[3 * n_bag :, :] = bias

    counts_t = jnp.transpose(bag_counts, (1, 2, 0))[0]
    bags = call(
        bags_body,
        [shape(msg_rows, pair)] * n_z,
        (counts_t, emb_rows[0], v_emb, bias_rows),
        "bags",
    )
    bags = [bags[0]] + [to_z(bags[k], k) for k in range(1, n_z)]
    u_z = [u_emb] + [to_z(u_emb, k) for k in range(1, n_z)]

    def cot_body(spot, cot_ref, out):
        _, _, c = spot
        for t in range(n_z):
            out[:, t * width : (t + 1) * width] = cot_ref[:, cols_of(2 * t + 1 - c, width)]

    (cot_out,) = call(cot_body, [shape(own_rows, n_z * width)], (cot_cross,), "cot_send")
    cot_in = swap(cot_out)

    feats_t = jnp.concatenate(
        [
            dense_feats.T,
            jnp.ones((1, own_rows), BF),
            jnp.zeros((feat_rows - n_feat - 1, own_rows), BF),
        ]
    )
    first_rows = jnp.concatenate(
        [w_first, b_first[None], jnp.zeros((feat_rows - n_feat - 1, hidden), BF)]
    )

    def mlp_body(
        spot, x_ref, w1_ref, w2_ref, b_ref, vb_ref, ub_ref, cot_ref,
        act_ref, slope1_ref, bottom_ref, slope2_ref, term_ref, back_ref,
    ):
        act, slope1_ref[...] = silu_parts(mul_tn(x_ref[...], w1_ref[...]))
        act = act.astype(BF)
        act_ref[...] = act
        bottom, slope2_ref[...] = silu_parts(mul_nn(act, w2_ref[...]) + b_ref[1:2, :])
        bottom = bottom.astype(BF)
        bottom_ref[...] = bottom
        term_ref[...] = mul_nn(bottom, vb_ref[...])
        d_lift = (cot_ref[...].astype(F32) * bottom.astype(F32)).astype(BF)
        back_ref[...] = mul_nt(d_lift, ub_ref[...])

    act, slope1, bottom, slope2, bot_term, bot_back = call(
        mlp_body,
        [
            shape(own_rows, hidden),
            shape(own_rows, hidden, F32),
            shape(own_rows, width),
            shape(own_rows, width, F32),
            shape(own_rows, width, F32),
            shape(own_rows, width, F32),
        ],
        (feats_t, first_rows, w_second, bias_rows, v_bot, u_bot, cot_bottom),
        "mlp_forward",
    )

    def cot_of(cot_ref, cot_in_ref, zk, c):
        return jnp.concatenate(
            [cot_ref[:, cols_of(2 * zk + c, width)], cot_in_ref[:, cols_of(zk, width)]], axis=0
        ).astype(F32)

    def low_body(spot, *refs):
        bag = refs[:n_z]
        term_ref, part_ref, pooled_ref = refs[n_z:]
        low = jnp.zeros((pair, width), F32)
        for k in range(n_z):
            base = k * width
            counts = bag[k][:n_bag, :]
            pooled = mul_tn(counts, bag[k][n_bag : 2 * n_bag, :]).astype(BF)
            low += mul_tn(counts, bag[k][2 * n_bag : 3 * n_bag, :])
            pooled_ref[base : base + width, :] = pooled
        part_ref[:own_rows, :] = (low[:own_rows] + term_ref[...]).astype(BF)
        part_ref[own_rows:pair, :] = low[own_rows:].astype(BF)

    low_part, pooled = call(
        low_body, [shape(pair, width), shape(n_z * pair, width)], (*bags, bot_term), "low_terms"
    )
    low_in = swap(low_part)

    def summed(part_ref, in_ref):
        own = part_ref[:own_rows, :].astype(F32) + in_ref[own_rows:, :].astype(F32)
        other = part_ref[own_rows:, :].astype(F32) + in_ref[:own_rows, :].astype(F32)
        return own.astype(BF), other.astype(BF)

    def u_grad_body(spot, part_ref, in_ref, pooled_ref, cot_ref, cot_in_ref, low_ref, lift_ref, gb_ref, *outs):
        r, z, c = spot
        *outs, stack = outs
        low_ref[:own_rows, :], low_ref[own_rows:, :] = summed(part_ref, in_ref)
        low = low_ref[...]
        gb_ref[...] = jnp.zeros_like(gb_ref)
        for k in range(n_z):
            base = k * width
            pooled_full = pooled_ref[base : base + width, :].astype(F32)
            d_lift = cot_of(cot_ref, cot_in_ref, z ^ k, c) * pooled_full
            gb_ref[k : k + 1, :] = jnp.sum(d_lift, axis=0, keepdims=True) * grad_scale
            d_lift = d_lift.astype(BF)
            lift_ref[base : base + width, :] = d_lift
            stack[...] = (mul_tn(low, d_lift) * grad_scale).astype(BF)
            for j, out in enumerate(outs):
                out[k * u_part : (k + 1) * u_part, :] = stack[rows_of(r ^ j, u_part), :]

    low, d_lift, grad_b, *u_outs = call(
        u_grad_body,
        [shape(pair, width), shape(n_z * pair, width), shape(gb_rows, width, F32)]
        + [shape(n_z * u_part, width)] * n_rep,
        (low_part, low_in, pooled, cot_cross, cot_in),
        "u_grads",
        [pltpu.VMEM((width, width), BF)],
    )
    u_ins = [u_outs[0]] + [to_rep(u_outs[j], j) for j in range(1, n_rep)]

    def back_body(spot, *refs):
        u_refs = refs[:n_z]
        lift_ref, back_ref, part_ref = refs[n_z:]
        back = jnp.zeros((pair, width), F32)
        for k in range(n_z):
            back += mul_nt(lift_ref[k * width : (k + 1) * width, :], u_refs[k][...])
        part_ref[:own_rows, :] = (back[:own_rows] + back_ref[...]).astype(BF)
        part_ref[own_rows:pair, :] = back[own_rows:].astype(BF)

    (back_part,) = call(back_body, [shape(pair, width)], (*u_z, d_lift, bot_back), "back_terms")
    back_in = swap(back_part)

    def dense_body(
        spot, low_ref, part_ref, in_ref, act_ref, slope1_ref, bottom_ref, slope2_ref, cot_ref, x_ref,
        w2_ref, vb_ref, ub_ref, b_ref, gb_ref,
        cross_ref, send_ref, keep_ref, pack, small,
    ):
        _, z, c = spot
        low = low_ref[:own_rows, :]
        d_low, _ = summed(part_ref, in_ref)
        bottom = bottom_ref[...]
        bottom_full = bottom.astype(F32)
        cot = cot_ref[...].astype(F32)
        lift = mul_nn(low, ub_ref[...]) + b_ref[2:3, :] + 1.0
        cross_ref[...] = (bottom_full * lift).astype(BF)
        d_second = (cot * lift + mul_nt(d_low, vb_ref[...])) * slope2_ref[...]
        d_second_round = d_second.astype(BF)
        d_first = mul_nt(d_second_round, w2_ref[...]) * slope1_ref[...]
        d_bias = cot * bottom_full
        pack[...] = jnp.zeros_like(pack)

        def put(first, value):
            value = (value * grad_scale).astype(BF)
            at, last = first, first + value.shape[0]
            while at < last:
                block = at // dense_part
                end = min(last, (block + 1) * dense_part)
                start = block * rep_part + at - block * dense_part
                pack[start : start + end - at, :] = value[at - first : end - first]
                at = end

        put(0, mul_tn(act_ref[...], d_second_round))
        put(hidden, mul_tn(bottom, d_low))
        put(hidden + width, mul_tn(low, d_bias.astype(BF)))
        small[...] = jnp.zeros_like(small)
        g_first = mul_nn(x_ref[...], d_first.astype(BF)) * grad_scale
        for q in range(n_wide):
            small[q * feat_rows : (q + 1) * feat_rows, :] = g_first[
                :, q * width : (q + 1) * width
            ]
        small[slots[0] : slots[0] + 1, :] = jnp.sum(d_second, axis=0, keepdims=True) * grad_scale
        small[slots[1] : slots[1] + 1, :] = jnp.sum(d_bias, axis=0, keepdims=True) * grad_scale
        for slot in slots[2:]:
            small[slot : slot + 1, :] = jnp.zeros((1, width), F32)

        def put_small(which):
            for j in range(n_rep):
                start = pl.multiple_of((which * n_rep + j) * rep_part + dense_part, TILE)
                pack[pl.ds(start, small_part), :] = small[
                    j * small_part : (j + 1) * small_part, :
                ].astype(BF)

        put_small(1 - c)
        send_ref[...] = pack[rows_of(1 - c, half), :]
        for k in range(n_z):
            for t in range(n_z):

                @pl.when((z ^ k) == t)
                def _():
                    small[slots[2 + t] : slots[2 + t] + 1, :] = gb_ref[k : k + 1, :]

        put_small(c)
        keep_ref[...] = pack[rows_of(c, half), :]

    cross_bot, dense_out, dense_keep = call(
        dense_body,
        [shape(own_rows, width), shape(half, width), shape(half, width)],
        (
            low, back_part, back_in, act, slope1, bottom, slope2, cot_bottom, feats_t,
            w_second, v_bot, u_bot, bias_rows, grad_b,
        ),
        "dense_grads",
        [pltpu.VMEM((2 * half, width), BF), pltpu.VMEM((small_rows, width), F32)],
    )
    dense_in = swap(dense_out)

    def table_body(spot, *refs):
        bag = refs[:n_z]
        u_refs = refs[n_z : 2 * n_z]
        low_ref, part_ref, in_ref, pooled_ref, cot_ref, cot_in_ref = refs[2 * n_z : 2 * n_z + 6]
        own_ref, send_ref, out = refs[2 * n_z + 6 :]
        _, z, c = spot
        low = low_ref[...]
        d_low = jnp.concatenate(summed(part_ref, in_ref), axis=0)
        if bag_full > 2 * n_bag:
            out[...] = jnp.zeros_like(out)
        for k in range(n_z):
            base = k * width
            counts = bag[k][:n_bag, :]
            bias = bag[k][3 * n_bag :, :].astype(F32)[0:1]
            lift = mul_nn(low, u_refs[k][...]) + bias + 1.0
            cross = (pooled_ref[base : base + width, :].astype(F32) * lift).astype(BF)
            own_ref[:, cols_of(z ^ k, width)] = cross[:own_rows]
            send_ref[:, cols_of(z ^ k, width)] = cross[own_rows:]
            direct = (cot_of(cot_ref, cot_in_ref, z ^ k, c) * lift).astype(BF)
            start = k * bag_full
            out[start : start + n_bag, :] = (mul_nn(counts, d_low) * grad_scale).astype(BF)
            out[start + n_bag : start + 2 * n_bag, :] = (
                mul_nn(counts, direct) * grad_scale
            ).astype(BF)

    cross_own, cross_out, bag_keep = call(
        table_body,
        [shape(own_rows, n_z * width)] * 2 + [shape(n_z * bag_full, width)],
        (*bags, *u_z, low, back_part, back_in, pooled, cot_cross, cot_in),
        "table_grads",
    )

    def pair_body(spot, keep_ref, in_ref, bag_ref, *outs):
        r, _, _ = spot
        for j, out in enumerate(outs):
            rows = rows_of(r ^ j, rep_part)
            out[:rep_part, :] = (
                keep_ref[rows, :].astype(F32) + in_ref[rows, :].astype(F32)
            ).astype(BF)
            for k in range(n_z):
                rows = pl.ds(pl.multiple_of(k * bag_full + (r ^ j) * bag_part, TILE), bag_part)
                start = rep_part + k * bag_part
                out[start : start + bag_part, :] = bag_ref[rows, :]

    rep_outs = call(
        pair_body,
        [shape(rep_part + n_z * bag_part, width)] * n_rep,
        (dense_keep, dense_in, bag_keep),
        "pair_sum",
    )
    rep_ins = [rep_outs[0]] + [to_rep(rep_outs[j], j) for j in range(1, n_rep)]
    cross_in = swap(cross_out)

    def total(refs, first, count):
        return tree_sum([ref[first : first + count, :].astype(F32) for ref in refs]).astype(BF)

    def rep_body(spot, *refs):
        ins, u_refs, outs = refs[:n_rep], refs[n_rep : 2 * n_rep], refs[2 * n_rep :]
        dense = total(ins, 0, rep_part)
        for k, out in enumerate(outs):
            out[:rep_part, :] = dense
            out[rep_part : rep_part + u_part, :] = total(u_refs, k * u_part, u_part)
            out[rep_part + u_part :, :] = total(ins, rep_part + k * bag_part, bag_part)

    z_outs = call(rep_body, [shape(z_rows, width)] * n_z, (*rep_ins, *u_ins), "rep_sum")
    z_ins = [z_outs[0]] + [to_z(z_outs[k], k) for k in range(1, n_z)]

    def z_body(spot, *refs):
        refs[n_z][...] = total(refs[:n_z], 0, z_rows)

    (mine,) = call(z_body, [shape(z_rows, width)], z_ins, "z_sum")

    pieces = [mine] + [to_rep(mine, j) for j in range(1, n_rep)]

    def gather_body(spot, *refs):
        r, _, _ = spot
        for j in range(n_rep):
            refs[n_rep][rows_of(r ^ j, dense_part), :] = refs[j][:dense_part, :]

    (dense_own,) = call(gather_body, [shape(n_rep * dense_part, width)], pieces, "dense_gather")
    dense_other = swap(dense_own)

    def cross_body(spot, own_ref, in_ref, out):
        _, _, c = spot
        for t in range(n_z):
            cols = slice(t * width, (t + 1) * width)
            out[:, cols_of(2 * t + c, width)] = own_ref[:, cols]
            out[:, cols_of(2 * t + 1 - c, width)] = in_ref[:, cols]

    (cross_emb,) = call(
        cross_body, [shape(own_rows, 2 * n_z * width)], (cross_own, cross_in), "cross_rows"
    )

    def table_last_body(spot, *refs):
        ins = refs[:n_rep]
        emb_ref, v_ref, g_table, g_v, g_u, g_wide, g_rows, stack, small = refs[n_rep:]
        r, z, _ = spot
        for j in range(n_rep):
            rows = slice(rep_part, rep_part + u_part)
            g_u[rows_of(r ^ j, u_part), :] = ins[j][rows, :]
            stack[rows_of(r ^ j, bag_part), :] = ins[j][rep_part + u_part :, :]
            small[rows_of(r ^ j, small_part), :] = ins[j][dense_part:rep_part, :].astype(F32)
        bag_low = stack[:n_bag, :]
        g_v[...] = mul_tn(emb_ref[...], bag_low).astype(BF)
        direct = stack[n_bag : 2 * n_bag, :].astype(F32)
        g_table[...] = (direct + mul_nt(bag_low, v_ref[...])).astype(BF)
        for q in range(n_wide):
            g_wide[:, q * width : (q + 1) * width] = small[q * feat_rows : (q + 1) * feat_rows, :]
        g_rows[...] = jnp.zeros_like(g_rows)
        for i in range(2):
            g_rows[i : i + 1, :] = small[slots[i] : slots[i] + 1, :]
        for t in range(n_z):

            @pl.when(z == t)
            def _():
                g_rows[2:3, :] = small[slots[2 + t] : slots[2 + t] + 1, :]

    grad_table, grad_v, grad_u, g_wide, g_rows = call(
        table_last_body,
        [
            shape(n_bag, width),
            shape(width, width),
            shape(width, width),
            shape(feat_rows, hidden, F32),
            shape(8, width, F32),
        ],
        (*pieces, emb_rows[0], v_emb),
        "table_last",
        [pltpu.VMEM((bag_full, width), BF), pltpu.VMEM((small_rows, width), F32)],
    )
    g_wide, g_rows = g_wide.astype(BF), g_rows.astype(BF)

    def dense_last_body(spot, own_ref, other_ref, g_second, g_vb, g_ub, stack):
        _, _, c = spot
        stack[rows_of(c, n_rep * dense_part), :] = own_ref[...]
        stack[rows_of(1 - c, n_rep * dense_part), :] = other_ref[...]
        g_second[...] = stack[:hidden, :]
        g_vb[...] = stack[hidden : hidden + width, :]
        g_ub[...] = stack[hidden + width : dense_rows, :]

    grad_ws, grad_vb, grad_ub = call(
        dense_last_body,
        [shape(hidden, width), shape(width, width), shape(width, width)],
        (dense_own, dense_other),
        "dense_last",
        [pltpu.VMEM((2 * n_rep * dense_part, width), BF)],
    )
    return (
        cross_emb,
        cross_bot,
        grad_table[None],
        grad_v,
        grad_u,
        g_rows[2],
        grad_vb,
        grad_ub,
        g_rows[1],
        g_wide[:n_feat],
        g_wide[n_feat],
        grad_ws,
        g_rows[0],
    )


def solution(mesh):
    n_rep, n_mp = mesh.devices.shape
    mesh = Mesh(mesh.devices.reshape(n_rep, n_mp // 2, 2), ("rep", "z", "core"))
    return jax.shard_map(
        local,
        mesh=mesh,
        in_specs=(
            P(("rep", "z", "core"), None),
            P("rep", ("z", "core"), None),
            P(("z", "core"), None, None),
            P(("z", "core"), None),
            P(None, ("z", "core")),
            P(("z", "core")),
            P(),
            P(),
            P(),
            P(),
            P(),
            P(),
            P(),
            P(("rep", "z", "core"), None),
            P(("rep", "z", "core"), None),
        ),
        out_specs=(
            P(("rep", "z", "core"), None),
            P(("rep", "z", "core"), None),
            P(("z", "core"), None, None),
            P(("z", "core"), None),
            P(None, ("z", "core")),
            P(("z", "core")),
            P(),
            P(),
            P(),
            P(),
            P(),
            P(),
            P(),
        ),
        check_vma=False,
    )
```

time: 221 us -> 90.9 us (0.41)
  blocking collectives: 89.3 us -> 0 us
  waiting for transfers between devices: 78.8 us -> 42.6 us
  starting transfers between devices: 10.1 us -> 26.1 us
  matrix products: 15.8 us -> 0 us
  Pallas kernels: 0 us -> 15.5 us
  between operations: 13.9 us -> 0.91 us
  local copies, waits for them, and re-layouts: 11.3 us -> 4.81 us
    psum x2 -> x0, blocking collectives: 74.2 us -> none  [the longest x1 56.8 us: local(): lax.psum((grad_wf, grad_bf, grad_ws, grad_bs, grad_vb, grad_ub, grad_bb),...]
    psum x2 -> x0, waiting for transfers between devices: 57.1 us -> none  [the longest x1 57.1 us: local(): low_rank = lax.psum(partial_value.astype(jnp.bfloat16), 'mp')]
    ppermute x0 -> x24, waiting for transfers between devices: none -> 42.6 us  [the longest x9 26.2 us: to_z(): return lax.ppermute(value, 'z', [(i, i ^ k) for i in range(n_z)])]
    ppermute x0 -> x24, starting transfers between devices: none -> 26.1 us  [the longest x9 14.6 us: to_z(): return lax.ppermute(value, 'z', [(i, i ^ k) for i in range(n_z)])]
    dot_general x18 -> x0, matrix products: 15.8 us -> none  [the longest x7 6.1 us: contract_rows(): lax.dot_general(left_side, right_side, (((0,), (0,)), ((), ())), preferre...]
    pallas_call x0 -> x15, Pallas kernels: none -> 15.5 us  [run(): pl.pallas_call(placed, out_shape=out_shapes, in_specs=[pl.BlockSpec(memor...]
    all_gather x1 -> x0, blocking collectives: 15 us -> none  [local(): d_low = lax.all_gather(own_d_low, 'mp', axis=0, tiled=True)]
    all_to_all x2 -> x0, waiting for transfers between devices: 13.7 us -> none  [the longest x1 13.7 us: local(): lax.all_to_all(cross_local, 'mp', split_axis=0, concat_axis=1, tiled=True)]
  transfers between devices with their start and end apart: 5 -> 24, of which waited for: 3 -> 10; matrix products, arithmetic and copies ran while one was open for 4% -> 2% of each run, Pallas kernels for 0% -> 10%
where the time goes in v1:
time: 90.9 us; the launch traced here: 90.2 us
  waiting for transfers between devices  42.6 us (47%)
  starting transfers between devices  26.1 us (29%)
  Pallas kernels  15.5 us (17%)
  local copies, waits for them, and re-layouts  4.81 us (5%)
  between operations  0.91 us (1%)
    ppermute x9, waiting for transfers between devices, to_z(): return lax.ppermute(value, 'z', [(i, i ^ k) for i in range(n_z)])  26.2 us
    pallas_call x15, Pallas kernels, run(): pl.pallas_call(placed, out_shape=out_shapes, in_specs=[pl.BlockSpec(memor...  15.5 us
    ppermute x9, waiting for transfers between devices, to_rep(): return lax.ppermute(value, 'rep', [(i, i ^ k) for i in range(n_rep)])  15.1 us
    ppermute x9, starting transfers between devices, to_z(): return lax.ppermute(value, 'z', [(i, i ^ k) for i in range(n_z)])  14.6 us
    ppermute x9, starting transfers between devices, to_rep(): return lax.ppermute(value, 'rep', [(i, i ^ k) for i in range(n_rep)])  10.6 us
    unnamed x34, local copies, waits for them, and re-layouts  3.43 us
  transfers between devices with their start and end apart: 24, of which 10 were waited for; matrix products, arithmetic and copies ran while one was open for 2% of the time, Pallas kernels for 10%

profile of v1, /device:TPU:0, one launch (start us, length us, event | category | flops | bytes accessed | tf_op | source)
XLA Modules:
  0.0 90.2 jit_solution(7065025601210944128)
XLA Ops:
  5.5 3.1 %collective-permute-start = (bf16[208,256]{1,0:T(8,128)(2,1)S(1)}, bf16[208,256]{1,0:T(8,128)(2,1)S(1)}, u32[]{:S(2)}, u32[]{:S(2)}) collective-permute-start(bf16[208,256]{1,0:T(8,128)(2,1)S(1)} %get-tuple-element.55), channel_id=1, source_target_pairs={{0,2},{2,0},{4,6},{6,4},{1,3},{3,1},{5,7},{7,5},{8,10},{10,8},{12,... | collective-permute-start | bytes 319496 | tf_op jit(solution)/shard_map/ppermute | solution.py:122
  8.6 2.6 %collective-permute-start.1 = (bf16[208,256]{1,0:T(8,128)(2,1)S(1)}, bf16[208,256]{1,0:T(8,128)(2,1)S(1)}, u32[]{:S(2)}, u32[]{:S(2)}) collective-permute-start(bf16[208,256]{1,0:T(8,128)(2,1)S(1)} %get-tuple-element.56), channel_id=1, source_target_pairs={{0,4},{2,6},{4,0},{6,2},{1,5},{3,7},{5,1},{7,3},{8,12},{10,14},{12... | collective-permute-start | bytes 319496 | tf_op jit(solution)/shard_map/ppermute | solution.py:122
  12.2 1.2 %mlp_forward.1 = (bf16[128,1024]{1,0:T(8,128)(2,1)S(1)}, f32[128,1024]{1,0:T(8,128)S(1)}, bf16[128,256]{1,0:T(8,128)(2,1)S(1)}, f32[128,256]{1,0:T(8,128)S(1)}, ...) custom-call(s32[3]{0:T(128)S(1)} %pad_add_fusion.spot_ref, bf16[16,128]{1,0:T(8,128)(2,1)S(1)} %maximum_maximum_fusion.2.refs_0_.refs_8_, ...), custom_call_target="tpu_custom_call" | custom-call | flops 100000000 | bytes 2142220 | tf_op jit(solution)/shard_map/mlp_forward/pallas_call | solution.py:58
  13.4 6.4 %collective-permute-done.1.refs_2_ = bf16[208,256]{1,0:T(8,128)(2,1)S(1)} collective-permute-done((bf16[208,256]{1,0:T(8,128)(2,1)S(1)}, bf16[208,256]{1,0:T(8,128)(2,1)S(1)}, u32[]{:S(2)}, u32[]{:S(2)}) %collective-permute-start.1) | collective-permute-done | bytes 106528 | tf_op jit(solution)/shard_map/ppermute | solution.py:122
  20.9 2.5 %collective-permute-start.5 = (bf16[256,256]{1,0:T(8,128)(2,1)S(1)}, bf16[256,256]{1,0:T(8,128)(2,1)S(1)}, u32[]{:S(2)}, u32[]{:S(2)}) collective-permute-start(bf16[256,256]{1,0:T(8,128)(2,1)S(1)} %copy-done.5), channel_id=1, source_target_pairs={{0,6},{2,4},{4,2},{6,0},{1,7},{3,5},{5,3},{7,1},{8,14},{10,12},{12... | collective-permute-start | bytes 393224 | tf_op jit(solution)/shard_map/ppermute | solution.py:122
  26.4 2.8 %collective-permute-done.5.refs_3_.refs_7_ = bf16[256,256]{1,0:T(8,128)(2,1)S(1)} collective-permute-done((bf16[256,256]{1,0:T(8,128)(2,1)S(1)}, bf16[256,256]{1,0:T(8,128)(2,1)S(1)}, u32[]{:S(2)}, u32[]{:S(2)}) %collective-permute-start.5) | collective-permute-done | bytes 131104 | tf_op jit(solution)/shard_map/ppermute | solution.py:122
  29.2 7.2 %collective-permute-done.4.refs_2_.refs_6_ = bf16[256,256]{1,0:T(8,128)(2,1)S(1)} collective-permute-done((bf16[256,256]{1,0:T(8,128)(2,1)S(1)}, bf16[256,256]{1,0:T(8,128)(2,1)S(1)}, u32[]{:S(2)}, u32[]{:S(2)}) %collective-permute-start.4) | collective-permute-done | bytes 131104 | tf_op jit(solution)/shard_map/ppermute | solution.py:122
  37.3 1.3 %collective-permute-done.8.refs_10_.refs_2_ = bf16[256,256]{1,0:T(8,128)(2,1)S(1)} collective-permute-done((bf16[256,256]{1,0:T(8,128)(2,1)S(1)}, bf16[256,256]{1,0:T(8,128)(2,1)S(1)}, u32[]{:S(2)}, u32[]{:S(2)}) %collective-permute-start.8) | collective-permute-done | bytes 131104 | tf_op jit(solution)/shard_map/ppermute | solution.py:119
  38.7 2.0 %dense_grads.1 = (bf16[128,256]{1,0:T(8,128)(2,1)}, bf16[832,256]{1,0:T(8,128)(2,1)S(1)}, bf16[832,256]{1,0:T(8,128)(2,1)S(1)}) custom-call(s32[3]{0:T(128)S(1)} %pad_add_fusion.spot_ref, bf16[256,256]{1,0:T(8,128)(2,1)S(1)} %get-tuple-element.61.refs_8_.refs_0_, bf16[256,256]{1,0:T(8,128)(2,1)S(1)} %back_terms.1.refs_9_.refs_1_, ...), custom_call_target="tpu_custom_call" | custom-call | flops 100000000 | bytes 3166220 | tf_op jit(solution)/shard_map/dense_grads/pallas_call | solution.py:58
  40.8 1.5 %collective-permute-start.14 = (bf16[256,256]{1,0:T(8,128)(2,1)S(1)}, bf16[256,256]{1,0:T(8,128)(2,1)S(1)}, u32[]{:S(2)}, u32[]{:S(2)}) collective-permute-start(bf16[256,256]{1,0:T(8,128)(2,1)S(1)} %get-tuple-element.80), channel_id=1, source_target_pairs={{0,8},{8,0},{16,24},{24,16},{1,9},{9,1},{17,25},{25,17},{2,10},{10... | collective-permute-start | bytes 393224 | tf_op jit(solution)/shard_map/ppermute | solution.py:125
  44.7 1.5 %collective-permute-start.12 = (bf16[336,256]{1,0:T(8,128)(2,1)S(1)}, bf16[336,256]{1,0:T(8,128)(2,1)S(1)}, u32[]{:S(2)}, u32[]{:S(2)}) collective-permute-start(bf16[336,256]{1,0:T(8,128)(2,1)S(1)} %get-tuple-element.77), channel_id=1, source_target_pairs={{0,16},{8,24},{16,0},{24,8},{1,17},{9,25},{17,1},{25,9},{2,18},{10... | collective-permute-start | bytes 516104 | tf_op jit(solution)/shard_map/ppermute | solution.py:125
  46.3 1.4 %collective-permute-start.13 = (bf16[336,256]{1,0:T(8,128)(2,1)S(1)}, bf16[336,256]{1,0:T(8,128)(2,1)S(1)}, u32[]{:S(2)}, u32[]{:S(2)}) collective-permute-start(bf16[336,256]{1,0:T(8,128)(2,1)S(1)} %get-tuple-element.78), channel_id=1, source_target_pairs={{0,24},{8,16},{16,8},{24,0},{1,25},{9,17},{17,9},{25,1},{2,26},{10... | collective-permute-start | bytes 516104 | tf_op jit(solution)/shard_map/ppermute | solution.py:125
  47.7 1.5 %collective-permute-start.15 = (bf16[256,256]{1,0:T(8,128)(2,1)S(1)}, bf16[256,256]{1,0:T(8,128)(2,1)S(1)}, u32[]{:S(2)}, u32[]{:S(2)}) collective-permute-start(bf16[256,256]{1,0:T(8,128)(2,1)S(1)} %get-tuple-element.81), channel_id=1, source_target_pairs={{0,16},{8,24},{16,0},{24,8},{1,17},{9,25},{17,1},{25,9},{2,18},{10... | collective-permute-start | bytes 393224 | tf_op jit(solution)/shard_map/ppermute | solution.py:125
  49.7 10.4 %collective-permute-done.15.refs_6_ = bf16[256,256]{1,0:T(8,128)(2,1)S(1)} collective-permute-done((bf16[256,256]{1,0:T(8,128)(2,1)S(1)}, bf16[256,256]{1,0:T(8,128)(2,1)S(1)}, u32[]{:S(2)}, u32[]{:S(2)}) %collective-permute-start.15) | collective-permute-done | bytes 131104 | tf_op jit(solution)/shard_map/ppermute | solution.py:125
  60.9 3.0 %collective-permute-start.18 = (bf16[304,256]{1,0:T(8,128)(2,1)S(1)}, bf16[304,256]{1,0:T(8,128)(2,1)S(1)}, u32[]{:S(2)}, u32[]{:S(2)}) collective-permute-start(bf16[304,256]{1,0:T(8,128)(2,1)S(1)} %get-tuple-element.85), channel_id=1, source_target_pairs={{0,4},{2,6},{4,0},{6,2},{1,5},{3,7},{5,1},{7,3},{8,12},{10,14},{12... | collective-permute-start | bytes 466952 | tf_op jit(solution)/shard_map/ppermute | solution.py:122
  63.9 1.4 %collective-permute-start.19 = (bf16[304,256]{1,0:T(8,128)(2,1)S(1)}, bf16[304,256]{1,0:T(8,128)(2,1)S(1)}, u32[]{:S(2)}, u32[]{:S(2)}) collective-permute-start(bf16[304,256]{1,0:T(8,128)(2,1)S(1)} %get-tuple-element.86), channel_id=1, source_target_pairs={{0,6},{2,4},{4,2},{6,0},{1,7},{3,5},{5,3},{7,1},{8,14},{10,12},{12... | collective-permute-start | bytes 466952 | tf_op jit(solution)/shard_map/ppermute | solution.py:122
  65.3 2.8 %collective-permute-done.17.refs_1_ = bf16[304,256]{1,0:T(8,128)(2,1)S(1)} collective-permute-done((bf16[304,256]{1,0:T(8,128)(2,1)S(1)}, bf16[304,256]{1,0:T(8,128)(2,1)S(1)}, u32[]{:S(2)}, u32[]{:S(2)}) %collective-permute-start.17) | collective-permute-done | bytes 155680 | tf_op jit(solution)/shard_map/ppermute | solution.py:122
  68.1 7.0 %collective-permute-done.18.refs_2_ = bf16[304,256]{1,0:T(8,128)(2,1)S(1)} collective-permute-done((bf16[304,256]{1,0:T(8,128)(2,1)S(1)}, bf16[304,256]{1,0:T(8,128)(2,1)S(1)}, u32[]{:S(2)}, u32[]{:S(2)}) %collective-permute-start.18) | collective-permute-done | bytes 155680 | tf_op jit(solution)/shard_map/ppermute | solution.py:122
  75.8 2.5 %collective-permute-start.22 = (bf16[304,256]{1,0:T(8,128)(2,1)S(1)}, bf16[304,256]{1,0:T(8,128)(2,1)S(1)}, u32[]{:S(2)}, u32[]{:S(2)}) collective-permute-start(bf16[304,256]{1,0:T(8,128)(2,1)S(1)} %z_sum.1.refs_0_), channel_id=1, source_target_pairs={{0,24},{8,16},{16,8},{24,0},{1,25},{9,17},{17,9},{25,1},{2,26},{10... | collective-permute-start | bytes 466952 | tf_op jit(solution)/shard_map/ppermute | solution.py:125
  79.3 2.6 %collective-permute-done.22.refs_3_ = bf16[304,256]{1,0:T(8,128)(2,1)S(1)} collective-permute-done((bf16[304,256]{1,0:T(8,128)(2,1)S(1)}, bf16[304,256]{1,0:T(8,128)(2,1)S(1)}, u32[]{:S(2)}, u32[]{:S(2)}) %collective-permute-start.22) | collective-permute-done | bytes 155680 | tf_op jit(solution)/shard_map/ppermute | solution.py:125
  82.0 1.7 %collective-permute-done.21.refs_2_ = bf16[304,256]{1,0:T(8,128)(2,1)S(1)} collective-permute-done((bf16[304,256]{1,0:T(8,128)(2,1)S(1)}, bf16[304,256]{1,0:T(8,128)(2,1)S(1)}, u32[]{:S(2)}, u32[]{:S(2)}) %collective-permute-start.21) | collective-permute-done | bytes 155680 | tf_op jit(solution)/shard_map/ppermute | solution.py:125
  84.7 1.4 %cross_rows.1 = bf16[128,2048]{1,0:T(8,128)(2,1)} custom-call(s32[3]{0:T(128)S(1)} %pad_add_fusion.spot_ref, bf16[128,1024]{1,0:T(8,128)(2,1)S(1)} %get-tuple-element.64.refs_0_, bf16[128,1024]{1,0:T(8,128)(2,1)S(1)} %collective-permute-done.9.refs_1_), custom_call_target="tpu_custom_call" | custom-call | flops 100000000 | bytes 1048588 | tf_op jit(solution)/shard_map/cross_rows/pallas_call | solution.py:58
  86.1 1.5 %table_last.1 = (bf16[64,256]{1,0:T(8,128)(2,1)}, bf16[256,256]{1,0:T(8,128)(2,1)}, bf16[256,256]{1,0:T(8,128)(2,1)}, f32[16,1024]{1,0:T(8,128)S(1)}, f32[8,256]{1,0:T(8,128)S(1)}) custom-call(s32[3]{0:T(128)S(1)} %pad_add_fusion.spot_ref, bf16[304,256]{1,0:T(8,128)(2,1)S(1)} %z_sum.1.refs_0_, bf16[304,256]{1,0:T(8,128)(2,1)S(1)} %collective-permute-done.20.refs_1_, ...), custom_call_target="tpu_custom_call" | custom-call | flops 100000000 | bytes 1155084 | tf_op jit(solution)/shard_map/table_last/pallas_call | solution.py:58
  88.7 1.5 %dense_last.1 = (bf16[1024,256]{1,0:T(8,128)(2,1)}, bf16[256,256]{1,0:T(8,128)(2,1)}, bf16[256,256]{1,0:T(8,128)(2,1)}) custom-call(s32[3]{0:T(128)S(1)} %pad_add_fusion.spot_ref, bf16[768,256]{1,0:T(8,128)(2,1)S(1)} %dense_gather.1.refs_0_, bf16[768,256]{1,0:T(8,128)(2,1)S(1)} %collective-permute-done.23.refs_1_), custom_call_target="tpu_custom_call" | custom-call | flops 100000000 | bytes 1572876 | tf_op jit(solution)/shard_map/dense_last/pallas_call | solution.py:58
  (90 shorter events, 18.4 us)
Async XLA Ops:
  2.4 23.0 %collective-permute-start.7 = (bf16[128,1024]{1,0:T(8,128)(2,1)S(1)}, bf16[128,1024]{1,0:T(8,128)(2,1)S(1)}, u32[]{:S(2)}, u32[]{:S(2)}) collective-permute-start(bf16[128,1024]{1,0:T(8,128)(2,1)S(1)} %cot_send.1), channel_id=1, source_target_pairs={{0,1},{1,0},{2,3},{3,2},{4,5},{5,4},{6,7},{7,6},{8,9},{9,8},{10,11... | collective-permute-start | bytes 786440 | tf_op jit(solution)/shard_map/ppermute | solution.py:119
  5.5 7.9 %collective-permute-start = (bf16[208,256]{1,0:T(8,128)(2,1)S(1)}, bf16[208,256]{1,0:T(8,128)(2,1)S(1)}, u32[]{:S(2)}, u32[]{:S(2)}) collective-permute-start(bf16[208,256]{1,0:T(8,128)(2,1)S(1)} %get-tuple-element.55), channel_id=1, source_target_pairs={{0,2},{2,0},{4,6},{6,4},{1,3},{3,1},{5,7},{7,5},{8,10},{10,8},{12,... | collective-permute-start | bytes 319496 | tf_op jit(solution)/shard_map/ppermute | solution.py:122
  8.6 11.2 %collective-permute-start.1 = (bf16[208,256]{1,0:T(8,128)(2,1)S(1)}, bf16[208,256]{1,0:T(8,128)(2,1)S(1)}, u32[]{:S(2)}, u32[]{:S(2)}) collective-permute-start(bf16[208,256]{1,0:T(8,128)(2,1)S(1)} %get-tuple-element.56), channel_id=1, source_target_pairs={{0,4},{2,6},{4,0},{6,2},{1,5},{3,7},{5,1},{7,3},{8,12},{10,14},{12... | collective-permute-start | bytes 319496 | tf_op jit(solution)/shard_map/ppermute | solution.py:122
  11.2 8.6 %collective-permute-start.2 = (bf16[208,256]{1,0:T(8,128)(2,1)S(1)}, bf16[208,256]{1,0:T(8,128)(2,1)S(1)}, u32[]{:S(2)}, u32[]{:S(2)}) collective-permute-start(bf16[208,256]{1,0:T(8,128)(2,1)S(1)} %get-tuple-element.57), channel_id=1, source_target_pairs={{0,6},{2,4},{4,2},{6,0},{1,7},{3,5},{5,3},{7,1},{8,14},{10,12},{12... | collective-permute-start | bytes 319496 | tf_op jit(solution)/shard_map/ppermute | solution.py:122
  20.8 4.5 %collective-permute-start.6 = (bf16[256,256]{1,0:T(8,128)(2,1)S(1)}, bf16[256,256]{1,0:T(8,128)(2,1)S(1)}, u32[]{:S(2)}, u32[]{:S(2)}) collective-permute-start(bf16[256,256]{1,0:T(8,128)(2,1)S(1)} %get-tuple-element.59.refs_0_), channel_id=1, source_target_pairs={{0,1},{1,0},{2,3},{3,2},{4,5},{5,4},{6,7},{7,6},{8,9},{9,8},{10,11... | collective-permute-start | bytes 393224 | tf_op jit(solution)/shard_map/ppermute | solution.py:119
  20.9 8.3 %collective-permute-start.5 = (bf16[256,256]{1,0:T(8,128)(2,1)S(1)}, bf16[256,256]{1,0:T(8,128)(2,1)S(1)}, u32[]{:S(2)}, u32[]{:S(2)}) collective-permute-start(bf16[256,256]{1,0:T(8,128)(2,1)S(1)} %copy-done.5), channel_id=1, source_target_pairs={{0,6},{2,4},{4,2},{6,0},{1,7},{3,5},{5,3},{7,1},{8,14},{10,12},{12... | collective-permute-start | bytes 393224 | tf_op jit(solution)/shard_map/ppermute | solution.py:122
  23.4 13.0 %collective-permute-start.4 = (bf16[256,256]{1,0:T(8,128)(2,1)S(1)}, bf16[256,256]{1,0:T(8,128)(2,1)S(1)}, u32[]{:S(2)}, u32[]{:S(2)}) collective-permute-start(bf16[256,256]{1,0:T(8,128)(2,1)S(1)} %copy-done.5), channel_id=1, source_target_pairs={{0,4},{2,6},{4,0},{6,2},{1,5},{3,7},{5,1},{7,3},{8,12},{10,14},{12... | collective-permute-start | bytes 393224 | tf_op jit(solution)/shard_map/ppermute | solution.py:122
  24.1 12.2 %collective-permute-start.3 = (bf16[256,256]{1,0:T(8,128)(2,1)S(1)}, bf16[256,256]{1,0:T(8,128)(2,1)S(1)}, u32[]{:S(2)}, u32[]{:S(2)}) collective-permute-start(bf16[256,256]{1,0:T(8,128)(2,1)S(1)} %copy-done.5), channel_id=1, source_target_pairs={{0,2},{2,0},{4,6},{6,4},{1,3},{3,1},{5,7},{7,5},{8,10},{10,8},{12,... | collective-permute-start | bytes 393224 | tf_op jit(solution)/shard_map/ppermute | solution.py:122
  37.2 1.4 %collective-permute-start.8 = (bf16[256,256]{1,0:T(8,128)(2,1)S(1)}, bf16[256,256]{1,0:T(8,128)(2,1)S(1)}, u32[]{:S(2)}, u32[]{:S(2)}) collective-permute-start(bf16[256,256]{1,0:T(8,128)(2,1)S(1)} %back_terms.1.refs_9_.refs_1_), channel_id=1, source_target_pairs={{0,1},{1,0},{2,3},{3,2},{4,5},{5,4},{6,7},{7,6},{8,9},{9,8},{10,11... | collective-permute-start | bytes 393224 | tf_op jit(solution)/shard_map/ppermute | solution.py:119
  40.7 2.8 %collective-permute-start.10 = (bf16[832,256]{1,0:T(8,128)(2,1)S(1)}, bf16[832,256]{1,0:T(8,128)(2,1)S(1)}, u32[]{:S(2)}, u32[]{:S(2)}) collective-permute-start(bf16[832,256]{1,0:T(8,128)(2,1)S(1)} %get-tuple-element.73), channel_id=1, source_target_pairs={{0,1},{1,0},{2,3},{3,2},{4,5},{5,4},{6,7},{7,6},{8,9},{9,8},{10,11... | collective-permute-start | bytes 1277960 | tf_op jit(solution)/shard_map/ppermute | solution.py:119
  40.8 8.4 %collective-permute-start.14 = (bf16[256,256]{1,0:T(8,128)(2,1)S(1)}, bf16[256,256]{1,0:T(8,128)(2,1)S(1)}, u32[]{:S(2)}, u32[]{:S(2)}) collective-permute-start(bf16[256,256]{1,0:T(8,128)(2,1)S(1)} %get-tuple-element.80), channel_id=1, source_target_pairs={{0,8},{8,0},{16,24},{24,16},{1,9},{9,1},{17,25},{25,17},{2,10},{10... | collective-permute-start | bytes 393224 | tf_op jit(solution)/shard_map/ppermute | solution.py:125
  44.1 16.0 %collective-permute-start.11 = (bf16[336,256]{1,0:T(8,128)(2,1)S(1)}, bf16[336,256]{1,0:T(8,128)(2,1)S(1)}, u32[]{:S(2)}, u32[]{:S(2)}) collective-permute-start(bf16[336,256]{1,0:T(8,128)(2,1)S(1)} %get-tuple-element.76), channel_id=1, source_target_pairs={{0,8},{8,0},{16,24},{24,16},{1,9},{9,1},{17,25},{25,17},{2,10},{10... | collective-permute-start | bytes 516104 | tf_op jit(solution)/shard_map/ppermute | solution.py:125
  44.7 15.4 %collective-permute-start.12 = (bf16[336,256]{1,0:T(8,128)(2,1)S(1)}, bf16[336,256]{1,0:T(8,128)(2,1)S(1)}, u32[]{:S(2)}, u32[]{:S(2)}) collective-permute-start(bf16[336,256]{1,0:T(8,128)(2,1)S(1)} %get-tuple-element.77), channel_id=1, source_target_pairs={{0,16},{8,24},{16,0},{24,8},{1,17},{9,25},{17,1},{25,9},{2,18},{10... | collective-permute-start | bytes 516104 | tf_op jit(solution)/shard_map/ppermute | solution.py:125
  46.3 13.9 %collective-permute-start.13 = (bf16[336,256]{1,0:T(8,128)(2,1)S(1)}, bf16[336,256]{1,0:T(8,128)(2,1)S(1)}, u32[]{:S(2)}, u32[]{:S(2)}) collective-permute-start(bf16[336,256]{1,0:T(8,128)(2,1)S(1)} %get-tuple-element.78), channel_id=1, source_target_pairs={{0,24},{8,16},{16,8},{24,0},{1,25},{9,17},{17,9},{25,1},{2,26},{10... | collective-permute-start | bytes 516104 | tf_op jit(solution)/shard_map/ppermute | solution.py:125
  47.7 12.4 %collective-permute-start.15 = (bf16[256,256]{1,0:T(8,128)(2,1)S(1)}, bf16[256,256]{1,0:T(8,128)(2,1)S(1)}, u32[]{:S(2)}, u32[]{:S(2)}) collective-permute-start(bf16[256,256]{1,0:T(8,128)(2,1)S(1)} %get-tuple-element.81), channel_id=1, source_target_pairs={{0,16},{8,24},{16,0},{24,8},{1,17},{9,25},{17,1},{25,9},{2,18},{10... | collective-permute-start | bytes 393224 | tf_op jit(solution)/shard_map/ppermute | solution.py:125
  49.2 10.9 %collective-permute-start.16 = (bf16[256,256]{1,0:T(8,128)(2,1)S(1)}, bf16[256,256]{1,0:T(8,128)(2,1)S(1)}, u32[]{:S(2)}, u32[]{:S(2)}) collective-permute-start(bf16[256,256]{1,0:T(8,128)(2,1)S(1)} %get-tuple-element.82), channel_id=1, source_target_pairs={{0,24},{8,16},{16,8},{24,0},{1,25},{9,17},{17,9},{25,1},{2,26},{10... | collective-permute-start | bytes 393224 | tf_op jit(solution)/shard_map/ppermute | solution.py:125
  60.8 7.3 %collective-permute-start.17 = (bf16[304,256]{1,0:T(8,128)(2,1)S(1)}, bf16[304,256]{1,0:T(8,128)(2,1)S(1)}, u32[]{:S(2)}, u32[]{:S(2)}) collective-permute-start(bf16[304,256]{1,0:T(8,128)(2,1)S(1)} %get-tuple-element.84), channel_id=1, source_target_pairs={{0,2},{2,0},{4,6},{6,4},{1,3},{3,1},{5,7},{7,5},{8,10},{10,8},{12,... | collective-permute-start | bytes 466952 | tf_op jit(solution)/shard_map/ppermute | solution.py:122
  60.9 14.2 %collective-permute-start.18 = (bf16[304,256]{1,0:T(8,128)(2,1)S(1)}, bf16[304,256]{1,0:T(8,128)(2,1)S(1)}, u32[]{:S(2)}, u32[]{:S(2)}) collective-permute-start(bf16[304,256]{1,0:T(8,128)(2,1)S(1)} %get-tuple-element.85), channel_id=1, source_target_pairs={{0,4},{2,6},{4,0},{6,2},{1,5},{3,7},{5,1},{7,3},{8,12},{10,14},{12... | collective-permute-start | bytes 466952 | tf_op jit(solution)/shard_map/ppermute | solution.py:122
  63.9 11.2 %collective-permute-start.19 = (bf16[304,256]{1,0:T(8,128)(2,1)S(1)}, bf16[304,256]{1,0:T(8,128)(2,1)S(1)}, u32[]{:S(2)}, u32[]{:S(2)}) collective-permute-start(bf16[304,256]{1,0:T(8,128)(2,1)S(1)} %get-tuple-element.86), channel_id=1, source_target_pairs={{0,6},{2,4},{4,2},{6,0},{1,7},{3,5},{5,3},{7,1},{8,14},{10,12},{12... | collective-permute-start | bytes 466952 | tf_op jit(solution)/shard_map/ppermute | solution.py:122
  75.8 6.2 %collective-permute-start.22 = (bf16[304,256]{1,0:T(8,128)(2,1)S(1)}, bf16[304,256]{1,0:T(8,128)(2,1)S(1)}, u32[]{:S(2)}, u32[]{:S(2)}) collective-permute-start(bf16[304,256]{1,0:T(8,128)(2,1)S(1)} %z_sum.1.refs_0_), channel_id=1, source_target_pairs={{0,24},{8,16},{16,8},{24,0},{1,25},{9,17},{17,9},{25,1},{2,26},{10... | collective-permute-start | bytes 466952 | tf_op jit(solution)/shard_map/ppermute | solution.py:125
  78.3 5.4 %collective-permute-start.21 = (bf16[304,256]{1,0:T(8,128)(2,1)S(1)}, bf16[304,256]{1,0:T(8,128)(2,1)S(1)}, u32[]{:S(2)}, u32[]{:S(2)}) collective-permute-start(bf16[304,256]{1,0:T(8,128)(2,1)S(1)} %z_sum.1.refs_0_), channel_id=1, source_target_pairs={{0,16},{8,24},{16,0},{24,8},{1,17},{9,25},{17,1},{25,9},{2,18},{10... | collective-permute-start | bytes 466952 | tf_op jit(solution)/shard_map/ppermute | solution.py:125
  78.8 5.2 %collective-permute-start.20 = (bf16[304,256]{1,0:T(8,128)(2,1)S(1)}, bf16[304,256]{1,0:T(8,128)(2,1)S(1)}, u32[]{:S(2)}, u32[]{:S(2)}) collective-permute-start(bf16[304,256]{1,0:T(8,128)(2,1)S(1)} %z_sum.1.refs_0_), channel_id=1, source_target_pairs={{0,8},{8,0},{16,24},{24,16},{1,9},{9,1},{17,25},{25,17},{2,10},{10... | collective-permute-start | bytes 466952 | tf_op jit(solution)/shard_map/ppermute | solution.py:125
  79.3 5.4 %collective-permute-start.9 = (bf16[128,1024]{1,0:T(8,128)(2,1)S(1)}, bf16[128,1024]{1,0:T(8,128)(2,1)S(1)}, u32[]{:S(2)}, u32[]{:S(2)}) collective-permute-start(bf16[128,1024]{1,0:T(8,128)(2,1)S(1)} %get-tuple-element.65), channel_id=1, source_target_pairs={{0,1},{1,0},{2,3},{3,2},{4,5},{5,4},{6,7},{7,6},{8,9},{9,8},{10,11... | collective-permute-start | bytes 786440 | tf_op jit(solution)/shard_map/ppermute | solution.py:119
  84.6 4.2 %collective-permute-start.23 = (bf16[768,256]{1,0:T(8,128)(2,1)S(1)}, bf16[768,256]{1,0:T(8,128)(2,1)S(1)}, u32[]{:S(2)}, u32[]{:S(2)}) collective-permute-start(bf16[768,256]{1,0:T(8,128)(2,1)S(1)} %dense_gather.1.refs_0_), channel_id=1, source_target_pairs={{0,1},{1,0},{2,3},{3,2},{4,5},{5,4},{6,7},{7,6},{8,9},{9,8},{10,11... | collective-permute-start | bytes 1179656 | tf_op jit(solution)/shard_map/ppermute | solution.py:119
  (17 other events, 71.1 us)

commit v2 on v1

--- a/solution.py
+++ b/solution.py
@@ -53,12 +53,12 @@
     moved = sum(math.prod(a.shape) * a.dtype.itemsize for a in (*args, *out_shapes))
 
     def placed(spot_ref, *refs):
-        body((spot_ref[0], spot_ref[1], spot_ref[2]), *refs)
+        body((spot_ref[0, 0], spot_ref[1, 0], spot_ref[2, 0]), *refs)
 
     return pl.pallas_call(
         placed,
         out_shape=out_shapes,
-        in_specs=[pl.BlockSpec(memory_space=pltpu.SMEM)] + [in_vmem] * (len(args) - 1),
+        in_specs=[in_vmem] * len(args),
         out_specs=[in_vmem] * len(out_shapes),
         scratch_shapes=list(scratch),
         compiler_params=pltpu.CompilerParams(vmem_limit_bytes=limit * 2**20),
@@ -111,7 +111,8 @@
     small_part = small_rows // n_rep
     rep_part = dense_part + small_part
     half = rep_part * n_rep
-    z_rows = rep_part + u_part + bag_part
+    tab_part = u_part + bag_part
+    z_rows = rep_part + tab_part
     msg_rows = 3 * n_bag + TILE
     gb_rows = round_up(n_z, 8)
 
@@ -124,20 +125,35 @@
     def to_rep(value, k):
         return lax.ppermute(value, "rep", [(i, i ^ k) for i in range(n_rep)])
 
+    def spread(send, values, near_first=False):
+        order = range(1, len(values))
+        got = {k: send(values[k], k) for k in (order if near_first else reversed(order))}
+        return [values[0]] + [got[k] for k in order]
+
     def call(body, out_shapes, args, name, scratch=()):
         return run(body, out_shapes, (spots, *args), name, scratch)
 
     spots = jnp.stack([lax.axis_index(name) for name in ("rep", "z", "core")]).astype(jnp.int32)
-
+    spots = jnp.broadcast_to(jnp.pad(spots, (0, 5))[:, None], (8, 128))
+
+    u_mine = lax.dynamic_slice_in_dim(u_emb, lax.axis_index("rep") * u_part, u_part, 0)
+    u_z = spread(to_z, [u_mine] * n_z, True)[1:]
+
+    def u_body(spot, *refs):
+        for k, ref in enumerate(refs[:-1]):
+            refs[-1][k * u_part : (k + 1) * u_part, :] = ref[...]
+
+    (u_z,) = call(u_body, [shape((n_z - 1) * u_part, width)], u_z, "u_rows")
+    u_r = spread(to_rep, [u_z] * n_rep)
     bias_rows = jnp.concatenate(
-        [b[None].astype(F32) for b in (b_emb, b_second, b_bot)] + [jnp.zeros((5, width), F32)]
+        [b[None].astype(F32) for b in (b_second, b_bot)] + [jnp.zeros((6, width), F32)]
     )
 
     def bags_body(spot, ct_ref, emb_ref, v_ref, b_ref, *outs):
         _, z, c = spot
         emb = emb_ref[...]
         emb_v = mul_nn(emb, v_ref[...]).astype(BF)
-        bias = jnp.broadcast_to(b_ref[0:1, :], (TILE, width)).astype(BF)
+        bias = b_ref[...]
         for k, out in enumerate(outs):
             first = (z ^ k) * 2
             out[:n_bag, :own_rows] = ct_ref[:, cols_of(first + c, own_rows)].astype(F32).astype(BF)
@@ -152,11 +168,10 @@
     bags = call(
         bags_body,
         [shape(msg_rows, pair)] * n_z,
-        (counts_t, emb_rows[0], v_emb, bias_rows),
+        (counts_t, emb_rows[0], v_emb, jnp.broadcast_to(b_emb[None], (TILE, width))),
         "bags",
     )
-    bags = [bags[0]] + [to_z(bags[k], k) for k in range(1, n_z)]
-    u_z = [u_emb] + [to_z(u_emb, k) for k in range(1, n_z)]
+    bags = spread(to_z, bags, True)
 
     def cot_body(spot, cot_ref, out):
         _, _, c = spot
@@ -184,7 +199,7 @@
         act, slope1_ref[...] = silu_parts(mul_tn(x_ref[...], w1_ref[...]))
         act = act.astype(BF)
         act_ref[...] = act
-        bottom, slope2_ref[...] = silu_parts(mul_nn(act, w2_ref[...]) + b_ref[1:2, :])
+        bottom, slope2_ref[...] = silu_parts(mul_nn(act, w2_ref[...]) + b_ref[0:1, :])
         bottom = bottom.astype(BF)
         bottom_ref[...] = bottom
         term_ref[...] = mul_nn(bottom, vb_ref[...])
@@ -205,85 +220,72 @@
         "mlp_forward",
     )
 
-    def cot_of(cot_ref, cot_in_ref, zk, c):
-        return jnp.concatenate(
-            [cot_ref[:, cols_of(2 * zk + c, width)], cot_in_ref[:, cols_of(zk, width)]], axis=0
-        ).astype(F32)
-
-    def low_body(spot, *refs):
-        bag = refs[:n_z]
-        term_ref, part_ref, pooled_ref = refs[n_z:]
+    def part_body(spot, *refs):
+        bag, u_refs = refs[:n_z], refs[n_z + 1 : n_z + 1 + n_rep]
+        own_u, refs = refs[n_z], refs[n_z + 1 + n_rep :]
+        cot_ref, cot_in_ref, term_ref, back_ref = refs[:4]
+        part_ref, pooled_ref, lift_ref, u_ref, gb_ref = refs[4:]
+        r, z, c = spot
+        u_ref[:width, :] = own_u[...]
+        for k in range(1, n_z):
+            for j in range(n_rep):
+                start = pl.multiple_of(k * width + (r ^ j) * u_part, TILE)
+                u_ref[pl.ds(start, u_part), :] = u_refs[j][(k - 1) * u_part : k * u_part, :]
         low = jnp.zeros((pair, width), F32)
+        back = jnp.zeros((pair, width), F32)
+        gb_ref[...] = jnp.zeros_like(gb_ref)
         for k in range(n_z):
-            base = k * width
+            rows = slice(k * width, (k + 1) * width)
             counts = bag[k][:n_bag, :]
             pooled = mul_tn(counts, bag[k][n_bag : 2 * n_bag, :]).astype(BF)
             low += mul_tn(counts, bag[k][2 * n_bag : 3 * n_bag, :])
-            pooled_ref[base : base + width, :] = pooled
+            pooled_ref[rows, :] = pooled
+            cot = jnp.concatenate(
+                [cot_ref[:, cols_of(2 * (z ^ k) + c, width)], cot_in_ref[:, cols_of(z ^ k, width)]],
+                axis=0,
+            )
+            d_lift = cot.astype(F32) * pooled.astype(F32)
+            gb_ref[k : k + 1, :] = jnp.sum(d_lift, axis=0, keepdims=True) * grad_scale
+            d_lift = d_lift.astype(BF)
+            lift_ref[rows, :] = d_lift
+            back += mul_nt(d_lift, u_ref[rows, :])
         part_ref[:own_rows, :] = (low[:own_rows] + term_ref[...]).astype(BF)
         part_ref[own_rows:pair, :] = low[own_rows:].astype(BF)
-
-    low_part, pooled = call(
-        low_body, [shape(pair, width), shape(n_z * pair, width)], (*bags, bot_term), "low_terms"
-    )
-    low_in = swap(low_part)
-
-    def summed(part_ref, in_ref):
-        own = part_ref[:own_rows, :].astype(F32) + in_ref[own_rows:, :].astype(F32)
-        other = part_ref[own_rows:, :].astype(F32) + in_ref[:own_rows, :].astype(F32)
+        part_ref[pair : pair + own_rows, :] = (back[:own_rows] + back_ref[...]).astype(BF)
+        part_ref[pair + own_rows :, :] = back[own_rows:].astype(BF)
+
+    part, pooled, d_lift, u_all, grad_b = call(
+        part_body,
+        [
+            shape(2 * pair, width),
+            shape(n_z * pair, width),
+            shape(n_z * pair, width),
+            shape(n_z * width, width),
+            shape(gb_rows, width, F32),
+        ],
+        (*bags, u_emb, *u_r, cot_cross, cot_in, bot_term, bot_back),
+        "partials",
+    )
+    part_in = swap(part)
+
+    def summed(part_ref, in_ref, start):
+        mid, end = start + own_rows, start + pair
+        own = part_ref[start:mid, :].astype(F32) + in_ref[mid:end, :].astype(F32)
+        other = part_ref[mid:end, :].astype(F32) + in_ref[start:mid, :].astype(F32)
         return own.astype(BF), other.astype(BF)
 
-    def u_grad_body(spot, part_ref, in_ref, pooled_ref, cot_ref, cot_in_ref, low_ref, lift_ref, gb_ref, *outs):
-        r, z, c = spot
-        *outs, stack = outs
-        low_ref[:own_rows, :], low_ref[own_rows:, :] = summed(part_ref, in_ref)
-        low = low_ref[...]
-        gb_ref[...] = jnp.zeros_like(gb_ref)
-        for k in range(n_z):
-            base = k * width
-            pooled_full = pooled_ref[base : base + width, :].astype(F32)
-            d_lift = cot_of(cot_ref, cot_in_ref, z ^ k, c) * pooled_full
-            gb_ref[k : k + 1, :] = jnp.sum(d_lift, axis=0, keepdims=True) * grad_scale
-            d_lift = d_lift.astype(BF)
-            lift_ref[base : base + width, :] = d_lift
-            stack[...] = (mul_tn(low, d_lift) * grad_scale).astype(BF)
-            for j, out in enumerate(outs):
-                out[k * u_part : (k + 1) * u_part, :] = stack[rows_of(r ^ j, u_part), :]
-
-    low, d_lift, grad_b, *u_outs = call(
-        u_grad_body,
-        [shape(pair, width), shape(n_z * pair, width), shape(gb_rows, width, F32)]
-        + [shape(n_z * u_part, width)] * n_rep,
-        (low_part, low_in, pooled, cot_cross, cot_in),
-        "u_grads",
-        [pltpu.VMEM((width, width), BF)],
-    )
-    u_ins = [u_outs[0]] + [to_rep(u_outs[j], j) for j in range(1, n_rep)]
-
-    def back_body(spot, *refs):
-        u_refs = refs[:n_z]
-        lift_ref, back_ref, part_ref = refs[n_z:]
-        back = jnp.zeros((pair, width), F32)
-        for k in range(n_z):
-            back += mul_nt(lift_ref[k * width : (k + 1) * width, :], u_refs[k][...])
-        part_ref[:own_rows, :] = (back[:own_rows] + back_ref[...]).astype(BF)
-        part_ref[own_rows:pair, :] = back[own_rows:].astype(BF)
-
-    (back_part,) = call(back_body, [shape(pair, width)], (*u_z, d_lift, bot_back), "back_terms")
-    back_in = swap(back_part)
-
     def dense_body(
-        spot, low_ref, part_ref, in_ref, act_ref, slope1_ref, bottom_ref, slope2_ref, cot_ref, x_ref,
+        spot, part_ref, in_ref, act_ref, slope1_ref, bottom_ref, slope2_ref, cot_ref, x_ref,
         w2_ref, vb_ref, ub_ref, b_ref, gb_ref,
         cross_ref, send_ref, keep_ref, pack, small,
     ):
         _, z, c = spot
-        low = low_ref[:own_rows, :]
-        d_low, _ = summed(part_ref, in_ref)
+        low, _ = summed(part_ref, in_ref, 0)
+        d_low, _ = summed(part_ref, in_ref, pair)
         bottom = bottom_ref[...]
         bottom_full = bottom.astype(F32)
         cot = cot_ref[...].astype(F32)
-        lift = mul_nn(low, ub_ref[...]) + b_ref[2:3, :] + 1.0
+        lift = mul_nn(low, ub_ref[...]) + b_ref[1:2, :] + 1.0
         cross_ref[...] = (bottom_full * lift).astype(BF)
         d_second = (cot * lift + mul_nt(d_low, vb_ref[...])) * slope2_ref[...]
         d_second_round = d_second.astype(BF)
@@ -338,7 +340,7 @@
         dense_body,
         [shape(own_rows, width), shape(half, width), shape(half, width)],
         (
-            low, back_part, back_in, act, slope1, bottom, slope2, cot_bottom, feats_t,
+            part, part_in, act, slope1, bottom, slope2, cot_bottom, feats_t,
             w_second, v_bot, u_bot, bias_rows, grad_b,
         ),
         "dense_grads",
@@ -348,37 +350,44 @@
 
     def table_body(spot, *refs):
         bag = refs[:n_z]
-        u_refs = refs[n_z : 2 * n_z]
-        low_ref, part_ref, in_ref, pooled_ref, cot_ref, cot_in_ref = refs[2 * n_z : 2 * n_z + 6]
-        own_ref, send_ref, out = refs[2 * n_z + 6 :]
+        u_ref, part_ref, in_ref, pooled_ref, lift_ref, cot_ref, cot_in_ref = refs[n_z : n_z + 7]
+        own_ref, send_ref, g_u, out = refs[n_z + 7 :]
         _, z, c = spot
-        low = low_ref[...]
-        d_low = jnp.concatenate(summed(part_ref, in_ref), axis=0)
+        low = jnp.concatenate(summed(part_ref, in_ref, 0), axis=0)
+        d_low = jnp.concatenate(summed(part_ref, in_ref, pair), axis=0)
         if bag_full > 2 * n_bag:
             out[...] = jnp.zeros_like(out)
         for k in range(n_z):
             base = k * width
             counts = bag[k][:n_bag, :]
             bias = bag[k][3 * n_bag :, :].astype(F32)[0:1]
-            lift = mul_nn(low, u_refs[k][...]) + bias + 1.0
+            lift = mul_nn(low, u_ref[base : base + width, :]) + bias + 1.0
             cross = (pooled_ref[base : base + width, :].astype(F32) * lift).astype(BF)
             own_ref[:, cols_of(z ^ k, width)] = cross[:own_rows]
             send_ref[:, cols_of(z ^ k, width)] = cross[own_rows:]
-            direct = (cot_of(cot_ref, cot_in_ref, z ^ k, c) * lift).astype(BF)
+            cot = jnp.concatenate(
+                [cot_ref[:, cols_of(2 * (z ^ k) + c, width)], cot_in_ref[:, cols_of(z ^ k, width)]],
+                axis=0,
+            )
+            direct = (cot.astype(F32) * lift).astype(BF)
+            g_u[base : base + width, :] = (
+                mul_tn(low, lift_ref[base : base + width, :]) * grad_scale
+            ).astype(BF)
             start = k * bag_full
             out[start : start + n_bag, :] = (mul_nn(counts, d_low) * grad_scale).astype(BF)
             out[start + n_bag : start + 2 * n_bag, :] = (
                 mul_nn(counts, direct) * grad_scale
             ).astype(BF)
 
-    cross_own, cross_out, bag_keep = call(
+    cross_own, cross_out, u_keep, bag_keep = call(
         table_body,
-        [shape(own_rows, n_z * width)] * 2 + [shape(n_z * bag_full, width)],
-        (*bags, *u_z, low, back_part, back_in, pooled, cot_cross, cot_in),
+        [shape(own_rows, n_z * width)] * 2
+        + [shape(n_z * width, width), shape(n_z * bag_full, width)],
+        (*bags, u_all, part, part_in, pooled, d_lift, cot_cross, cot_in),
         "table_grads",
     )
 
-    def pair_body(spot, keep_ref, in_ref, bag_ref, *outs):
+    def pair_body(spot, keep_ref, in_ref, u_ref, bag_ref, *outs):
         r, _, _ = spot
         for j, out in enumerate(outs):
             rows = rows_of(r ^ j, rep_part)
@@ -386,39 +395,55 @@
                 keep_ref[rows, :].astype(F32) + in_ref[rows, :].astype(F32)
             ).astype(BF)
             for k in range(n_z):
+                start = rep_part + k * tab_part
+                rows = pl.ds(pl.multiple_of(k * width + (r ^ j) * u_part, TILE), u_part)
+                out[start : start + u_part, :] = u_ref[rows, :]
                 rows = pl.ds(pl.multiple_of(k * bag_full + (r ^ j) * bag_part, TILE), bag_part)
-                start = rep_part + k * bag_part
-                out[start : start + bag_part, :] = bag_ref[rows, :]
+                out[start + u_part : start + tab_part, :] = bag_ref[rows, :]
 
     rep_outs = call(
         pair_body,
-        [shape(rep_part + n_z * bag_part, width)] * n_rep,
-        (dense_keep, dense_in, bag_keep),
+        [shape(rep_part + n_z * tab_part, width)] * n_rep,
+        (dense_keep, dense_in, u_keep, bag_keep),
         "pair_sum",
     )
-    rep_ins = [rep_outs[0]] + [to_rep(rep_outs[j], j) for j in range(1, n_rep)]
+    rep_ins = spread(to_rep, rep_outs)
     cross_in = swap(cross_out)
 
     def total(refs, first, count):
         return tree_sum([ref[first : first + count, :].astype(F32) for ref in refs]).astype(BF)
 
     def rep_body(spot, *refs):
-        ins, u_refs, outs = refs[:n_rep], refs[n_rep : 2 * n_rep], refs[2 * n_rep :]
+        ins, outs = refs[:n_rep], refs[n_rep:]
         dense = total(ins, 0, rep_part)
         for k, out in enumerate(outs):
             out[:rep_part, :] = dense
-            out[rep_part : rep_part + u_part, :] = total(u_refs, k * u_part, u_part)
-            out[rep_part + u_part :, :] = total(ins, rep_part + k * bag_part, bag_part)
-
-    z_outs = call(rep_body, [shape(z_rows, width)] * n_z, (*rep_ins, *u_ins), "rep_sum")
-    z_ins = [z_outs[0]] + [to_z(z_outs[k], k) for k in range(1, n_z)]
-
-    def z_body(spot, *refs):
+            out[rep_part:, :] = total(ins, rep_part + k * tab_part, tab_part)
+
+    z_outs = call(rep_body, [shape(z_rows, width)] * n_z, rep_ins, "rep_sum")
+    z_ins = spread(to_z, z_outs, True)
+
+    def cross_body(spot, own_ref, in_ref, out, done):
+        _, _, c = spot
+        done[...] = jnp.zeros_like(done)
+        for t in range(n_z):
+            cols = slice(t * width, (t + 1) * width)
+            out[:, cols_of(2 * t + c, width)] = own_ref[:, cols]
+            out[:, cols_of(2 * t + 1 - c, width)] = in_ref[:, cols]
+
+    cross_emb, cross_done = call(
+        cross_body,
+        [shape(own_rows, 2 * n_z * width), shape(8, 128, F32)],
+        (cross_own, cross_in),
+        "cross_rows",
+    )
+
+    def z_body(spot, _, *refs):
         refs[n_z][...] = total(refs[:n_z], 0, z_rows)
 
-    (mine,) = call(z_body, [shape(z_rows, width)], z_ins, "z_sum")
-
-    pieces = [mine] + [to_rep(mine, j) for j in range(1, n_rep)]
+    (mine,) = call(z_body, [shape(z_rows, width)], (cross_done, *z_ins), "z_sum")
+
+    pieces = spread(to_rep, [mine] * n_rep)
 
     def gather_body(spot, *refs):
         r, _, _ = spot
@@ -427,17 +452,6 @@
 
     (dense_own,) = call(gather_body, [shape(n_rep * dense_part, width)], pieces, "dense_gather")
     dense_other = swap(dense_own)
-
-    def cross_body(spot, own_ref, in_ref, out):
-        _, _, c = spot
-        for t in range(n_z):
-            cols = slice(t * width, (t + 1) * width)
-            out[:, cols_of(2 * t + c, width)] = own_ref[:, cols]
-            out[:, cols_of(2 * t + 1 - c, width)] = in_ref[:, cols]
-
-    (cross_emb,) = call(
-        cross_body, [shape(own_rows, 2 * n_z * width)], (cross_own, cross_in), "cross_rows"
-    )
 
     def table_last_body(spot, *refs):
         ins = refs[:n_rep]

time: 90.9 us -> 76.3 us (0.84)
  waiting for transfers between devices: 42.6 us -> 33.6 us
  Pallas kernels: 15.5 us -> 7.24 us
  local copies, waits for them, and re-layouts: 4.81 us -> 6.83 us
    ppermute x9, waiting for transfers between devices: 26.2 us -> 12.1 us  [to_z(): return lax.ppermute(value, 'z', [(i, i ^ k) for i in range(n_z)])]
    pallas_call x15 -> x14, Pallas kernels: 15.5 us -> 7.24 us  [run(): pl.pallas_call(placed, out_shape=out_shapes, in_specs=[in_vmem] * len(arg...]
    ppermute x9, waiting for transfers between devices: 15.1 us -> 19 us  [to_rep(): return lax.ppermute(value, 'rep', [(i, i ^ k) for i in range(n_rep)])]
    ppermute x9, starting transfers between devices: 10.6 us -> 11.7 us  [to_rep(): return lax.ppermute(value, 'rep', [(i, i ^ k) for i in range(n_rep)])]
    ppermute x6 -> x5, waiting for transfers between devices: 1.35 us -> 2.45 us  [swap(): return lax.ppermute(value, 'core', [(0, 1), (1, 0)])]
  transfers between devices with their start and end apart: 24 -> 23, of which waited for: 10 -> 13; matrix products, arithmetic and copies ran while one was open for 2% -> 3% of each run, Pallas kernels for 10% -> 5%
where the time goes in v2:
time: 76.3 us; the launch traced here: 75.5 us
  waiting for transfers between devices  33.6 us (44%)
  starting transfers between devices  26.7 us (35%)
  Pallas kernels  7.24 us (9%)
  local copies, waits for them, and re-layouts  6.83 us (9%)
  between operations  0.86 us (1%)
    ppermute x9, waiting for transfers between devices, to_rep(): return lax.ppermute(value, 'rep', [(i, i ^ k) for i in range(n_rep)])  19 us
    ppermute x9, starting transfers between devices, to_z(): return lax.ppermute(value, 'z', [(i, i ^ k) for i in range(n_z)])  14.6 us
    ppermute x9, waiting for transfers between devices, to_z(): return lax.ppermute(value, 'z', [(i, i ^ k) for i in range(n_z)])  12.1 us
    ppermute x9, starting transfers between devices, to_rep(): return lax.ppermute(value, 'rep', [(i, i ^ k) for i in range(n_rep)])  11.7 us
    pallas_call x14, Pallas kernels, run(): pl.pallas_call(placed, out_shape=out_shapes, in_specs=[in_vmem] * len(arg...  7.24 us
    unnamed x34, local copies, waits for them, and re-layouts  3.9 us
    ppermute x5, waiting for transfers between devices, swap(): return lax.ppermute(value, 'core', [(0, 1), (1, 0)])  2.45 us
  transfers between devices with their start and end apart: 23, of which 13 were waited for; matrix products, arithmetic and copies ran while one was open for 3% of the time, Pallas kernels for 5%

profile of v2, /device:TPU:0, one launch (start us, length us, event | category | flops | bytes accessed | tf_op | source)
XLA Modules:
  0.0 75.5 jit_solution(7156400641014211290)
XLA Ops:
  1.5 3.0 %collective-permute-start.3 = (bf16[64,256]{1,0:T(8,128)(2,1)S(1)}, bf16[64,256]{1,0:T(8,128)(2,1)S(1)}, u32[]{:S(2)}, u32[]{:S(2)}) collective-permute-start(bf16[64,256]{1,0:T(8,128)(2,1)S(1)} %constant_dynamic-slice_fusion), channel_id=1, source_target_pairs={{0,2},{2,0},{4,6},{6,4},{1,3},{3,1},{5,7},{7,5},{8,10},{10,8},{12,... | collective-permute-start | bytes 98312 | tf_op jit(solution)/shard_map/ppermute | solution.py:123
  4.5 2.6 %collective-permute-start.4 = (bf16[64,256]{1,0:T(8,128)(2,1)S(1)}, bf16[64,256]{1,0:T(8,128)(2,1)S(1)}, u32[]{:S(2)}, u32[]{:S(2)}) collective-permute-start(bf16[64,256]{1,0:T(8,128)(2,1)S(1)} %constant_dynamic-slice_fusion), channel_id=1, source_target_pairs={{0,4},{2,6},{4,0},{6,2},{1,5},{3,7},{5,1},{7,3},{8,12},{10,14},{12... | collective-permute-start | bytes 98312 | tf_op jit(solution)/shard_map/ppermute | solution.py:123
  10.7 1.0 %collective-permute-start = (bf16[208,256]{1,0:T(8,128)(2,1)S(1)}, bf16[208,256]{1,0:T(8,128)(2,1)S(1)}, u32[]{:S(2)}, u32[]{:S(2)}) collective-permute-start(bf16[208,256]{1,0:T(8,128)(2,1)S(1)} %get-tuple-element.54), channel_id=1, source_target_pairs={{0,2},{2,0},{4,6},{6,4},{1,3},{3,1},{5,7},{7,5},{8,10},{10,8},{12,... | collective-permute-start | bytes 319496 | tf_op jit(solution)/shard_map/ppermute | solution.py:123
  11.7 3.5 %collective-permute-start.1 = (bf16[208,256]{1,0:T(8,128)(2,1)S(1)}, bf16[208,256]{1,0:T(8,128)(2,1)S(1)}, u32[]{:S(2)}, u32[]{:S(2)}) collective-permute-start(bf16[208,256]{1,0:T(8,128)(2,1)S(1)} %get-tuple-element.55), channel_id=1, source_target_pairs={{0,4},{2,6},{4,0},{6,2},{1,5},{3,7},{5,1},{7,3},{8,12},{10,14},{12... | collective-permute-start | bytes 319496 | tf_op jit(solution)/shard_map/ppermute | solution.py:123
  17.1 1.7 %collective-permute-start.6 = (bf16[192,256]{1,0:T(8,128)(2,1)S(1)}, bf16[192,256]{1,0:T(8,128)(2,1)S(1)}, u32[]{:S(2)}, u32[]{:S(2)}) collective-permute-start(bf16[192,256]{1,0:T(8,128)(2,1)S(1)} %u_rows.1.refs_5_), channel_id=1, source_target_pairs={{0,8},{8,0},{16,24},{24,16},{1,9},{9,1},{17,25},{25,17},{2,10},{10... | collective-permute-start | bytes 294920 | tf_op jit(solution)/shard_map/ppermute | solution.py:126
  18.8 1.5 %collective-permute-start.7 = (bf16[192,256]{1,0:T(8,128)(2,1)S(1)}, bf16[192,256]{1,0:T(8,128)(2,1)S(1)}, u32[]{:S(2)}, u32[]{:S(2)}) collective-permute-start(bf16[192,256]{1,0:T(8,128)(2,1)S(1)} %u_rows.1.refs_5_), channel_id=1, source_target_pairs={{0,16},{8,24},{16,0},{24,8},{1,17},{9,25},{17,1},{25,9},{2,18},{10... | collective-permute-start | bytes 294920 | tf_op jit(solution)/shard_map/ppermute | solution.py:126
  20.4 1.4 %collective-permute-start.8 = (bf16[192,256]{1,0:T(8,128)(2,1)S(1)}, bf16[192,256]{1,0:T(8,128)(2,1)S(1)}, u32[]{:S(2)}, u32[]{:S(2)}) collective-permute-start(bf16[192,256]{1,0:T(8,128)(2,1)S(1)} %u_rows.1.refs_5_), channel_id=1, source_target_pairs={{0,24},{8,16},{16,8},{24,0},{1,25},{9,17},{17,9},{25,1},{2,26},{10... | collective-permute-start | bytes 294920 | tf_op jit(solution)/shard_map/ppermute | solution.py:126
  22.5 1.7 %collective-permute-done.2.refs_3_ = bf16[208,256]{1,0:T(8,128)(2,1)S(1)} collective-permute-done((bf16[208,256]{1,0:T(8,128)(2,1)S(1)}, bf16[208,256]{1,0:T(8,128)(2,1)S(1)}, u32[]{:S(2)}, u32[]{:S(2)}) %collective-permute-start.2) | collective-permute-done | bytes 106528 | tf_op jit(solution)/shard_map/ppermute | solution.py:123
  24.7 1.2 %collective-permute-done.8.refs_8_ = bf16[192,256]{1,0:T(8,128)(2,1)S(1)} collective-permute-done((bf16[192,256]{1,0:T(8,128)(2,1)S(1)}, bf16[192,256]{1,0:T(8,128)(2,1)S(1)}, u32[]{:S(2)}, u32[]{:S(2)}) %collective-permute-start.8) | collective-permute-done | bytes 98336 | tf_op jit(solution)/shard_map/ppermute | solution.py:126
  26.8 1.5 %collective-permute-done.10.refs_6_.refs_1_ = bf16[512,256]{1,0:T(8,128)(2,1)S(1)} collective-permute-done((bf16[512,256]{1,0:T(8,128)(2,1)S(1)}, bf16[512,256]{1,0:T(8,128)(2,1)S(1)}, u32[]{:S(2)}, u32[]{:S(2)}) %collective-permute-start.10) | collective-permute-done | bytes 262176 | tf_op jit(solution)/shard_map/ppermute | solution.py:120
  28.3 1.5 %dense_grads.1 = (bf16[128,256]{1,0:T(8,128)(2,1)}, bf16[832,256]{1,0:T(8,128)(2,1)S(1)}, bf16[832,256]{1,0:T(8,128)(2,1)S(1)}) custom-call(s32[8,128]{1,0:T(8,128)S(1)} %broadcast_in_dim.32.spot_ref, bf16[512,256]{1,0:T(8,128)(2,1)S(1)} %get-tuple-element.60.refs_5_.refs_0_, bf16[512,256]{1,0:T(8,128)(2,1)S(1)} %collective-permute-done.10.refs_6_.refs_1_, ...), custom_call_target="tpu_custom_call" | custom-call | flops 100000000 | bytes 3301376 | tf_op jit(solution)/shard_map/dense_grads/pallas_call | solution.py:58
  31.7 1.1 %collective-permute-start.13 = (bf16[592,256]{1,0:T(8,128)(2,1)S(1)}, bf16[592,256]{1,0:T(8,128)(2,1)S(1)}, u32[]{:S(2)}, u32[]{:S(2)}) collective-permute-start(bf16[592,256]{1,0:T(8,128)(2,1)S(1)} %get-tuple-element.78), channel_id=1, source_target_pairs={{0,8},{8,0},{16,24},{24,16},{1,9},{9,1},{17,25},{25,17},{2,10},{10... | collective-permute-start | bytes 909320 | tf_op jit(solution)/shard_map/ppermute | solution.py:126
  33.7 1.6 %collective-permute-start.15 = (bf16[592,256]{1,0:T(8,128)(2,1)S(1)}, bf16[592,256]{1,0:T(8,128)(2,1)S(1)}, u32[]{:S(2)}, u32[]{:S(2)}) collective-permute-start(bf16[592,256]{1,0:T(8,128)(2,1)S(1)} %get-tuple-element.80), channel_id=1, source_target_pairs={{0,24},{8,16},{16,8},{24,0},{1,25},{9,17},{17,9},{25,1},{2,26},{10... | collective-permute-start | bytes 909320 | tf_op jit(solution)/shard_map/ppermute | solution.py:126
  35.3 6.5 %collective-permute-done.13.refs_1_ = bf16[592,256]{1,0:T(8,128)(2,1)S(1)} collective-permute-done((bf16[592,256]{1,0:T(8,128)(2,1)S(1)}, bf16[592,256]{1,0:T(8,128)(2,1)S(1)}, u32[]{:S(2)}, u32[]{:S(2)}) %collective-permute-start.13) | collective-permute-done | bytes 303136 | tf_op jit(solution)/shard_map/ppermute | solution.py:126
  42.6 5.7 %collective-permute-done.15.refs_3_ = bf16[592,256]{1,0:T(8,128)(2,1)S(1)} collective-permute-done((bf16[592,256]{1,0:T(8,128)(2,1)S(1)}, bf16[592,256]{1,0:T(8,128)(2,1)S(1)}, u32[]{:S(2)}, u32[]{:S(2)}) %collective-permute-start.15) | collective-permute-done | bytes 303136 | tf_op jit(solution)/shard_map/ppermute | solution.py:126
  48.8 3.8 %collective-permute-start.17 = (bf16[304,256]{1,0:T(8,128)(2,1)S(1)}, bf16[304,256]{1,0:T(8,128)(2,1)S(1)}, u32[]{:S(2)}, u32[]{:S(2)}) collective-permute-start(bf16[304,256]{1,0:T(8,128)(2,1)S(1)} %get-tuple-element.83), channel_id=1, source_target_pairs={{0,4},{2,6},{4,0},{6,2},{1,5},{3,7},{5,1},{7,3},{8,12},{10,14},{12... | collective-permute-start | bytes 466952 | tf_op jit(solution)/shard_map/ppermute | solution.py:123
  53.8 2.0 %collective-permute-done.16.refs_2_ = bf16[304,256]{1,0:T(8,128)(2,1)S(1)} collective-permute-done((bf16[304,256]{1,0:T(8,128)(2,1)S(1)}, bf16[304,256]{1,0:T(8,128)(2,1)S(1)}, u32[]{:S(2)}, u32[]{:S(2)}) %collective-permute-start.16) | collective-permute-done | bytes 155680 | tf_op jit(solution)/shard_map/ppermute | solution.py:123
  55.8 8.4 %collective-permute-done.17.refs_3_ = bf16[304,256]{1,0:T(8,128)(2,1)S(1)} collective-permute-done((bf16[304,256]{1,0:T(8,128)(2,1)S(1)}, bf16[304,256]{1,0:T(8,128)(2,1)S(1)}, u32[]{:S(2)}, u32[]{:S(2)}) %collective-permute-start.17) | collective-permute-done | bytes 155680 | tf_op jit(solution)/shard_map/ppermute | solution.py:123
  64.9 1.2 %collective-permute-start.20 = (bf16[304,256]{1,0:T(8,128)(2,1)S(1)}, bf16[304,256]{1,0:T(8,128)(2,1)S(1)}, u32[]{:S(2)}, u32[]{:S(2)}) collective-permute-start(bf16[304,256]{1,0:T(8,128)(2,1)S(1)} %z_sum.1.refs_0_), channel_id=1, source_target_pairs={{0,16},{8,24},{16,0},{24,8},{1,17},{9,25},{17,1},{25,9},{2,18},{10... | collective-permute-start | bytes 466952 | tf_op jit(solution)/shard_map/ppermute | solution.py:126
  66.1 1.8 %collective-permute-start.21 = (bf16[304,256]{1,0:T(8,128)(2,1)S(1)}, bf16[304,256]{1,0:T(8,128)(2,1)S(1)}, u32[]{:S(2)}, u32[]{:S(2)}) collective-permute-start(bf16[304,256]{1,0:T(8,128)(2,1)S(1)} %z_sum.1.refs_0_), channel_id=1, source_target_pairs={{0,24},{8,16},{16,8},{24,0},{1,25},{9,17},{17,9},{25,1},{2,26},{10... | collective-permute-start | bytes 466952 | tf_op jit(solution)/shard_map/ppermute | solution.py:126
  67.8 1.7 %collective-permute-done.19.refs_1_ = bf16[304,256]{1,0:T(8,128)(2,1)S(1)} collective-permute-done((bf16[304,256]{1,0:T(8,128)(2,1)S(1)}, bf16[304,256]{1,0:T(8,128)(2,1)S(1)}, u32[]{:S(2)}, u32[]{:S(2)}) %collective-permute-start.19) | collective-permute-done | bytes 155680 | tf_op jit(solution)/shard_map/ppermute | solution.py:126
  70.1 2.1 %collective-permute-done.21.refs_3_ = bf16[304,256]{1,0:T(8,128)(2,1)S(1)} collective-permute-done((bf16[304,256]{1,0:T(8,128)(2,1)S(1)}, bf16[304,256]{1,0:T(8,128)(2,1)S(1)}, u32[]{:S(2)}, u32[]{:S(2)}) %collective-permute-start.21) | collective-permute-done | bytes 155680 | tf_op jit(solution)/shard_map/ppermute | solution.py:126
  72.4 1.0 %table_last.1 = (bf16[64,256]{1,0:T(8,128)(2,1)}, bf16[256,256]{1,0:T(8,128)(2,1)}, bf16[256,256]{1,0:T(8,128)(2,1)}, f32[16,1024]{1,0:T(8,128)S(1)}, f32[8,256]{1,0:T(8,128)S(1)}) custom-call(s32[8,128]{1,0:T(8,128)S(1)} %broadcast_in_dim.32.spot_ref, bf16[304,256]{1,0:T(8,128)(2,1)S(1)} %z_sum.1.refs_0_, ...), custom_call_target="tpu_custom_call" | custom-call | flops 100000000 | bytes 1159168 | tf_op jit(solution)/shard_map/table_last/pallas_call | solution.py:58
  74.5 1.0 %dense_last.1 = (bf16[1024,256]{1,0:T(8,128)(2,1)}, bf16[256,256]{1,0:T(8,128)(2,1)}, bf16[256,256]{1,0:T(8,128)(2,1)}) custom-call(s32[8,128]{1,0:T(8,128)S(1)} %broadcast_in_dim.32.spot_ref, bf16[768,256]{1,0:T(8,128)(2,1)S(1)} %dense_gather.1.refs_0_, bf16[768,256]{1,0:T(8,128)(2,1)S(1)} %collective-permute-done.22.refs_1_), custom_call_target="tpu_custom_call" | custom-call | flops 100000000 | bytes 1576960 | tf_op jit(solution)/shard_map/dense_last/pallas_call | solution.py:58
  (90 shorter events, 16.3 us)
Async XLA Ops:
  0.6 16.0 %copy-start = (bf16[128,2048]{1,0:T(8,128)(2,1)S(1)}, bf16[128,2048]{1,0:T(8,128)(2,1)}, u32[]{:S(2)}) copy-start(bf16[128,2048]{1,0:T(8,128)(2,1)} %refs_9_.4) | copy-start | bytes 1572868
  1.5 15.2 %collective-permute-start.3 = (bf16[64,256]{1,0:T(8,128)(2,1)S(1)}, bf16[64,256]{1,0:T(8,128)(2,1)S(1)}, u32[]{:S(2)}, u32[]{:S(2)}) collective-permute-start(bf16[64,256]{1,0:T(8,128)(2,1)S(1)} %constant_dynamic-slice_fusion), channel_id=1, source_target_pairs={{0,2},{2,0},{4,6},{6,4},{1,3},{3,1},{5,7},{7,5},{8,10},{10,8},{12,... | collective-permute-start | bytes 98312 | tf_op jit(solution)/shard_map/ppermute | solution.py:123
  4.5 12.5 %collective-permute-start.4 = (bf16[64,256]{1,0:T(8,128)(2,1)S(1)}, bf16[64,256]{1,0:T(8,128)(2,1)S(1)}, u32[]{:S(2)}, u32[]{:S(2)}) collective-permute-start(bf16[64,256]{1,0:T(8,128)(2,1)S(1)} %constant_dynamic-slice_fusion), channel_id=1, source_target_pairs={{0,4},{2,6},{4,0},{6,2},{1,5},{3,7},{5,1},{7,3},{8,12},{10,14},{12... | collective-permute-start | bytes 98312 | tf_op jit(solution)/shard_map/ppermute | solution.py:123
  7.1 10.0 %collective-permute-start.5 = (bf16[64,256]{1,0:T(8,128)(2,1)S(1)}, bf16[64,256]{1,0:T(8,128)(2,1)S(1)}, u32[]{:S(2)}, u32[]{:S(2)}) collective-permute-start(bf16[64,256]{1,0:T(8,128)(2,1)S(1)} %constant_dynamic-slice_fusion), channel_id=1, source_target_pairs={{0,6},{2,4},{4,2},{6,0},{1,7},{3,5},{5,3},{7,1},{8,14},{10,12},{12... | collective-permute-start | bytes 98312 | tf_op jit(solution)/shard_map/ppermute | solution.py:123
  10.7 8.1 %collective-permute-start = (bf16[208,256]{1,0:T(8,128)(2,1)S(1)}, bf16[208,256]{1,0:T(8,128)(2,1)S(1)}, u32[]{:S(2)}, u32[]{:S(2)}) collective-permute-start(bf16[208,256]{1,0:T(8,128)(2,1)S(1)} %get-tuple-element.54), channel_id=1, source_target_pairs={{0,2},{2,0},{4,6},{6,4},{1,3},{3,1},{5,7},{7,5},{8,10},{10,8},{12,... | collective-permute-start | bytes 319496 | tf_op jit(solution)/shard_map/ppermute | solution.py:123
  11.7 8.7 %collective-permute-start.1 = (bf16[208,256]{1,0:T(8,128)(2,1)S(1)}, bf16[208,256]{1,0:T(8,128)(2,1)S(1)}, u32[]{:S(2)}, u32[]{:S(2)}) collective-permute-start(bf16[208,256]{1,0:T(8,128)(2,1)S(1)} %get-tuple-element.55), channel_id=1, source_target_pairs={{0,4},{2,6},{4,0},{6,2},{1,5},{3,7},{5,1},{7,3},{8,12},{10,14},{12... | collective-permute-start | bytes 319496 | tf_op jit(solution)/shard_map/ppermute | solution.py:123
  16.7 9.1 %collective-permute-start.9 = (bf16[128,1024]{1,0:T(8,128)(2,1)S(1)}, bf16[128,1024]{1,0:T(8,128)(2,1)S(1)}, u32[]{:S(2)}, u32[]{:S(2)}) collective-permute-start(bf16[128,1024]{1,0:T(8,128)(2,1)S(1)} %cot_send.1), channel_id=1, source_target_pairs={{0,1},{1,0},{2,3},{3,2},{4,5},{5,4},{6,7},{7,6},{8,9},{9,8},{10,11... | collective-permute-start | bytes 786440 | tf_op jit(solution)/shard_map/ppermute | solution.py:120
  17.0 7.2 %collective-permute-start.2 = (bf16[208,256]{1,0:T(8,128)(2,1)S(1)}, bf16[208,256]{1,0:T(8,128)(2,1)S(1)}, u32[]{:S(2)}, u32[]{:S(2)}) collective-permute-start(bf16[208,256]{1,0:T(8,128)(2,1)S(1)} %get-tuple-element.56), channel_id=1, source_target_pairs={{0,6},{2,4},{4,2},{6,0},{1,7},{3,5},{5,3},{7,1},{8,14},{10,12},{12... | collective-permute-start | bytes 319496 | tf_op jit(solution)/shard_map/ppermute | solution.py:123
  17.1 7.1 %collective-permute-start.6 = (bf16[192,256]{1,0:T(8,128)(2,1)S(1)}, bf16[192,256]{1,0:T(8,128)(2,1)S(1)}, u32[]{:S(2)}, u32[]{:S(2)}) collective-permute-start(bf16[192,256]{1,0:T(8,128)(2,1)S(1)} %u_rows.1.refs_5_), channel_id=1, source_target_pairs={{0,8},{8,0},{16,24},{24,16},{1,9},{9,1},{17,25},{25,17},{2,10},{10... | collective-permute-start | bytes 294920 | tf_op jit(solution)/shard_map/ppermute | solution.py:126
  18.8 5.9 %collective-permute-start.7 = (bf16[192,256]{1,0:T(8,128)(2,1)S(1)}, bf16[192,256]{1,0:T(8,128)(2,1)S(1)}, u32[]{:S(2)}, u32[]{:S(2)}) collective-permute-start(bf16[192,256]{1,0:T(8,128)(2,1)S(1)} %u_rows.1.refs_5_), channel_id=1, source_target_pairs={{0,16},{8,24},{16,0},{24,8},{1,17},{9,25},{17,1},{25,9},{2,18},{10... | collective-permute-start | bytes 294920 | tf_op jit(solution)/shard_map/ppermute | solution.py:126
  20.4 5.5 %collective-permute-start.8 = (bf16[192,256]{1,0:T(8,128)(2,1)S(1)}, bf16[192,256]{1,0:T(8,128)(2,1)S(1)}, u32[]{:S(2)}, u32[]{:S(2)}) collective-permute-start(bf16[192,256]{1,0:T(8,128)(2,1)S(1)} %u_rows.1.refs_5_), channel_id=1, source_target_pairs={{0,24},{8,16},{16,8},{24,0},{1,25},{9,17},{17,9},{25,1},{2,26},{10... | collective-permute-start | bytes 294920 | tf_op jit(solution)/shard_map/ppermute | solution.py:126
  26.7 1.6 %collective-permute-start.10 = (bf16[512,256]{1,0:T(8,128)(2,1)S(1)}, bf16[512,256]{1,0:T(8,128)(2,1)S(1)}, u32[]{:S(2)}, u32[]{:S(2)}) collective-permute-start(bf16[512,256]{1,0:T(8,128)(2,1)S(1)} %get-tuple-element.60.refs_5_.refs_0_), channel_id=1, source_target_pairs={{0,1},{1,0},{2,3},{3,2},{4,5},{5,4},{6,7},{7,6},{8,9},{9,8},{10,11... | collective-permute-start | bytes 786440 | tf_op jit(solution)/shard_map/ppermute | solution.py:120
  29.8 1.8 %collective-permute-start.12 = (bf16[832,256]{1,0:T(8,128)(2,1)S(1)}, bf16[832,256]{1,0:T(8,128)(2,1)S(1)}, u32[]{:S(2)}, u32[]{:S(2)}) collective-permute-start(bf16[832,256]{1,0:T(8,128)(2,1)S(1)} %get-tuple-element.74), channel_id=1, source_target_pairs={{0,1},{1,0},{2,3},{3,2},{4,5},{5,4},{6,7},{7,6},{8,9},{9,8},{10,11... | collective-permute-start | bytes 1277960 | tf_op jit(solution)/shard_map/ppermute | solution.py:120
  31.7 10.1 %collective-permute-start.13 = (bf16[592,256]{1,0:T(8,128)(2,1)S(1)}, bf16[592,256]{1,0:T(8,128)(2,1)S(1)}, u32[]{:S(2)}, u32[]{:S(2)}) collective-permute-start(bf16[592,256]{1,0:T(8,128)(2,1)S(1)} %get-tuple-element.78), channel_id=1, source_target_pairs={{0,8},{8,0},{16,24},{24,16},{1,9},{9,1},{17,25},{25,17},{2,10},{10... | collective-permute-start | bytes 909320 | tf_op jit(solution)/shard_map/ppermute | solution.py:126
  32.8 9.7 %collective-permute-start.14 = (bf16[592,256]{1,0:T(8,128)(2,1)S(1)}, bf16[592,256]{1,0:T(8,128)(2,1)S(1)}, u32[]{:S(2)}, u32[]{:S(2)}) collective-permute-start(bf16[592,256]{1,0:T(8,128)(2,1)S(1)} %get-tuple-element.79), channel_id=1, source_target_pairs={{0,16},{8,24},{16,0},{24,8},{1,17},{9,25},{17,1},{25,9},{2,18},{10... | collective-permute-start | bytes 909320 | tf_op jit(solution)/shard_map/ppermute | solution.py:126
  33.7 14.6 %collective-permute-start.15 = (bf16[592,256]{1,0:T(8,128)(2,1)S(1)}, bf16[592,256]{1,0:T(8,128)(2,1)S(1)}, u32[]{:S(2)}, u32[]{:S(2)}) collective-permute-start(bf16[592,256]{1,0:T(8,128)(2,1)S(1)} %get-tuple-element.80), channel_id=1, source_target_pairs={{0,24},{8,16},{16,8},{24,0},{1,25},{9,17},{17,9},{25,1},{2,26},{10... | collective-permute-start | bytes 909320 | tf_op jit(solution)/shard_map/ppermute | solution.py:126
  35.3 17.6 %collective-permute-start.11 = (bf16[128,1024]{1,0:T(8,128)(2,1)S(1)}, bf16[128,1024]{1,0:T(8,128)(2,1)S(1)}, u32[]{:S(2)}, u32[]{:S(2)}) collective-permute-start(bf16[128,1024]{1,0:T(8,128)(2,1)S(1)} %get-tuple-element.64), channel_id=1, source_target_pairs={{0,1},{1,0},{2,3},{3,2},{4,5},{5,4},{6,7},{7,6},{8,9},{9,8},{10,11... | collective-permute-start | bytes 786440 | tf_op jit(solution)/shard_map/ppermute | solution.py:120
  48.4 7.4 %collective-permute-start.16 = (bf16[304,256]{1,0:T(8,128)(2,1)S(1)}, bf16[304,256]{1,0:T(8,128)(2,1)S(1)}, u32[]{:S(2)}, u32[]{:S(2)}) collective-permute-start(bf16[304,256]{1,0:T(8,128)(2,1)S(1)} %get-tuple-element.82), channel_id=1, source_target_pairs={{0,2},{2,0},{4,6},{6,4},{1,3},{3,1},{5,7},{7,5},{8,10},{10,8},{12,... | collective-permute-start | bytes 466952 | tf_op jit(solution)/shard_map/ppermute | solution.py:123
  48.8 15.4 %collective-permute-start.17 = (bf16[304,256]{1,0:T(8,128)(2,1)S(1)}, bf16[304,256]{1,0:T(8,128)(2,1)S(1)}, u32[]{:S(2)}, u32[]{:S(2)}) collective-permute-start(bf16[304,256]{1,0:T(8,128)(2,1)S(1)} %get-tuple-element.83), channel_id=1, source_target_pairs={{0,4},{2,6},{4,0},{6,2},{1,5},{3,7},{5,1},{7,3},{8,12},{10,14},{12... | collective-permute-start | bytes 466952 | tf_op jit(solution)/shard_map/ppermute | solution.py:123
  52.6 11.6 %collective-permute-start.18 = (bf16[304,256]{1,0:T(8,128)(2,1)S(1)}, bf16[304,256]{1,0:T(8,128)(2,1)S(1)}, u32[]{:S(2)}, u32[]{:S(2)}) collective-permute-start(bf16[304,256]{1,0:T(8,128)(2,1)S(1)} %get-tuple-element.84), channel_id=1, source_target_pairs={{0,6},{2,4},{4,2},{6,0},{1,7},{3,5},{5,3},{7,1},{8,14},{10,12},{12... | collective-permute-start | bytes 466952 | tf_op jit(solution)/shard_map/ppermute | solution.py:123
  64.3 5.3 %collective-permute-start.19 = (bf16[304,256]{1,0:T(8,128)(2,1)S(1)}, bf16[304,256]{1,0:T(8,128)(2,1)S(1)}, u32[]{:S(2)}, u32[]{:S(2)}) collective-permute-start(bf16[304,256]{1,0:T(8,128)(2,1)S(1)} %z_sum.1.refs_0_), channel_id=1, source_target_pairs={{0,8},{8,0},{16,24},{24,16},{1,9},{9,1},{17,25},{25,17},{2,10},{10... | collective-permute-start | bytes 466952 | tf_op jit(solution)/shard_map/ppermute | solution.py:126
  64.9 5.2 %collective-permute-start.20 = (bf16[304,256]{1,0:T(8,128)(2,1)S(1)}, bf16[304,256]{1,0:T(8,128)(2,1)S(1)}, u32[]{:S(2)}, u32[]{:S(2)}) collective-permute-start(bf16[304,256]{1,0:T(8,128)(2,1)S(1)} %z_sum.1.refs_0_), channel_id=1, source_target_pairs={{0,16},{8,24},{16,0},{24,8},{1,17},{9,25},{17,1},{25,9},{2,18},{10... | collective-permute-start | bytes 466952 | tf_op jit(solution)/shard_map/ppermute | solution.py:126
  66.1 6.1 %collective-permute-start.21 = (bf16[304,256]{1,0:T(8,128)(2,1)S(1)}, bf16[304,256]{1,0:T(8,128)(2,1)S(1)}, u32[]{:S(2)}, u32[]{:S(2)}) collective-permute-start(bf16[304,256]{1,0:T(8,128)(2,1)S(1)} %z_sum.1.refs_0_), channel_id=1, source_target_pairs={{0,24},{8,16},{16,8},{24,0},{1,25},{9,17},{17,9},{25,1},{2,26},{10... | collective-permute-start | bytes 466952 | tf_op jit(solution)/shard_map/ppermute | solution.py:126
  72.3 2.2 %collective-permute-start.22 = (bf16[768,256]{1,0:T(8,128)(2,1)S(1)}, bf16[768,256]{1,0:T(8,128)(2,1)S(1)}, u32[]{:S(2)}, u32[]{:S(2)}) collective-permute-start(bf16[768,256]{1,0:T(8,128)(2,1)S(1)} %dense_gather.1.refs_0_), channel_id=1, source_target_pairs={{0,1},{1,0},{2,3},{3,2},{4,5},{5,4},{6,7},{7,6},{8,9},{9,8},{10,11... | collective-permute-start | bytes 1179656 | tf_op jit(solution)/shard_map/ppermute | solution.py:120
  (16 other events, 59.9 us)

commit v3 on v2

--- a/solution.py
+++ b/solution.py
@@ -130,13 +130,16 @@
         got = {k: send(values[k], k) for k in (order if near_first else reversed(order))}
         return [values[0]] + [got[k] for k in order]
 
-    def call(body, out_shapes, args, name, scratch=()):
-        return run(body, out_shapes, (spots, *args), name, scratch)
+    def call(body, out_shapes, args, name, scratch=(), **options):
+        return run(body, out_shapes, (spots, *args), name, scratch, **options)
 
     spots = jnp.stack([lax.axis_index(name) for name in ("rep", "z", "core")]).astype(jnp.int32)
     spots = jnp.broadcast_to(jnp.pad(spots, (0, 5))[:, None], (8, 128))
 
-    u_mine = lax.dynamic_slice_in_dim(u_emb, lax.axis_index("rep") * u_part, u_part, 0)
+    def cut_body(spot, u_ref, out):
+        out[...] = u_ref[rows_of(spot[0], u_part), :]
+
+    (u_mine,) = call(cut_body, [shape(u_part, width)], (u_emb,), "u_cut", flops=2 * 10**10)
     u_z = spread(to_z, [u_mine] * n_z, True)[1:]
 
     def u_body(spot, *refs):
@@ -145,6 +148,7 @@
 
     (u_z,) = call(u_body, [shape((n_z - 1) * u_part, width)], u_z, "u_rows")
     u_r = spread(to_rep, [u_z] * n_rep)
+
     bias_rows = jnp.concatenate(
         [b[None].astype(F32) for b in (b_second, b_bot)] + [jnp.zeros((6, width), F32)]
     )
@@ -387,38 +391,91 @@
         "table_grads",
     )
 
+    rep_rows = rep_part + n_z * tab_part
+    cut = round_up(rep_rows // 2, TILE) - TILE if n_rep == 4 else rep_rows
+    if n_rep == 4:
+        homes = {
+            (0, 0): (0, 0), (2, 0): (0, cut), (1, 0): (1, 0), (3, 0): (1, cut),
+            (0, 1): (2, 0), (1, 1): (2, rep_rows - cut), (2, 1): (3, 0), (3, 1): (3, rep_rows - cut),
+        }
+        pair_shapes = [shape(2 * cut, width)] * 2 + [shape(2 * (rep_rows - cut), width)] * 2
+    else:
+        homes = {(j, 0): (j, 0) for j in range(n_rep)}
+        pair_shapes = [shape(rep_rows, width)] * n_rep
+
     def pair_body(spot, keep_ref, in_ref, u_ref, bag_ref, *outs):
         r, _, _ = spot
-        for j, out in enumerate(outs):
+
+        def put(j, first, value):
+            last = first + value.shape[0]
+            for part, (low, high) in enumerate(((0, cut), (cut, rep_rows))):
+                start, end = max(first, low), min(last, high)
+                if start < end:
+                    which, base = homes[j, part]
+                    outs[which][base + start - low : base + end - low, :] = value[
+                        start - first : end - first
+                    ]
+
+        for j in range(n_rep):
             rows = rows_of(r ^ j, rep_part)
-            out[:rep_part, :] = (
-                keep_ref[rows, :].astype(F32) + in_ref[rows, :].astype(F32)
-            ).astype(BF)
+            put(j, 0, (keep_ref[rows, :].astype(F32) + in_ref[rows, :].astype(F32)).astype(BF))
             for k in range(n_z):
                 start = rep_part + k * tab_part
                 rows = pl.ds(pl.multiple_of(k * width + (r ^ j) * u_part, TILE), u_part)
-                out[start : start + u_part, :] = u_ref[rows, :]
+                put(j, start, u_ref[rows, :])
                 rows = pl.ds(pl.multiple_of(k * bag_full + (r ^ j) * bag_part, TILE), bag_part)
-                out[start + u_part : start + tab_part, :] = bag_ref[rows, :]
-
-    rep_outs = call(
-        pair_body,
-        [shape(rep_part + n_z * tab_part, width)] * n_rep,
-        (dense_keep, dense_in, u_keep, bag_keep),
-        "pair_sum",
-    )
-    rep_ins = spread(to_rep, rep_outs)
-    cross_in = swap(cross_out)
+                put(j, start + u_part, bag_ref[rows, :])
+
+    outs = call(pair_body, pair_shapes, (dense_keep, dense_in, u_keep, bag_keep), "pair_sum")
 
     def total(refs, first, count):
         return tree_sum([ref[first : first + count, :].astype(F32) for ref in refs]).astype(BF)
 
+    if n_rep == 4:
+        one_in, two_in = to_rep(outs[1], 1), to_rep(outs[3], 2)
+
+        def half_body(spot, one_ref, one_in_ref, two_ref, two_in_ref, keep, one_out, two_out):
+            rest = rep_rows - cut
+            keep[:cut, :] = total((one_ref, one_in_ref), 0, cut)
+            one_out[...] = total((one_ref, one_in_ref), cut, cut)
+            keep[cut:, :] = total((two_ref, two_in_ref), 0, rest)
+            two_out[...] = total((two_ref, two_in_ref), rest, rest)
+
+        keep, one_out, two_out = call(
+            half_body,
+            [shape(rep_rows, width), shape(cut, width), shape(rep_rows - cut, width)],
+            (outs[0], one_in, outs[2], two_in),
+            "half_sum",
+        )
+        rep_ins = [keep, to_rep(one_out, 2), to_rep(two_out, 1)]
+    else:
+        rep_ins = spread(to_rep, outs)
+    cross_in = swap(cross_out)
+
     def rep_body(spot, *refs):
-        ins, outs = refs[:n_rep], refs[n_rep:]
-        dense = total(ins, 0, rep_part)
+        ins, outs = refs[: len(rep_ins)], refs[len(rep_ins) :]
+
+        def rows_sum(first, count):
+            if n_rep != 4:
+                return [total(ins, first, count)]
+            parts = []
+            if first < cut:
+                parts.append(total(ins[:2], first, min(count, cut - first)))
+            if first + count > cut:
+                start, end = max(first, cut), first + count
+                kept = ins[0][start:end, :].astype(F32)
+                parts.append((kept + ins[2][start - cut : end - cut, :].astype(F32)).astype(BF))
+            return parts
+
+        def put(out, at, parts):
+            for value in parts:
+                out[at : at + value.shape[0], :] = value
+                at += value.shape[0]
+
+        dense = rows_sum(0, rep_part)
         for k, out in enumerate(outs):
-            out[:rep_part, :] = dense
-            out[rep_part:, :] = total(ins, rep_part + k * tab_part, tab_part)
+            put(out, 0, dense)
+            put(out, rep_part, rows_sum(rep_part + k * tab_part, tab_part))
 
     z_outs = call(rep_body, [shape(z_rows, width)] * n_z, rep_ins, "rep_sum")
     z_ins = spread(to_z, z_outs, True)

time: 76.3 us -> 71.4 us (0.936)
  local copies, waits for them, and re-layouts: 6.83 us -> 3.66 us
  waiting for transfers between devices: 33.6 us -> 31.2 us
  starting transfers between devices: 26.7 us -> 27.7 us
    ppermute x9, waiting for transfers between devices: 12.1 us -> 9.68 us  [to_z(): return lax.ppermute(value, 'z', [(i, i ^ k) for i in range(n_z)])]
    unnamed x34, local copies, waits for them, and re-layouts: 3.9 us -> 2.2 us
    ppermute x9 -> x10, starting transfers between devices: 11.7 us -> 12.7 us  [to_rep(): return lax.ppermute(value, 'rep', [(i, i ^ k) for i in range(n_rep)])]
    dynamic_slice x1 -> x0, local copies, waits for them, and re-layouts: 0.82 us -> none  [local(): lax.dynamic_slice_in_dim(u_emb, lax.axis_index('rep') * u_part, u_part, 0)]
    pallas_call x14 -> x16, Pallas kernels: 7.24 us -> 7.36 us  [run(): pl.pallas_call(placed, out_shape=out_shapes, in_specs=[in_vmem] * len(arg...]
    ppermute x9 -> x10, waiting for transfers between devices: 19 us -> 19.1 us  [to_rep(): return lax.ppermute(value, 'rep', [(i, i ^ k) for i in range(n_rep)])]
  transfers between devices with their start and end apart: 23 -> 24, of which waited for: 13 -> 12; matrix products, arithmetic and copies ran while one was open for 3% -> 2% of each run, Pallas kernels for 5% -> 5%
where the time goes in v3:
time: 71.4 us; the launch traced here: 71.1 us
  waiting for transfers between devices  31.2 us (44%)
  starting transfers between devices  27.7 us (39%)
  Pallas kernels  7.36 us (10%)
  local copies, waits for them, and re-layouts  3.66 us (5%)
  between operations  0.9 us (1%)
    ppermute x10, waiting for transfers between devices, to_rep(): return lax.ppermute(value, 'rep', [(i, i ^ k) for i in range(n_rep)])  19.1 us
    ppermute x9, starting transfers between devices, to_z(): return lax.ppermute(value, 'z', [(i, i ^ k) for i in range(n_z)])  14.6 us
    ppermute x10, starting transfers between devices, to_rep(): return lax.ppermute(value, 'rep', [(i, i ^ k) for i in range(n_rep)])  12.7 us
    ppermute x9, waiting for transfers between devices, to_z(): return lax.ppermute(value, 'z', [(i, i ^ k) for i in range(n_z)])  9.68 us
    pallas_call x16, Pallas kernels, run(): pl.pallas_call(placed, out_shape=out_shapes, in_specs=[in_vmem] * len(arg...  7.36 us
    ppermute x5, waiting for transfers between devices, swap(): return lax.ppermute(value, 'core', [(0, 1), (1, 0)])  2.46 us
    unnamed x34, local copies, waits for them, and re-layouts  2.2 us
  transfers between devices with their start and end apart: 24, of which 12 were waited for; matrix products, arithmetic and copies ran while one was open for 2% of the time, Pallas kernels for 5%

profile of v3, /device:TPU:0, one launch (start us, length us, event | category | flops | bytes accessed | tf_op | source)
XLA Modules:
  0.0 71.1 jit_solution(544025687449925857)
XLA Ops:
  1.8 3.1 %collective-permute-start.3 = (bf16[64,256]{1,0:T(8,128)(2,1)S(1)}, bf16[64,256]{1,0:T(8,128)(2,1)S(1)}, u32[]{:S(2)}, u32[]{:S(2)}) collective-permute-start(bf16[64,256]{1,0:T(8,128)(2,1)S(1)} %u_cut.1), channel_id=1, source_target_pairs={{0,2},{2,0},{4,6},{6,4},{1,3},{3,1},{5,7},{7,5},{8,10},{10,8},{12,... | collective-permute-start | bytes 98312 | tf_op jit(solution)/shard_map/ppermute | solution.py:123
  4.9 2.6 %collective-permute-start.4 = (bf16[64,256]{1,0:T(8,128)(2,1)S(1)}, bf16[64,256]{1,0:T(8,128)(2,1)S(1)}, u32[]{:S(2)}, u32[]{:S(2)}) collective-permute-start(bf16[64,256]{1,0:T(8,128)(2,1)S(1)} %u_cut.1), channel_id=1, source_target_pairs={{0,4},{2,6},{4,0},{6,2},{1,5},{3,7},{5,1},{7,3},{8,12},{10,14},{12... | collective-permute-start | bytes 98312 | tf_op jit(solution)/shard_map/ppermute | solution.py:123
  7.7 1.0 %collective-permute-start = (bf16[208,256]{1,0:T(8,128)(2,1)S(1)}, bf16[208,256]{1,0:T(8,128)(2,1)S(1)}, u32[]{:S(2)}, u32[]{:S(2)}) collective-permute-start(bf16[208,256]{1,0:T(8,128)(2,1)S(1)} %get-tuple-element.57), channel_id=1, source_target_pairs={{0,2},{2,0},{4,6},{6,4},{1,3},{3,1},{5,7},{7,5},{8,10},{10,8},{12,... | collective-permute-start | bytes 319496 | tf_op jit(solution)/shard_map/ppermute | solution.py:123
  8.6 3.5 %collective-permute-start.1 = (bf16[208,256]{1,0:T(8,128)(2,1)S(1)}, bf16[208,256]{1,0:T(8,128)(2,1)S(1)}, u32[]{:S(2)}, u32[]{:S(2)}) collective-permute-start(bf16[208,256]{1,0:T(8,128)(2,1)S(1)} %get-tuple-element.58), channel_id=1, source_target_pairs={{0,4},{2,6},{4,0},{6,2},{1,5},{3,7},{5,1},{7,3},{8,12},{10,14},{12... | collective-permute-start | bytes 319496 | tf_op jit(solution)/shard_map/ppermute | solution.py:123
  14.1 1.7 %collective-permute-start.6 = (bf16[192,256]{1,0:T(8,128)(2,1)S(1)}, bf16[192,256]{1,0:T(8,128)(2,1)S(1)}, u32[]{:S(2)}, u32[]{:S(2)}) collective-permute-start(bf16[192,256]{1,0:T(8,128)(2,1)S(1)} %u_rows.1.refs_5_), channel_id=1, source_target_pairs={{0,8},{8,0},{16,24},{24,16},{1,9},{9,1},{17,25},{25,17},{2,10},{10... | collective-permute-start | bytes 294920 | tf_op jit(solution)/shard_map/ppermute | solution.py:126
  15.8 1.5 %collective-permute-start.7 = (bf16[192,256]{1,0:T(8,128)(2,1)S(1)}, bf16[192,256]{1,0:T(8,128)(2,1)S(1)}, u32[]{:S(2)}, u32[]{:S(2)}) collective-permute-start(bf16[192,256]{1,0:T(8,128)(2,1)S(1)} %u_rows.1.refs_5_), channel_id=1, source_target_pairs={{0,16},{8,24},{16,0},{24,8},{1,17},{9,25},{17,1},{25,9},{2,18},{10... | collective-permute-start | bytes 294920 | tf_op jit(solution)/shard_map/ppermute | solution.py:126
  17.3 1.7 %collective-permute-start.8 = (bf16[192,256]{1,0:T(8,128)(2,1)S(1)}, bf16[192,256]{1,0:T(8,128)(2,1)S(1)}, u32[]{:S(2)}, u32[]{:S(2)}) collective-permute-start(bf16[192,256]{1,0:T(8,128)(2,1)S(1)} %u_rows.1.refs_5_), channel_id=1, source_target_pairs={{0,24},{8,16},{16,8},{24,0},{1,25},{9,17},{17,9},{25,1},{2,26},{10... | collective-permute-start | bytes 294920 | tf_op jit(solution)/shard_map/ppermute | solution.py:126
  19.9 1.3 %collective-permute-done.2.refs_3_ = bf16[208,256]{1,0:T(8,128)(2,1)S(1)} collective-permute-done((bf16[208,256]{1,0:T(8,128)(2,1)S(1)}, bf16[208,256]{1,0:T(8,128)(2,1)S(1)}, u32[]{:S(2)}, u32[]{:S(2)}) %collective-permute-start.2) | collective-permute-done | bytes 106528 | tf_op jit(solution)/shard_map/ppermute | solution.py:123
  21.7 1.1 %collective-permute-done.8.refs_8_ = bf16[192,256]{1,0:T(8,128)(2,1)S(1)} collective-permute-done((bf16[192,256]{1,0:T(8,128)(2,1)S(1)}, bf16[192,256]{1,0:T(8,128)(2,1)S(1)}, u32[]{:S(2)}, u32[]{:S(2)}) %collective-permute-start.8) | collective-permute-done | bytes 98336 | tf_op jit(solution)/shard_map/ppermute | solution.py:126
  23.8 1.5 %collective-permute-done.10.refs_6_.refs_1_ = bf16[512,256]{1,0:T(8,128)(2,1)S(1)} collective-permute-done((bf16[512,256]{1,0:T(8,128)(2,1)S(1)}, bf16[512,256]{1,0:T(8,128)(2,1)S(1)}, u32[]{:S(2)}, u32[]{:S(2)}) %collective-permute-start.10) | collective-permute-done | bytes 262176 | tf_op jit(solution)/shard_map/ppermute | solution.py:120
  25.3 1.5 %dense_grads.1 = (bf16[128,256]{1,0:T(8,128)(2,1)}, bf16[832,256]{1,0:T(8,128)(2,1)S(1)}, bf16[832,256]{1,0:T(8,128)(2,1)S(1)}) custom-call(s32[8,128]{1,0:T(8,128)S(1)} %broadcast_in_dim.32.spot_ref, bf16[512,256]{1,0:T(8,128)(2,1)S(1)} %get-tuple-element.63.refs_5_.refs_0_, bf16[512,256]{1,0:T(8,128)(2,1)S(1)} %collective-permute-done.10.refs_6_.refs_1_, ...), custom_call_target="tpu_custom_call" | custom-call | flops 100000000 | bytes 3301376 | tf_op jit(solution)/shard_map/dense_grads/pallas_call | solution.py:58
  28.7 1.4 %collective-permute-start.14 = (bf16[608,256]{1,0:T(8,128)(2,1)S(1)}, bf16[608,256]{1,0:T(8,128)(2,1)S(1)}, u32[]{:S(2)}, u32[]{:S(2)}) collective-permute-start(bf16[608,256]{1,0:T(8,128)(2,1)S(1)} %get-tuple-element.83), channel_id=1, source_target_pairs={{0,16},{8,24},{16,0},{24,8},{1,17},{9,25},{17,1},{25,9},{2,18},{10... | collective-permute-start | bytes 933896 | tf_op jit(solution)/shard_map/ppermute | solution.py:126
  30.1 1.0 %collective-permute-start.13 = (bf16[576,256]{1,0:T(8,128)(2,1)S(1)}, bf16[576,256]{1,0:T(8,128)(2,1)S(1)}, u32[]{:S(2)}, u32[]{:S(2)}) collective-permute-start(bf16[576,256]{1,0:T(8,128)(2,1)S(1)} %get-tuple-element.81), channel_id=1, source_target_pairs={{0,8},{8,0},{16,24},{24,16},{1,9},{9,1},{17,25},{25,17},{2,10},{10... | collective-permute-start | bytes 884744 | tf_op jit(solution)/shard_map/ppermute | solution.py:126
  31.1 7.8 %collective-permute-done.13.refs_1_ = bf16[576,256]{1,0:T(8,128)(2,1)S(1)} collective-permute-done((bf16[576,256]{1,0:T(8,128)(2,1)S(1)}, bf16[576,256]{1,0:T(8,128)(2,1)S(1)}, u32[]{:S(2)}, u32[]{:S(2)}) %collective-permute-start.13) | collective-permute-done | bytes 294944 | tf_op jit(solution)/shard_map/ppermute | solution.py:126
  39.0 1.0 %collective-permute-start.16 = (bf16[304,256]{1,0:T(8,128)(2,1)S(1)}, bf16[304,256]{1,0:T(8,128)(2,1)S(1)}, u32[]{:S(2)}, u32[]{:S(2)}) collective-permute-start(bf16[304,256]{1,0:T(8,128)(2,1)S(1)} %get-tuple-element.86), channel_id=1, source_target_pairs={{0,8},{8,0},{16,24},{24,16},{1,9},{9,1},{17,25},{25,17},{2,10},{10... | collective-permute-start | bytes 466952 | tf_op jit(solution)/shard_map/ppermute | solution.py:126
  40.8 4.4 %collective-permute-done.15.refs_1_ = bf16[288,256]{1,0:T(8,128)(2,1)S(1)} collective-permute-done((bf16[288,256]{1,0:T(8,128)(2,1)S(1)}, bf16[288,256]{1,0:T(8,128)(2,1)S(1)}, u32[]{:S(2)}, u32[]{:S(2)}) %collective-permute-start.15) | collective-permute-done | bytes 147488 | tf_op jit(solution)/shard_map/ppermute | solution.py:126
  45.8 3.1 %collective-permute-start.18 = (bf16[304,256]{1,0:T(8,128)(2,1)S(1)}, bf16[304,256]{1,0:T(8,128)(2,1)S(1)}, u32[]{:S(2)}, u32[]{:S(2)}) collective-permute-start(bf16[304,256]{1,0:T(8,128)(2,1)S(1)} %get-tuple-element.89), channel_id=1, source_target_pairs={{0,4},{2,6},{4,0},{6,2},{1,5},{3,7},{5,1},{7,3},{8,12},{10,14},{12... | collective-permute-start | bytes 466952 | tf_op jit(solution)/shard_map/ppermute | solution.py:123
  51.3 7.7 %collective-permute-done.18.refs_3_ = bf16[304,256]{1,0:T(8,128)(2,1)S(1)} collective-permute-done((bf16[304,256]{1,0:T(8,128)(2,1)S(1)}, bf16[304,256]{1,0:T(8,128)(2,1)S(1)}, u32[]{:S(2)}, u32[]{:S(2)}) %collective-permute-start.18) | collective-permute-done | bytes 155680 | tf_op jit(solution)/shard_map/ppermute | solution.py:123
  59.0 1.7 %collective-permute-start.20 = (bf16[304,256]{1,0:T(8,128)(2,1)S(1)}, bf16[304,256]{1,0:T(8,128)(2,1)S(1)}, u32[]{:S(2)}, u32[]{:S(2)}) collective-permute-start(bf16[304,256]{1,0:T(8,128)(2,1)S(1)} %z_sum.1.refs_0_), channel_id=1, source_target_pairs={{0,8},{8,0},{16,24},{24,16},{1,9},{9,1},{17,25},{25,17},{2,10},{10... | collective-permute-start | bytes 466952 | tf_op jit(solution)/shard_map/ppermute | solution.py:126
  62.6 1.7 %collective-permute-done.20.refs_1_ = bf16[304,256]{1,0:T(8,128)(2,1)S(1)} collective-permute-done((bf16[304,256]{1,0:T(8,128)(2,1)S(1)}, bf16[304,256]{1,0:T(8,128)(2,1)S(1)}, u32[]{:S(2)}, u32[]{:S(2)}) %collective-permute-start.20) | collective-permute-done | bytes 155680 | tf_op jit(solution)/shard_map/ppermute | solution.py:126
  64.3 1.6 %collective-permute-done.21.refs_2_ = bf16[304,256]{1,0:T(8,128)(2,1)S(1)} collective-permute-done((bf16[304,256]{1,0:T(8,128)(2,1)S(1)}, bf16[304,256]{1,0:T(8,128)(2,1)S(1)}, u32[]{:S(2)}, u32[]{:S(2)}) %collective-permute-start.21) | collective-permute-done | bytes 155680 | tf_op jit(solution)/shard_map/ppermute | solution.py:126
  66.0 1.8 %collective-permute-done.22.refs_3_ = bf16[304,256]{1,0:T(8,128)(2,1)S(1)} collective-permute-done((bf16[304,256]{1,0:T(8,128)(2,1)S(1)}, bf16[304,256]{1,0:T(8,128)(2,1)S(1)}, u32[]{:S(2)}, u32[]{:S(2)}) %collective-permute-start.22) | collective-permute-done | bytes 155680 | tf_op jit(solution)/shard_map/ppermute | solution.py:126
  68.0 1.0 %table_last.1 = (bf16[64,256]{1,0:T(8,128)(2,1)}, bf16[256,256]{1,0:T(8,128)(2,1)}, bf16[256,256]{1,0:T(8,128)(2,1)}, f32[16,1024]{1,0:T(8,128)S(1)}, f32[8,256]{1,0:T(8,128)S(1)}) custom-call(s32[8,128]{1,0:T(8,128)S(1)} %broadcast_in_dim.32.spot_ref, bf16[304,256]{1,0:T(8,128)(2,1)S(1)} %z_sum.1.refs_0_, ...), custom_call_target="tpu_custom_call" | custom-call | flops 100000000 | bytes 1159168 | tf_op jit(solution)/shard_map/table_last/pallas_call | solution.py:58
  70.1 1.0 %dense_last.1 = (bf16[1024,256]{1,0:T(8,128)(2,1)}, bf16[256,256]{1,0:T(8,128)(2,1)}, bf16[256,256]{1,0:T(8,128)(2,1)}) custom-call(s32[8,128]{1,0:T(8,128)S(1)} %broadcast_in_dim.32.spot_ref, bf16[768,256]{1,0:T(8,128)(2,1)S(1)} %dense_gather.1.refs_0_, bf16[768,256]{1,0:T(8,128)(2,1)S(1)} %collective-permute-done.23.refs_1_), custom_call_target="tpu_custom_call" | custom-call | flops 100000000 | bytes 1576960 | tf_op jit(solution)/shard_map/dense_last/pallas_call | solution.py:58
  (93 shorter events, 14.4 us)
Async XLA Ops:
  1.8 11.9 %collective-permute-start.3 = (bf16[64,256]{1,0:T(8,128)(2,1)S(1)}, bf16[64,256]{1,0:T(8,128)(2,1)S(1)}, u32[]{:S(2)}, u32[]{:S(2)}) collective-permute-start(bf16[64,256]{1,0:T(8,128)(2,1)S(1)} %u_cut.1), channel_id=1, source_target_pairs={{0,2},{2,0},{4,6},{6,4},{1,3},{3,1},{5,7},{7,5},{8,10},{10,8},{12,... | collective-permute-start | bytes 98312 | tf_op jit(solution)/shard_map/ppermute | solution.py:123
  4.9 9.1 %collective-permute-start.4 = (bf16[64,256]{1,0:T(8,128)(2,1)S(1)}, bf16[64,256]{1,0:T(8,128)(2,1)S(1)}, u32[]{:S(2)}, u32[]{:S(2)}) collective-permute-start(bf16[64,256]{1,0:T(8,128)(2,1)S(1)} %u_cut.1), channel_id=1, source_target_pairs={{0,4},{2,6},{4,0},{6,2},{1,5},{3,7},{5,1},{7,3},{8,12},{10,14},{12... | collective-permute-start | bytes 98312 | tf_op jit(solution)/shard_map/ppermute | solution.py:123
  7.5 6.6 %collective-permute-start.5 = (bf16[64,256]{1,0:T(8,128)(2,1)S(1)}, bf16[64,256]{1,0:T(8,128)(2,1)S(1)}, u32[]{:S(2)}, u32[]{:S(2)}) collective-permute-start(bf16[64,256]{1,0:T(8,128)(2,1)S(1)} %u_cut.1), channel_id=1, source_target_pairs={{0,6},{2,4},{4,2},{6,0},{1,7},{3,5},{5,3},{7,1},{8,14},{10,12},{12... | collective-permute-start | bytes 98312 | tf_op jit(solution)/shard_map/ppermute | solution.py:123
  7.7 8.1 %collective-permute-start = (bf16[208,256]{1,0:T(8,128)(2,1)S(1)}, bf16[208,256]{1,0:T(8,128)(2,1)S(1)}, u32[]{:S(2)}, u32[]{:S(2)}) collective-permute-start(bf16[208,256]{1,0:T(8,128)(2,1)S(1)} %get-tuple-element.57), channel_id=1, source_target_pairs={{0,2},{2,0},{4,6},{6,4},{1,3},{3,1},{5,7},{7,5},{8,10},{10,8},{12,... | collective-permute-start | bytes 319496 | tf_op jit(solution)/shard_map/ppermute | solution.py:123
  8.6 8.7 %collective-permute-start.1 = (bf16[208,256]{1,0:T(8,128)(2,1)S(1)}, bf16[208,256]{1,0:T(8,128)(2,1)S(1)}, u32[]{:S(2)}, u32[]{:S(2)}) collective-permute-start(bf16[208,256]{1,0:T(8,128)(2,1)S(1)} %get-tuple-element.58), channel_id=1, source_target_pairs={{0,4},{2,6},{4,0},{6,2},{1,5},{3,7},{5,1},{7,3},{8,12},{10,14},{12... | collective-permute-start | bytes 319496 | tf_op jit(solution)/shard_map/ppermute | solution.py:123
  13.7 9.1 %collective-permute-start.9 = (bf16[128,1024]{1,0:T(8,128)(2,1)S(1)}, bf16[128,1024]{1,0:T(8,128)(2,1)S(1)}, u32[]{:S(2)}, u32[]{:S(2)}) collective-permute-start(bf16[128,1024]{1,0:T(8,128)(2,1)S(1)} %cot_send.1), channel_id=1, source_target_pairs={{0,1},{1,0},{2,3},{3,2},{4,5},{5,4},{6,7},{7,6},{8,9},{9,8},{10,11... | collective-permute-start | bytes 786440 | tf_op jit(solution)/shard_map/ppermute | solution.py:120
  14.0 7.2 %collective-permute-start.2 = (bf16[208,256]{1,0:T(8,128)(2,1)S(1)}, bf16[208,256]{1,0:T(8,128)(2,1)S(1)}, u32[]{:S(2)}, u32[]{:S(2)}) collective-permute-start(bf16[208,256]{1,0:T(8,128)(2,1)S(1)} %get-tuple-element.59), channel_id=1, source_target_pairs={{0,6},{2,4},{4,2},{6,0},{1,7},{3,5},{5,3},{7,1},{8,14},{10,12},{12... | collective-permute-start | bytes 319496 | tf_op jit(solution)/shard_map/ppermute | solution.py:123
  14.1 7.1 %collective-permute-start.6 = (bf16[192,256]{1,0:T(8,128)(2,1)S(1)}, bf16[192,256]{1,0:T(8,128)(2,1)S(1)}, u32[]{:S(2)}, u32[]{:S(2)}) collective-permute-start(bf16[192,256]{1,0:T(8,128)(2,1)S(1)} %u_rows.1.refs_5_), channel_id=1, source_target_pairs={{0,8},{8,0},{16,24},{24,16},{1,9},{9,1},{17,25},{25,17},{2,10},{10... | collective-permute-start | bytes 294920 | tf_op jit(solution)/shard_map/ppermute | solution.py:126
  15.8 5.9 %collective-permute-start.7 = (bf16[192,256]{1,0:T(8,128)(2,1)S(1)}, bf16[192,256]{1,0:T(8,128)(2,1)S(1)}, u32[]{:S(2)}, u32[]{:S(2)}) collective-permute-start(bf16[192,256]{1,0:T(8,128)(2,1)S(1)} %u_rows.1.refs_5_), channel_id=1, source_target_pairs={{0,16},{8,24},{16,0},{24,8},{1,17},{9,25},{17,1},{25,9},{2,18},{10... | collective-permute-start | bytes 294920 | tf_op jit(solution)/shard_map/ppermute | solution.py:126
  17.3 5.5 %collective-permute-start.8 = (bf16[192,256]{1,0:T(8,128)(2,1)S(1)}, bf16[192,256]{1,0:T(8,128)(2,1)S(1)}, u32[]{:S(2)}, u32[]{:S(2)}) collective-permute-start(bf16[192,256]{1,0:T(8,128)(2,1)S(1)} %u_rows.1.refs_5_), channel_id=1, source_target_pairs={{0,24},{8,16},{16,8},{24,0},{1,25},{9,17},{17,9},{25,1},{2,26},{10... | collective-permute-start | bytes 294920 | tf_op jit(solution)/shard_map/ppermute | solution.py:126
  23.7 1.6 %collective-permute-start.10 = (bf16[512,256]{1,0:T(8,128)(2,1)S(1)}, bf16[512,256]{1,0:T(8,128)(2,1)S(1)}, u32[]{:S(2)}, u32[]{:S(2)}) collective-permute-start(bf16[512,256]{1,0:T(8,128)(2,1)S(1)} %get-tuple-element.63.refs_5_.refs_0_), channel_id=1, source_target_pairs={{0,1},{1,0},{2,3},{3,2},{4,5},{5,4},{6,7},{7,6},{8,9},{9,8},{10,11... | collective-permute-start | bytes 786440 | tf_op jit(solution)/shard_map/ppermute | solution.py:120
  26.7 1.8 %collective-permute-start.12 = (bf16[832,256]{1,0:T(8,128)(2,1)S(1)}, bf16[832,256]{1,0:T(8,128)(2,1)S(1)}, u32[]{:S(2)}, u32[]{:S(2)}) collective-permute-start(bf16[832,256]{1,0:T(8,128)(2,1)S(1)} %get-tuple-element.77), channel_id=1, source_target_pairs={{0,1},{1,0},{2,3},{3,2},{4,5},{5,4},{6,7},{7,6},{8,9},{9,8},{10,11... | collective-permute-start | bytes 1277960 | tf_op jit(solution)/shard_map/ppermute | solution.py:120
  28.7 10.2 %collective-permute-start.14 = (bf16[608,256]{1,0:T(8,128)(2,1)S(1)}, bf16[608,256]{1,0:T(8,128)(2,1)S(1)}, u32[]{:S(2)}, u32[]{:S(2)}) collective-permute-start(bf16[608,256]{1,0:T(8,128)(2,1)S(1)} %get-tuple-element.83), channel_id=1, source_target_pairs={{0,16},{8,24},{16,0},{24,8},{1,17},{9,25},{17,1},{25,9},{2,18},{10... | collective-permute-start | bytes 933896 | tf_op jit(solution)/shard_map/ppermute | solution.py:126
  30.1 8.8 %collective-permute-start.13 = (bf16[576,256]{1,0:T(8,128)(2,1)S(1)}, bf16[576,256]{1,0:T(8,128)(2,1)S(1)}, u32[]{:S(2)}, u32[]{:S(2)}) collective-permute-start(bf16[576,256]{1,0:T(8,128)(2,1)S(1)} %get-tuple-element.81), channel_id=1, source_target_pairs={{0,8},{8,0},{16,24},{24,16},{1,9},{9,1},{17,25},{25,17},{2,10},{10... | collective-permute-start | bytes 884744 | tf_op jit(solution)/shard_map/ppermute | solution.py:126
  39.0 6.2 %collective-permute-start.16 = (bf16[304,256]{1,0:T(8,128)(2,1)S(1)}, bf16[304,256]{1,0:T(8,128)(2,1)S(1)}, u32[]{:S(2)}, u32[]{:S(2)}) collective-permute-start(bf16[304,256]{1,0:T(8,128)(2,1)S(1)} %get-tuple-element.86), channel_id=1, source_target_pairs={{0,8},{8,0},{16,24},{24,16},{1,9},{9,1},{17,25},{25,17},{2,10},{10... | collective-permute-start | bytes 466952 | tf_op jit(solution)/shard_map/ppermute | solution.py:126
  40.0 5.1 %collective-permute-start.15 = (bf16[288,256]{1,0:T(8,128)(2,1)S(1)}, bf16[288,256]{1,0:T(8,128)(2,1)S(1)}, u32[]{:S(2)}, u32[]{:S(2)}) collective-permute-start(bf16[288,256]{1,0:T(8,128)(2,1)S(1)} %get-tuple-element.85), channel_id=1, source_target_pairs={{0,16},{8,24},{16,0},{24,8},{1,17},{9,25},{17,1},{25,9},{2,18},{10... | collective-permute-start | bytes 442376 | tf_op jit(solution)/shard_map/ppermute | solution.py:126
  40.8 8.9 %collective-permute-start.11 = (bf16[128,1024]{1,0:T(8,128)(2,1)S(1)}, bf16[128,1024]{1,0:T(8,128)(2,1)S(1)}, u32[]{:S(2)}, u32[]{:S(2)}) collective-permute-start(bf16[128,1024]{1,0:T(8,128)(2,1)S(1)} %get-tuple-element.67), channel_id=1, source_target_pairs={{0,1},{1,0},{2,3},{3,2},{4,5},{5,4},{6,7},{7,6},{8,9},{9,8},{10,11... | collective-permute-start | bytes 786440 | tf_op jit(solution)/shard_map/ppermute | solution.py:120
  45.3 6.0 %collective-permute-start.17 = (bf16[304,256]{1,0:T(8,128)(2,1)S(1)}, bf16[304,256]{1,0:T(8,128)(2,1)S(1)}, u32[]{:S(2)}, u32[]{:S(2)}) collective-permute-start(bf16[304,256]{1,0:T(8,128)(2,1)S(1)} %get-tuple-element.88), channel_id=1, source_target_pairs={{0,2},{2,0},{4,6},{6,4},{1,3},{3,1},{5,7},{7,5},{8,10},{10,8},{12,... | collective-permute-start | bytes 466952 | tf_op jit(solution)/shard_map/ppermute | solution.py:123
  45.8 13.1 %collective-permute-start.18 = (bf16[304,256]{1,0:T(8,128)(2,1)S(1)}, bf16[304,256]{1,0:T(8,128)(2,1)S(1)}, u32[]{:S(2)}, u32[]{:S(2)}) collective-permute-start(bf16[304,256]{1,0:T(8,128)(2,1)S(1)} %get-tuple-element.89), channel_id=1, source_target_pairs={{0,4},{2,6},{4,0},{6,2},{1,5},{3,7},{5,1},{7,3},{8,12},{10,14},{12... | collective-permute-start | bytes 466952 | tf_op jit(solution)/shard_map/ppermute | solution.py:123
  49.0 10.0 %collective-permute-start.19 = (bf16[304,256]{1,0:T(8,128)(2,1)S(1)}, bf16[304,256]{1,0:T(8,128)(2,1)S(1)}, u32[]{:S(2)}, u32[]{:S(2)}) collective-permute-start(bf16[304,256]{1,0:T(8,128)(2,1)S(1)} %get-tuple-element.90), channel_id=1, source_target_pairs={{0,6},{2,4},{4,2},{6,0},{1,7},{3,5},{5,3},{7,1},{8,14},{10,12},{12... | collective-permute-start | bytes 466952 | tf_op jit(solution)/shard_map/ppermute | solution.py:123
  59.0 5.3 %collective-permute-start.20 = (bf16[304,256]{1,0:T(8,128)(2,1)S(1)}, bf16[304,256]{1,0:T(8,128)(2,1)S(1)}, u32[]{:S(2)}, u32[]{:S(2)}) collective-permute-start(bf16[304,256]{1,0:T(8,128)(2,1)S(1)} %z_sum.1.refs_0_), channel_id=1, source_target_pairs={{0,8},{8,0},{16,24},{24,16},{1,9},{9,1},{17,25},{25,17},{2,10},{10... | collective-permute-start | bytes 466952 | tf_op jit(solution)/shard_map/ppermute | solution.py:126
  60.7 5.2 %collective-permute-start.21 = (bf16[304,256]{1,0:T(8,128)(2,1)S(1)}, bf16[304,256]{1,0:T(8,128)(2,1)S(1)}, u32[]{:S(2)}, u32[]{:S(2)}) collective-permute-start(bf16[304,256]{1,0:T(8,128)(2,1)S(1)} %z_sum.1.refs_0_), channel_id=1, source_target_pairs={{0,16},{8,24},{16,0},{24,8},{1,17},{9,25},{17,1},{25,9},{2,18},{10... | collective-permute-start | bytes 466952 | tf_op jit(solution)/shard_map/ppermute | solution.py:126
  61.7 6.1 %collective-permute-start.22 = (bf16[304,256]{1,0:T(8,128)(2,1)S(1)}, bf16[304,256]{1,0:T(8,128)(2,1)S(1)}, u32[]{:S(2)}, u32[]{:S(2)}) collective-permute-start(bf16[304,256]{1,0:T(8,128)(2,1)S(1)} %z_sum.1.refs_0_), channel_id=1, source_target_pairs={{0,24},{8,16},{16,8},{24,0},{1,25},{9,17},{17,9},{25,1},{2,26},{10... | collective-permute-start | bytes 466952 | tf_op jit(solution)/shard_map/ppermute | solution.py:126
  67.9 2.2 %collective-permute-start.23 = (bf16[768,256]{1,0:T(8,128)(2,1)S(1)}, bf16[768,256]{1,0:T(8,128)(2,1)S(1)}, u32[]{:S(2)}, u32[]{:S(2)}) collective-permute-start(bf16[768,256]{1,0:T(8,128)(2,1)S(1)} %dense_gather.1.refs_0_), channel_id=1, source_target_pairs={{0,1},{1,0},{2,3},{3,2},{4,5},{5,4},{6,7},{7,6},{8,9},{9,8},{10,11... | collective-permute-start | bytes 1179656 | tf_op jit(solution)/shard_map/ppermute | solution.py:120
  (17 other events, 90.1 us)

commit v4 on v3

--- a/solution.py
+++ b/solution.py
@@ -473,12 +473,33 @@
                 at += value.shape[0]
 
         dense = rows_sum(0, rep_part)
-        for k, out in enumerate(outs):
+        for i, out in enumerate(outs):
             put(out, 0, dense)
-            put(out, rep_part, rows_sum(rep_part + k * tab_part, tab_part))
-
-    z_outs = call(rep_body, [shape(z_rows, width)] * n_z, rep_ins, "rep_sum")
-    z_ins = spread(to_z, z_outs, True)
+            for n, k in enumerate(trips[i]):
+                put(out, rep_part + n * tab_part, rows_sum(rep_part + k * tab_part, tab_part))
+
+    trips = [(0, 2), (1, 3)] if n_z == 4 else [(k,) for k in range(n_z)]
+    z_outs = call(
+        rep_body,
+        [shape(rep_part + len(trip) * tab_part, width) for trip in trips],
+        rep_ins,
+        "rep_sum",
+    )
+    if n_z == 4:
+        z_in = to_z(z_outs[1], 1)
+
+        def z_half_body(spot, own_ref, in_ref, keep, out):
+            dense = total((own_ref, in_ref), 0, rep_part)
+            for n, ref in enumerate((keep, out)):
+                ref[:rep_part, :] = dense
+                ref[rep_part:, :] = total((own_ref, in_ref), rep_part + n * tab_part, tab_part)
+
+        keep, out = call(
+            z_half_body, [shape(z_rows, width)] * 2, (z_outs[0], z_in), "z_half_sum"
+        )
+        z_ins = [keep, to_z(out, 2)]
+    else:
+        z_ins = spread(to_z, z_outs, True)
 
     def cross_body(spot, own_ref, in_ref, out, done):
         _, _, c = spot
@@ -496,7 +517,7 @@
     )
 
     def z_body(spot, _, *refs):
-        refs[n_z][...] = total(refs[:n_z], 0, z_rows)
+        refs[-1][...] = total(refs[:-1], 0, z_rows)
 
     (mine,) = call(z_body, [shape(z_rows, width)], (cross_done, *z_ins), "z_sum")
 

time: 71.4 us -> 70.6 us (0.989)
  starting transfers between devices: 27.7 us -> 25.9 us
  waiting for transfers between devices: 31.2 us -> 32.2 us
    ppermute x9 -> x8, starting transfers between devices: 14.6 us -> 12.9 us  [to_z(): return lax.ppermute(value, 'z', [(i, i ^ k) for i in range(n_z)])]
    ppermute x9 -> x8, waiting for transfers between devices: 9.68 us -> 11.4 us  [to_z(): return lax.ppermute(value, 'z', [(i, i ^ k) for i in range(n_z)])]
    ppermute x10, waiting for transfers between devices: 19.1 us -> 18.3 us  [to_rep(): return lax.ppermute(value, 'rep', [(i, i ^ k) for i in range(n_rep)])]
    pallas_call x16 -> x17, Pallas kernels: 7.36 us -> 7.37 us  [run(): pl.pallas_call(placed, out_shape=out_shapes, in_specs=[in_vmem] * len(arg...]
  transfers between devices with their start and end apart: 24 -> 23, of which waited for: 12 -> 12; matrix products, arithmetic and copies ran while one was open for 2% -> 2% of each run, Pallas kernels for 5% -> 5%
where the time goes in v4:
time: 70.6 us; the launch traced here: 70.4 us
  waiting for transfers between devices  32.2 us (46%)
  starting transfers between devices  25.9 us (37%)
  Pallas kernels  7.37 us (10%)
  local copies, waits for them, and re-layouts  3.66 us (5%)
  between operations  0.9 us (1%)
    ppermute x10, waiting for transfers between devices, to_rep(): return lax.ppermute(value, 'rep', [(i, i ^ k) for i in range(n_rep)])  18.3 us
    ppermute x8, starting transfers between devices, to_z(): return lax.ppermute(value, 'z', [(i, i ^ k) for i in range(n_z)])  12.9 us
    ppermute x10, starting transfers between devices, to_rep(): return lax.ppermute(value, 'rep', [(i, i ^ k) for i in range(n_rep)])  12.7 us
    ppermute x8, waiting for transfers between devices, to_z(): return lax.ppermute(value, 'z', [(i, i ^ k) for i in range(n_z)])  11.4 us
    pallas_call x17, Pallas kernels, run(): pl.pallas_call(placed, out_shape=out_shapes, in_specs=[in_vmem] * len(arg...  7.37 us
    ppermute x5, waiting for transfers between devices, swap(): return lax.ppermute(value, 'core', [(0, 1), (1, 0)])  2.46 us
    unnamed x34, local copies, waits for them, and re-layouts  2.2 us
  transfers between devices with their start and end apart: 23, of which 12 were waited for; matrix products, arithmetic and copies ran while one was open for 2% of the time, Pallas kernels for 5%

profile of v4, /device:TPU:0, one launch (start us, length us, event | category | flops | bytes accessed | tf_op | source)
XLA Modules:
  0.0 70.4 jit_solution(14622137124305547421)
XLA Ops:
  1.8 3.1 %collective-permute-start.3 = (bf16[64,256]{1,0:T(8,128)(2,1)S(1)}, bf16[64,256]{1,0:T(8,128)(2,1)S(1)}, u32[]{:S(2)}, u32[]{:S(2)}) collective-permute-start(bf16[64,256]{1,0:T(8,128)(2,1)S(1)} %u_cut.1), channel_id=1, source_target_pairs={{0,2},{2,0},{4,6},{6,4},{1,3},{3,1},{5,7},{7,5},{8,10},{10,8},{12,... | collective-permute-start | bytes 98312 | tf_op jit(solution)/shard_map/ppermute | solution.py:123
  4.9 2.6 %collective-permute-start.4 = (bf16[64,256]{1,0:T(8,128)(2,1)S(1)}, bf16[64,256]{1,0:T(8,128)(2,1)S(1)}, u32[]{:S(2)}, u32[]{:S(2)}) collective-permute-start(bf16[64,256]{1,0:T(8,128)(2,1)S(1)} %u_cut.1), channel_id=1, source_target_pairs={{0,4},{2,6},{4,0},{6,2},{1,5},{3,7},{5,1},{7,3},{8,12},{10,14},{12... | collective-permute-start | bytes 98312 | tf_op jit(solution)/shard_map/ppermute | solution.py:123
  8.6 3.5 %collective-permute-start.1 = (bf16[208,256]{1,0:T(8,128)(2,1)S(1)}, bf16[208,256]{1,0:T(8,128)(2,1)S(1)}, u32[]{:S(2)}, u32[]{:S(2)}) collective-permute-start(bf16[208,256]{1,0:T(8,128)(2,1)S(1)} %get-tuple-element.58), channel_id=1, source_target_pairs={{0,4},{2,6},{4,0},{6,2},{1,5},{3,7},{5,1},{7,3},{8,12},{10,14},{12... | collective-permute-start | bytes 319496 | tf_op jit(solution)/shard_map/ppermute | solution.py:123
  14.1 1.7 %collective-permute-start.6 = (bf16[192,256]{1,0:T(8,128)(2,1)S(1)}, bf16[192,256]{1,0:T(8,128)(2,1)S(1)}, u32[]{:S(2)}, u32[]{:S(2)}) collective-permute-start(bf16[192,256]{1,0:T(8,128)(2,1)S(1)} %u_rows.1.refs_5_), channel_id=1, source_target_pairs={{0,8},{8,0},{16,24},{24,16},{1,9},{9,1},{17,25},{25,17},{2,10},{10... | collective-permute-start | bytes 294920 | tf_op jit(solution)/shard_map/ppermute | solution.py:126
  15.8 1.5 %collective-permute-start.7 = (bf16[192,256]{1,0:T(8,128)(2,1)S(1)}, bf16[192,256]{1,0:T(8,128)(2,1)S(1)}, u32[]{:S(2)}, u32[]{:S(2)}) collective-permute-start(bf16[192,256]{1,0:T(8,128)(2,1)S(1)} %u_rows.1.refs_5_), channel_id=1, source_target_pairs={{0,16},{8,24},{16,0},{24,8},{1,17},{9,25},{17,1},{25,9},{2,18},{10... | collective-permute-start | bytes 294920 | tf_op jit(solution)/shard_map/ppermute | solution.py:126
  17.3 1.7 %collective-permute-start.8 = (bf16[192,256]{1,0:T(8,128)(2,1)S(1)}, bf16[192,256]{1,0:T(8,128)(2,1)S(1)}, u32[]{:S(2)}, u32[]{:S(2)}) collective-permute-start(bf16[192,256]{1,0:T(8,128)(2,1)S(1)} %u_rows.1.refs_5_), channel_id=1, source_target_pairs={{0,24},{8,16},{16,8},{24,0},{1,25},{9,17},{17,9},{25,1},{2,26},{10... | collective-permute-start | bytes 294920 | tf_op jit(solution)/shard_map/ppermute | solution.py:126
  19.9 1.3 %collective-permute-done.2.refs_3_ = bf16[208,256]{1,0:T(8,128)(2,1)S(1)} collective-permute-done((bf16[208,256]{1,0:T(8,128)(2,1)S(1)}, bf16[208,256]{1,0:T(8,128)(2,1)S(1)}, u32[]{:S(2)}, u32[]{:S(2)}) %collective-permute-start.2) | collective-permute-done | bytes 106528 | tf_op jit(solution)/shard_map/ppermute | solution.py:123
  21.7 1.1 %collective-permute-done.8.refs_8_ = bf16[192,256]{1,0:T(8,128)(2,1)S(1)} collective-permute-done((bf16[192,256]{1,0:T(8,128)(2,1)S(1)}, bf16[192,256]{1,0:T(8,128)(2,1)S(1)}, u32[]{:S(2)}, u32[]{:S(2)}) %collective-permute-start.8) | collective-permute-done | bytes 98336 | tf_op jit(solution)/shard_map/ppermute | solution.py:126
  23.8 1.5 %collective-permute-done.10.refs_6_.refs_1_ = bf16[512,256]{1,0:T(8,128)(2,1)S(1)} collective-permute-done((bf16[512,256]{1,0:T(8,128)(2,1)S(1)}, bf16[512,256]{1,0:T(8,128)(2,1)S(1)}, u32[]{:S(2)}, u32[]{:S(2)}) %collective-permute-start.10) | collective-permute-done | bytes 262176 | tf_op jit(solution)/shard_map/ppermute | solution.py:120
  25.3 1.5 %dense_grads.1 = (bf16[128,256]{1,0:T(8,128)(2,1)}, bf16[832,256]{1,0:T(8,128)(2,1)S(1)}, bf16[832,256]{1,0:T(8,128)(2,1)S(1)}) custom-call(s32[8,128]{1,0:T(8,128)S(1)} %broadcast_in_dim.32.spot_ref, bf16[512,256]{1,0:T(8,128)(2,1)S(1)} %get-tuple-element.63.refs_5_.refs_0_, bf16[512,256]{1,0:T(8,128)(2,1)S(1)} %collective-permute-done.10.refs_6_.refs_1_, ...), custom_call_target="tpu_custom_call" | custom-call | flops 100000000 | bytes 3301376 | tf_op jit(solution)/shard_map/dense_grads/pallas_call | solution.py:58
  28.7 1.4 %collective-permute-start.14 = (bf16[608,256]{1,0:T(8,128)(2,1)S(1)}, bf16[608,256]{1,0:T(8,128)(2,1)S(1)}, u32[]{:S(2)}, u32[]{:S(2)}) collective-permute-start(bf16[608,256]{1,0:T(8,128)(2,1)S(1)} %get-tuple-element.83), channel_id=1, source_target_pairs={{0,16},{8,24},{16,0},{24,8},{1,17},{9,25},{17,1},{25,9},{2,18},{10... | collective-permute-start | bytes 933896 | tf_op jit(solution)/shard_map/ppermute | solution.py:126
  31.1 7.8 %collective-permute-done.13.refs_1_ = bf16[576,256]{1,0:T(8,128)(2,1)S(1)} collective-permute-done((bf16[576,256]{1,0:T(8,128)(2,1)S(1)}, bf16[576,256]{1,0:T(8,128)(2,1)S(1)}, u32[]{:S(2)}, u32[]{:S(2)}) %collective-permute-start.13) | collective-permute-done | bytes 294944 | tf_op jit(solution)/shard_map/ppermute | solution.py:126
  39.0 1.0 %collective-permute-start.16 = (bf16[304,256]{1,0:T(8,128)(2,1)S(1)}, bf16[304,256]{1,0:T(8,128)(2,1)S(1)}, u32[]{:S(2)}, u32[]{:S(2)}) collective-permute-start(bf16[304,256]{1,0:T(8,128)(2,1)S(1)} %get-tuple-element.86), channel_id=1, source_target_pairs={{0,8},{8,0},{16,24},{24,16},{1,9},{9,1},{17,25},{25,17},{2,10},{10... | collective-permute-start | bytes 466952 | tf_op jit(solution)/shard_map/ppermute | solution.py:126
  40.8 4.4 %collective-permute-done.15.refs_1_ = bf16[288,256]{1,0:T(8,128)(2,1)S(1)} collective-permute-done((bf16[288,256]{1,0:T(8,128)(2,1)S(1)}, bf16[288,256]{1,0:T(8,128)(2,1)S(1)}, u32[]{:S(2)}, u32[]{:S(2)}) %collective-permute-start.15) | collective-permute-done | bytes 147488 | tf_op jit(solution)/shard_map/ppermute | solution.py:126
  45.9 5.2 %collective-permute-done.17.refs_1_ = bf16[400,256]{1,0:T(8,128)(2,1)S(1)} collective-permute-done((bf16[400,256]{1,0:T(8,128)(2,1)S(1)}, bf16[400,256]{1,0:T(8,128)(2,1)S(1)}, u32[]{:S(2)}, u32[]{:S(2)}) %collective-permute-start.17) | collective-permute-done | bytes 204832 | tf_op jit(solution)/shard_map/ppermute | solution.py:123
  51.2 2.1 %collective-permute-start.18 = (bf16[304,256]{1,0:T(8,128)(2,1)S(1)}, bf16[304,256]{1,0:T(8,128)(2,1)S(1)}, u32[]{:S(2)}, u32[]{:S(2)}) collective-permute-start(bf16[304,256]{1,0:T(8,128)(2,1)S(1)} %get-tuple-element.90), channel_id=1, source_target_pairs={{0,4},{2,6},{4,0},{6,2},{1,5},{3,7},{5,1},{7,3},{8,12},{10,14},{12... | collective-permute-start | bytes 466952 | tf_op jit(solution)/shard_map/ppermute | solution.py:123
  54.1 4.9 %collective-permute-done.18.refs_2_ = bf16[304,256]{1,0:T(8,128)(2,1)S(1)} collective-permute-done((bf16[304,256]{1,0:T(8,128)(2,1)S(1)}, bf16[304,256]{1,0:T(8,128)(2,1)S(1)}, u32[]{:S(2)}, u32[]{:S(2)}) %collective-permute-start.18) | collective-permute-done | bytes 155680 | tf_op jit(solution)/shard_map/ppermute | solution.py:123
  59.1 1.1 %collective-permute-start.19 = (bf16[304,256]{1,0:T(8,128)(2,1)S(1)}, bf16[304,256]{1,0:T(8,128)(2,1)S(1)}, u32[]{:S(2)}, u32[]{:S(2)}) collective-permute-start(bf16[304,256]{1,0:T(8,128)(2,1)S(1)} %z_sum.1.refs_0_), channel_id=1, source_target_pairs={{0,8},{8,0},{16,24},{24,16},{1,9},{9,1},{17,25},{25,17},{2,10},{10... | collective-permute-start | bytes 466952 | tf_op jit(solution)/shard_map/ppermute | solution.py:126
  60.9 1.7 %collective-permute-start.21 = (bf16[304,256]{1,0:T(8,128)(2,1)S(1)}, bf16[304,256]{1,0:T(8,128)(2,1)S(1)}, u32[]{:S(2)}, u32[]{:S(2)}) collective-permute-start(bf16[304,256]{1,0:T(8,128)(2,1)S(1)} %z_sum.1.refs_0_), channel_id=1, source_target_pairs={{0,24},{8,16},{16,8},{24,0},{1,25},{9,17},{17,9},{25,1},{2,26},{10... | collective-permute-start | bytes 466952 | tf_op jit(solution)/shard_map/ppermute | solution.py:126
  62.6 1.7 %collective-permute-done.19.refs_1_ = bf16[304,256]{1,0:T(8,128)(2,1)S(1)} collective-permute-done((bf16[304,256]{1,0:T(8,128)(2,1)S(1)}, bf16[304,256]{1,0:T(8,128)(2,1)S(1)}, u32[]{:S(2)}, u32[]{:S(2)}) %collective-permute-start.19) | collective-permute-done | bytes 155680 | tf_op jit(solution)/shard_map/ppermute | solution.py:126
  64.4 1.1 %collective-permute-done.20.refs_2_ = bf16[304,256]{1,0:T(8,128)(2,1)S(1)} collective-permute-done((bf16[304,256]{1,0:T(8,128)(2,1)S(1)}, bf16[304,256]{1,0:T(8,128)(2,1)S(1)}, u32[]{:S(2)}, u32[]{:S(2)}) %collective-permute-start.20) | collective-permute-done | bytes 155680 | tf_op jit(solution)/shard_map/ppermute | solution.py:126
  65.4 1.7 %collective-permute-done.21.refs_3_ = bf16[304,256]{1,0:T(8,128)(2,1)S(1)} collective-permute-done((bf16[304,256]{1,0:T(8,128)(2,1)S(1)}, bf16[304,256]{1,0:T(8,128)(2,1)S(1)}, u32[]{:S(2)}, u32[]{:S(2)}) %collective-permute-start.21) | collective-permute-done | bytes 155680 | tf_op jit(solution)/shard_map/ppermute | solution.py:126
  67.3 1.0 %table_last.1 = (bf16[64,256]{1,0:T(8,128)(2,1)}, bf16[256,256]{1,0:T(8,128)(2,1)}, bf16[256,256]{1,0:T(8,128)(2,1)}, f32[16,1024]{1,0:T(8,128)S(1)}, f32[8,256]{1,0:T(8,128)S(1)}) custom-call(s32[8,128]{1,0:T(8,128)S(1)} %broadcast_in_dim.32.spot_ref, bf16[304,256]{1,0:T(8,128)(2,1)S(1)} %z_sum.1.refs_0_, ...), custom_call_target="tpu_custom_call" | custom-call | flops 100000000 | bytes 1159168 | tf_op jit(solution)/shard_map/table_last/pallas_call | solution.py:58
  69.4 1.0 %dense_last.1 = (bf16[1024,256]{1,0:T(8,128)(2,1)}, bf16[256,256]{1,0:T(8,128)(2,1)}, bf16[256,256]{1,0:T(8,128)(2,1)}) custom-call(s32[8,128]{1,0:T(8,128)S(1)} %broadcast_in_dim.32.spot_ref, bf16[768,256]{1,0:T(8,128)(2,1)S(1)} %dense_gather.1.refs_0_, bf16[768,256]{1,0:T(8,128)(2,1)S(1)} %collective-permute-done.22.refs_1_), custom_call_target="tpu_custom_call" | custom-call | flops 100000000 | bytes 1576960 | tf_op jit(solution)/shard_map/dense_last/pallas_call | solution.py:58
  (92 shorter events, 13.8 us)
Async XLA Ops:
  1.8 11.8 %copy-start = (bf16[128,2048]{1,0:T(8,128)(2,1)S(1)}, bf16[128,2048]{1,0:T(8,128)(2,1)}, u32[]{:S(2)}) copy-start(bf16[128,2048]{1,0:T(8,128)(2,1)} %refs_9_.4) | copy-start | bytes 1572868
  1.8 11.9 %collective-permute-start.3 = (bf16[64,256]{1,0:T(8,128)(2,1)S(1)}, bf16[64,256]{1,0:T(8,128)(2,1)S(1)}, u32[]{:S(2)}, u32[]{:S(2)}) collective-permute-start(bf16[64,256]{1,0:T(8,128)(2,1)S(1)} %u_cut.1), channel_id=1, source_target_pairs={{0,2},{2,0},{4,6},{6,4},{1,3},{3,1},{5,7},{7,5},{8,10},{10,8},{12,... | collective-permute-start | bytes 98312 | tf_op jit(solution)/shard_map/ppermute | solution.py:123
  4.9 9.1 %collective-permute-start.4 = (bf16[64,256]{1,0:T(8,128)(2,1)S(1)}, bf16[64,256]{1,0:T(8,128)(2,1)S(1)}, u32[]{:S(2)}, u32[]{:S(2)}) collective-permute-start(bf16[64,256]{1,0:T(8,128)(2,1)S(1)} %u_cut.1), channel_id=1, source_target_pairs={{0,4},{2,6},{4,0},{6,2},{1,5},{3,7},{5,1},{7,3},{8,12},{10,14},{12... | collective-permute-start | bytes 98312 | tf_op jit(solution)/shard_map/ppermute | solution.py:123
  7.5 6.6 %collective-permute-start.5 = (bf16[64,256]{1,0:T(8,128)(2,1)S(1)}, bf16[64,256]{1,0:T(8,128)(2,1)S(1)}, u32[]{:S(2)}, u32[]{:S(2)}) collective-permute-start(bf16[64,256]{1,0:T(8,128)(2,1)S(1)} %u_cut.1), channel_id=1, source_target_pairs={{0,6},{2,4},{4,2},{6,0},{1,7},{3,5},{5,3},{7,1},{8,14},{10,12},{12... | collective-permute-start | bytes 98312 | tf_op jit(solution)/shard_map/ppermute | solution.py:123
  7.7 8.1 %collective-permute-start = (bf16[208,256]{1,0:T(8,128)(2,1)S(1)}, bf16[208,256]{1,0:T(8,128)(2,1)S(1)}, u32[]{:S(2)}, u32[]{:S(2)}) collective-permute-start(bf16[208,256]{1,0:T(8,128)(2,1)S(1)} %get-tuple-element.57), channel_id=1, source_target_pairs={{0,2},{2,0},{4,6},{6,4},{1,3},{3,1},{5,7},{7,5},{8,10},{10,8},{12,... | collective-permute-start | bytes 319496 | tf_op jit(solution)/shard_map/ppermute | solution.py:123
  8.6 8.7 %collective-permute-start.1 = (bf16[208,256]{1,0:T(8,128)(2,1)S(1)}, bf16[208,256]{1,0:T(8,128)(2,1)S(1)}, u32[]{:S(2)}, u32[]{:S(2)}) collective-permute-start(bf16[208,256]{1,0:T(8,128)(2,1)S(1)} %get-tuple-element.58), channel_id=1, source_target_pairs={{0,4},{2,6},{4,0},{6,2},{1,5},{3,7},{5,1},{7,3},{8,12},{10,14},{12... | collective-permute-start | bytes 319496 | tf_op jit(solution)/shard_map/ppermute | solution.py:123
  13.7 9.1 %collective-permute-start.9 = (bf16[128,1024]{1,0:T(8,128)(2,1)S(1)}, bf16[128,1024]{1,0:T(8,128)(2,1)S(1)}, u32[]{:S(2)}, u32[]{:S(2)}) collective-permute-start(bf16[128,1024]{1,0:T(8,128)(2,1)S(1)} %cot_send.1), channel_id=1, source_target_pairs={{0,1},{1,0},{2,3},{3,2},{4,5},{5,4},{6,7},{7,6},{8,9},{9,8},{10,11... | collective-permute-start | bytes 786440 | tf_op jit(solution)/shard_map/ppermute | solution.py:120
  14.0 7.2 %collective-permute-start.2 = (bf16[208,256]{1,0:T(8,128)(2,1)S(1)}, bf16[208,256]{1,0:T(8,128)(2,1)S(1)}, u32[]{:S(2)}, u32[]{:S(2)}) collective-permute-start(bf16[208,256]{1,0:T(8,128)(2,1)S(1)} %get-tuple-element.59), channel_id=1, source_target_pairs={{0,6},{2,4},{4,2},{6,0},{1,7},{3,5},{5,3},{7,1},{8,14},{10,12},{12... | collective-permute-start | bytes 319496 | tf_op jit(solution)/shard_map/ppermute | solution.py:123
  14.1 7.1 %collective-permute-start.6 = (bf16[192,256]{1,0:T(8,128)(2,1)S(1)}, bf16[192,256]{1,0:T(8,128)(2,1)S(1)}, u32[]{:S(2)}, u32[]{:S(2)}) collective-permute-start(bf16[192,256]{1,0:T(8,128)(2,1)S(1)} %u_rows.1.refs_5_), channel_id=1, source_target_pairs={{0,8},{8,0},{16,24},{24,16},{1,9},{9,1},{17,25},{25,17},{2,10},{10... | collective-permute-start | bytes 294920 | tf_op jit(solution)/shard_map/ppermute | solution.py:126
  15.8 5.9 %collective-permute-start.7 = (bf16[192,256]{1,0:T(8,128)(2,1)S(1)}, bf16[192,256]{1,0:T(8,128)(2,1)S(1)}, u32[]{:S(2)}, u32[]{:S(2)}) collective-permute-start(bf16[192,256]{1,0:T(8,128)(2,1)S(1)} %u_rows.1.refs_5_), channel_id=1, source_target_pairs={{0,16},{8,24},{16,0},{24,8},{1,17},{9,25},{17,1},{25,9},{2,18},{10... | collective-permute-start | bytes 294920 | tf_op jit(solution)/shard_map/ppermute | solution.py:126
  17.3 5.5 %collective-permute-start.8 = (bf16[192,256]{1,0:T(8,128)(2,1)S(1)}, bf16[192,256]{1,0:T(8,128)(2,1)S(1)}, u32[]{:S(2)}, u32[]{:S(2)}) collective-permute-start(bf16[192,256]{1,0:T(8,128)(2,1)S(1)} %u_rows.1.refs_5_), channel_id=1, source_target_pairs={{0,24},{8,16},{16,8},{24,0},{1,25},{9,17},{17,9},{25,1},{2,26},{10... | collective-permute-start | bytes 294920 | tf_op jit(solution)/shard_map/ppermute | solution.py:126
  23.7 1.6 %collective-permute-start.10 = (bf16[512,256]{1,0:T(8,128)(2,1)S(1)}, bf16[512,256]{1,0:T(8,128)(2,1)S(1)}, u32[]{:S(2)}, u32[]{:S(2)}) collective-permute-start(bf16[512,256]{1,0:T(8,128)(2,1)S(1)} %get-tuple-element.63.refs_5_.refs_0_), channel_id=1, source_target_pairs={{0,1},{1,0},{2,3},{3,2},{4,5},{5,4},{6,7},{7,6},{8,9},{9,8},{10,11... | collective-permute-start | bytes 786440 | tf_op jit(solution)/shard_map/ppermute | solution.py:120
  26.7 1.8 %collective-permute-start.12 = (bf16[832,256]{1,0:T(8,128)(2,1)S(1)}, bf16[832,256]{1,0:T(8,128)(2,1)S(1)}, u32[]{:S(2)}, u32[]{:S(2)}) collective-permute-start(bf16[832,256]{1,0:T(8,128)(2,1)S(1)} %get-tuple-element.77), channel_id=1, source_target_pairs={{0,1},{1,0},{2,3},{3,2},{4,5},{5,4},{6,7},{7,6},{8,9},{9,8},{10,11... | collective-permute-start | bytes 1277960 | tf_op jit(solution)/shard_map/ppermute | solution.py:120
  28.7 10.2 %collective-permute-start.14 = (bf16[608,256]{1,0:T(8,128)(2,1)S(1)}, bf16[608,256]{1,0:T(8,128)(2,1)S(1)}, u32[]{:S(2)}, u32[]{:S(2)}) collective-permute-start(bf16[608,256]{1,0:T(8,128)(2,1)S(1)} %get-tuple-element.83), channel_id=1, source_target_pairs={{0,16},{8,24},{16,0},{24,8},{1,17},{9,25},{17,1},{25,9},{2,18},{10... | collective-permute-start | bytes 933896 | tf_op jit(solution)/shard_map/ppermute | solution.py:126
  30.1 8.8 %collective-permute-start.13 = (bf16[576,256]{1,0:T(8,128)(2,1)S(1)}, bf16[576,256]{1,0:T(8,128)(2,1)S(1)}, u32[]{:S(2)}, u32[]{:S(2)}) collective-permute-start(bf16[576,256]{1,0:T(8,128)(2,1)S(1)} %get-tuple-element.81), channel_id=1, source_target_pairs={{0,8},{8,0},{16,24},{24,16},{1,9},{9,1},{17,25},{25,17},{2,10},{10... | collective-permute-start | bytes 884744 | tf_op jit(solution)/shard_map/ppermute | solution.py:126
  39.0 6.2 %collective-permute-start.16 = (bf16[304,256]{1,0:T(8,128)(2,1)S(1)}, bf16[304,256]{1,0:T(8,128)(2,1)S(1)}, u32[]{:S(2)}, u32[]{:S(2)}) collective-permute-start(bf16[304,256]{1,0:T(8,128)(2,1)S(1)} %get-tuple-element.86), channel_id=1, source_target_pairs={{0,8},{8,0},{16,24},{24,16},{1,9},{9,1},{17,25},{25,17},{2,10},{10... | collective-permute-start | bytes 466952 | tf_op jit(solution)/shard_map/ppermute | solution.py:126
  40.0 5.1 %collective-permute-start.15 = (bf16[288,256]{1,0:T(8,128)(2,1)S(1)}, bf16[288,256]{1,0:T(8,128)(2,1)S(1)}, u32[]{:S(2)}, u32[]{:S(2)}) collective-permute-start(bf16[288,256]{1,0:T(8,128)(2,1)S(1)} %get-tuple-element.85), channel_id=1, source_target_pairs={{0,16},{8,24},{16,0},{24,8},{1,17},{9,25},{17,1},{25,9},{2,18},{10... | collective-permute-start | bytes 442376 | tf_op jit(solution)/shard_map/ppermute | solution.py:126
  45.3 5.8 %collective-permute-start.17 = (bf16[400,256]{1,0:T(8,128)(2,1)S(1)}, bf16[400,256]{1,0:T(8,128)(2,1)S(1)}, u32[]{:S(2)}, u32[]{:S(2)}) collective-permute-start(bf16[400,256]{1,0:T(8,128)(2,1)S(1)} %get-tuple-element.88), channel_id=1, source_target_pairs={{0,2},{2,0},{4,6},{6,4},{1,3},{3,1},{5,7},{7,5},{8,10},{10,8},{12,... | collective-permute-start | bytes 614408 | tf_op jit(solution)/shard_map/ppermute | solution.py:123
  45.9 7.4 %collective-permute-start.11 = (bf16[128,1024]{1,0:T(8,128)(2,1)S(1)}, bf16[128,1024]{1,0:T(8,128)(2,1)S(1)}, u32[]{:S(2)}, u32[]{:S(2)}) collective-permute-start(bf16[128,1024]{1,0:T(8,128)(2,1)S(1)} %get-tuple-element.67), channel_id=1, source_target_pairs={{0,1},{1,0},{2,3},{3,2},{4,5},{5,4},{6,7},{7,6},{8,9},{9,8},{10,11... | collective-permute-start | bytes 786440 | tf_op jit(solution)/shard_map/ppermute | solution.py:120
  51.2 7.9 %collective-permute-start.18 = (bf16[304,256]{1,0:T(8,128)(2,1)S(1)}, bf16[304,256]{1,0:T(8,128)(2,1)S(1)}, u32[]{:S(2)}, u32[]{:S(2)}) collective-permute-start(bf16[304,256]{1,0:T(8,128)(2,1)S(1)} %get-tuple-element.90), channel_id=1, source_target_pairs={{0,4},{2,6},{4,0},{6,2},{1,5},{3,7},{5,1},{7,3},{8,12},{10,14},{12... | collective-permute-start | bytes 466952 | tf_op jit(solution)/shard_map/ppermute | solution.py:123
  59.1 5.3 %collective-permute-start.19 = (bf16[304,256]{1,0:T(8,128)(2,1)S(1)}, bf16[304,256]{1,0:T(8,128)(2,1)S(1)}, u32[]{:S(2)}, u32[]{:S(2)}) collective-permute-start(bf16[304,256]{1,0:T(8,128)(2,1)S(1)} %z_sum.1.refs_0_), channel_id=1, source_target_pairs={{0,8},{8,0},{16,24},{24,16},{1,9},{9,1},{17,25},{25,17},{2,10},{10... | collective-permute-start | bytes 466952 | tf_op jit(solution)/shard_map/ppermute | solution.py:126
  60.2 5.2 %collective-permute-start.20 = (bf16[304,256]{1,0:T(8,128)(2,1)S(1)}, bf16[304,256]{1,0:T(8,128)(2,1)S(1)}, u32[]{:S(2)}, u32[]{:S(2)}) collective-permute-start(bf16[304,256]{1,0:T(8,128)(2,1)S(1)} %z_sum.1.refs_0_), channel_id=1, source_target_pairs={{0,16},{8,24},{16,0},{24,8},{1,17},{9,25},{17,1},{25,9},{2,18},{10... | collective-permute-start | bytes 466952 | tf_op jit(solution)/shard_map/ppermute | solution.py:126
  60.9 6.2 %collective-permute-start.21 = (bf16[304,256]{1,0:T(8,128)(2,1)S(1)}, bf16[304,256]{1,0:T(8,128)(2,1)S(1)}, u32[]{:S(2)}, u32[]{:S(2)}) collective-permute-start(bf16[304,256]{1,0:T(8,128)(2,1)S(1)} %z_sum.1.refs_0_), channel_id=1, source_target_pairs={{0,24},{8,16},{16,8},{24,0},{1,25},{9,17},{17,9},{25,1},{2,26},{10... | collective-permute-start | bytes 466952 | tf_op jit(solution)/shard_map/ppermute | solution.py:126
  67.2 2.2 %collective-permute-start.22 = (bf16[768,256]{1,0:T(8,128)(2,1)S(1)}, bf16[768,256]{1,0:T(8,128)(2,1)S(1)}, u32[]{:S(2)}, u32[]{:S(2)}) collective-permute-start(bf16[768,256]{1,0:T(8,128)(2,1)S(1)} %dense_gather.1.refs_0_), channel_id=1, source_target_pairs={{0,1},{1,0},{2,3},{3,2},{4,5},{5,4},{6,7},{7,6},{8,9},{9,8},{10,11... | collective-permute-start | bytes 1179656 | tf_op jit(solution)/shard_map/ppermute | solution.py:120
  (16 other events, 78.3 us)

commit v5 on v4

--- a/solution.py
+++ b/solution.py
@@ -295,7 +295,8 @@
         d_second_round = d_second.astype(BF)
         d_first = mul_nt(d_second_round, w2_ref[...]) * slope1_ref[...]
         d_bias = cot * bottom_full
-        pack[...] = jnp.zeros_like(pack)
+        if 2 * n_rep * dense_part > dense_rows:
+            pack[...] = jnp.zeros_like(pack)
 
         def put(first, value):
             value = (value * grad_scale).astype(BF)
@@ -523,29 +524,18 @@
 
     pieces = spread(to_rep, [mine] * n_rep)
 
-    def gather_body(spot, *refs):
-        r, _, _ = spot
-        for j in range(n_rep):
-            refs[n_rep][rows_of(r ^ j, dense_part), :] = refs[j][:dense_part, :]
-
-    (dense_own,) = call(gather_body, [shape(n_rep * dense_part, width)], pieces, "dense_gather")
-    dense_other = swap(dense_own)
-
-    def table_last_body(spot, *refs):
+    others = [swap(piece) for piece in pieces]
+
+    def small_last_body(spot, *refs):
         ins = refs[:n_rep]
-        emb_ref, v_ref, g_table, g_v, g_u, g_wide, g_rows, stack, small = refs[n_rep:]
+        g_wide, g_bias, g_rows, small = refs[n_rep:]
         r, z, _ = spot
         for j in range(n_rep):
-            rows = slice(rep_part, rep_part + u_part)
-            g_u[rows_of(r ^ j, u_part), :] = ins[j][rows, :]
-            stack[rows_of(r ^ j, bag_part), :] = ins[j][rep_part + u_part :, :]
             small[rows_of(r ^ j, small_part), :] = ins[j][dense_part:rep_part, :].astype(F32)
-        bag_low = stack[:n_bag, :]
-        g_v[...] = mul_tn(emb_ref[...], bag_low).astype(BF)
-        direct = stack[n_bag : 2 * n_bag, :].astype(F32)
-        g_table[...] = (direct + mul_nt(bag_low, v_ref[...])).astype(BF)
         for q in range(n_wide):
-            g_wide[:, q * width : (q + 1) * width] = small[q * feat_rows : (q + 1) * feat_rows, :]
+            cols, start = slice(q * width, (q + 1) * width), q * feat_rows
+            g_wide[:, cols] = small[start : start + n_feat, :].astype(BF)
+            g_bias[:, cols] = small[start + n_feat : start + n_feat + 1, :]
         g_rows[...] = jnp.zeros_like(g_rows)
         for i in range(2):
             g_rows[i : i + 1, :] = small[slots[i] : slots[i] + 1, :]
@@ -555,35 +545,45 @@
             def _():
                 g_rows[2:3, :] = small[slots[2 + t] : slots[2 + t] + 1, :]
 
-    grad_table, grad_v, grad_u, g_wide, g_rows = call(
-        table_last_body,
+    g_wide, g_bias, g_rows = call(
+        small_last_body,
+        [shape(n_feat, hidden), shape(1, hidden, F32), shape(8, width, F32)],
+        pieces,
+        "small_last",
+        [pltpu.VMEM((small_rows, width), F32)],
+    )
+    g_bias, g_rows = g_bias.astype(BF), g_rows.astype(BF)
+
+    def last_body(spot, *refs):
+        own, other = refs[:n_rep], refs[n_rep : 2 * n_rep]
+        emb_ref, v_ref, g_table, g_v, g_u, g_second, g_vb, g_ub, bags_all, stack = refs[2 * n_rep :]
+        r, _, c = spot
+        for j in range(n_rep):
+            stack[rows_of(c * n_rep + (r ^ j), dense_part), :] = own[j][:dense_part, :]
+            stack[rows_of((1 - c) * n_rep + (r ^ j), dense_part), :] = other[j][:dense_part, :]
+            g_u[rows_of(r ^ j, u_part), :] = own[j][rep_part : rep_part + u_part, :]
+            bags_all[rows_of(r ^ j, bag_part), :] = own[j][rep_part + u_part :, :]
+        g_second[...] = stack[:hidden, :]
+        g_vb[...] = stack[hidden : hidden + width, :]
+        g_ub[...] = stack[hidden + width : dense_rows, :]
+        bag_low = bags_all[:n_bag, :]
+        g_v[...] = mul_tn(emb_ref[...], bag_low).astype(BF)
+        direct = bags_all[n_bag : 2 * n_bag, :].astype(F32)
+        g_table[...] = (direct + mul_nt(bag_low, v_ref[...])).astype(BF)
+
+    grad_table, grad_v, grad_u, grad_ws, grad_vb, grad_ub = call(
+        last_body,
         [
             shape(n_bag, width),
             shape(width, width),
             shape(width, width),
-            shape(feat_rows, hidden, F32),
-            shape(8, width, F32),
+            shape(hidden, width),
+            shape(width, width),
+            shape(width, width),
         ],
-        (*pieces, emb_rows[0], v_emb),
-        "table_last",
-        [pltpu.VMEM((bag_full, width), BF), pltpu.VMEM((small_rows, width), F32)],
-    )
-    g_wide, g_rows = g_wide.astype(BF), g_rows.astype(BF)
-
-    def dense_last_body(spot, own_ref, other_ref, g_second, g_vb, g_ub, stack):
-        _, _, c = spot
-        stack[rows_of(c, n_rep * dense_part), :] = own_ref[...]
-        stack[rows_of(1 - c, n_rep * dense_part), :] = other_ref[...]
-        g_second[...] = stack[:hidden, :]
-        g_vb[...] = stack[hidden : hidden + width, :]
-        g_ub[...] = stack[hidden + width : dense_rows, :]
-
-    grad_ws, grad_vb, grad_ub = call(
-        dense_last_body,
-        [shape(hidden, width), shape(width, width), shape(width, width)],
-        (dense_own, dense_other),
-        "dense_last",
-        [pltpu.VMEM((2 * n_rep * dense_part, width), BF)],
+        (*pieces, *others, emb_rows[0], v_emb),
+        "last_rows",
+        [pltpu.VMEM((bag_full, width), BF), pltpu.VMEM((2 * n_rep * dense_part, width), BF)],
     )
     return (
         cross_emb,
@@ -595,8 +595,8 @@
         grad_vb,
         grad_ub,
         g_rows[1],
-        g_wide[:n_feat],
-        g_wide[n_feat],
+        g_wide,
+        g_bias[0],
         grad_ws,
         g_rows[0],
     )

time: 70.6 us -> 70.5 us (level)
    ppermute x5 -> x8, waiting for transfers between devices: 2.46 us -> 2.68 us  [swap(): return lax.ppermute(value, 'core', [(0, 1), (1, 0)])]
    pallas_call x17 -> x16, Pallas kernels: 7.37 us -> 7.16 us  [run(): pl.pallas_call(placed, out_shape=out_shapes, in_specs=[in_vmem] * len(arg...]
    unnamed x34 -> x32, local copies, waits for them, and re-layouts: 2.2 us -> 2.2 us
  transfers between devices with their start and end apart: 23 -> 26, of which waited for: 12 -> 13; matrix products, arithmetic and copies ran while one was open for 2% -> 2% of each run, Pallas kernels for 5% -> 5%
where the time goes in v5:
time: 70.5 us; the launch traced here: 70.3 us
  waiting for transfers between devices  32.4 us (46%)
  starting transfers between devices  25.8 us (37%)
  Pallas kernels  7.16 us (10%)
  local copies, waits for them, and re-layouts  3.06 us (4%)
  other arithmetic  0.91 us (1%)
  between operations  0.88 us (1%)
    ppermute x10, waiting for transfers between devices, to_rep(): return lax.ppermute(value, 'rep', [(i, i ^ k) for i in range(n_rep)])  18.3 us
    ppermute x8, starting transfers between devices, to_z(): return lax.ppermute(value, 'z', [(i, i ^ k) for i in range(n_z)])  12.9 us
    ppermute x10, starting transfers between devices, to_rep(): return lax.ppermute(value, 'rep', [(i, i ^ k) for i in range(n_rep)])  12.7 us
    ppermute x8, waiting for transfers between devices, to_z(): return lax.ppermute(value, 'z', [(i, i ^ k) for i in range(n_z)])  11.4 us
    pallas_call x16, Pallas kernels, run(): pl.pallas_call(placed, out_shape=out_shapes, in_specs=[in_vmem] * len(arg...  7.16 us
    ppermute x8, waiting for transfers between devices, swap(): return lax.ppermute(value, 'core', [(0, 1), (1, 0)])  2.68 us
    unnamed x32, local copies, waits for them, and re-layouts  2.2 us
  transfers between devices with their start and end apart: 26, of which 13 were waited for; matrix products, arithmetic and copies ran while one was open for 2% of the time, Pallas kernels for 5%

profile of v5, /device:TPU:0, one launch (start us, length us, event | category | flops | bytes accessed | tf_op | source)
XLA Modules:
  0.0 70.3 jit_solution(6714899818606132262)
XLA Ops:
  1.8 3.1 %collective-permute-start.3 = (bf16[64,256]{1,0:T(8,128)(2,1)S(1)}, bf16[64,256]{1,0:T(8,128)(2,1)S(1)}, u32[]{:S(2)}, u32[]{:S(2)}) collective-permute-start(bf16[64,256]{1,0:T(8,128)(2,1)S(1)} %u_cut.1), channel_id=1, source_target_pairs={{0,2},{2,0},{4,6},{6,4},{1,3},{3,1},{5,7},{7,5},{8,10},{10,8},{12,... | collective-permute-start | bytes 98312 | tf_op jit(solution)/shard_map/ppermute | solution.py:123
  4.9 2.6 %collective-permute-start.4 = (bf16[64,256]{1,0:T(8,128)(2,1)S(1)}, bf16[64,256]{1,0:T(8,128)(2,1)S(1)}, u32[]{:S(2)}, u32[]{:S(2)}) collective-permute-start(bf16[64,256]{1,0:T(8,128)(2,1)S(1)} %u_cut.1), channel_id=1, source_target_pairs={{0,4},{2,6},{4,0},{6,2},{1,5},{3,7},{5,1},{7,3},{8,12},{10,14},{12... | collective-permute-start | bytes 98312 | tf_op jit(solution)/shard_map/ppermute | solution.py:123
  7.7 1.0 %collective-permute-start = (bf16[208,256]{1,0:T(8,128)(2,1)S(1)}, bf16[208,256]{1,0:T(8,128)(2,1)S(1)}, u32[]{:S(2)}, u32[]{:S(2)}) collective-permute-start(bf16[208,256]{1,0:T(8,128)(2,1)S(1)} %get-tuple-element.58), channel_id=1, source_target_pairs={{0,2},{2,0},{4,6},{6,4},{1,3},{3,1},{5,7},{7,5},{8,10},{10,8},{12,... | collective-permute-start | bytes 319496 | tf_op jit(solution)/shard_map/ppermute | solution.py:123
  8.6 3.5 %collective-permute-start.1 = (bf16[208,256]{1,0:T(8,128)(2,1)S(1)}, bf16[208,256]{1,0:T(8,128)(2,1)S(1)}, u32[]{:S(2)}, u32[]{:S(2)}) collective-permute-start(bf16[208,256]{1,0:T(8,128)(2,1)S(1)} %get-tuple-element.59), channel_id=1, source_target_pairs={{0,4},{2,6},{4,0},{6,2},{1,5},{3,7},{5,1},{7,3},{8,12},{10,14},{12... | collective-permute-start | bytes 319496 | tf_op jit(solution)/shard_map/ppermute | solution.py:123
  14.1 1.7 %collective-permute-start.6 = (bf16[192,256]{1,0:T(8,128)(2,1)S(1)}, bf16[192,256]{1,0:T(8,128)(2,1)S(1)}, u32[]{:S(2)}, u32[]{:S(2)}) collective-permute-start(bf16[192,256]{1,0:T(8,128)(2,1)S(1)} %u_rows.1.refs_5_), channel_id=1, source_target_pairs={{0,8},{8,0},{16,24},{24,16},{1,9},{9,1},{17,25},{25,17},{2,10},{10... | collective-permute-start | bytes 294920 | tf_op jit(solution)/shard_map/ppermute | solution.py:126
  15.8 1.5 %collective-permute-start.7 = (bf16[192,256]{1,0:T(8,128)(2,1)S(1)}, bf16[192,256]{1,0:T(8,128)(2,1)S(1)}, u32[]{:S(2)}, u32[]{:S(2)}) collective-permute-start(bf16[192,256]{1,0:T(8,128)(2,1)S(1)} %u_rows.1.refs_5_), channel_id=1, source_target_pairs={{0,16},{8,24},{16,0},{24,8},{1,17},{9,25},{17,1},{25,9},{2,18},{10... | collective-permute-start | bytes 294920 | tf_op jit(solution)/shard_map/ppermute | solution.py:126
  17.3 1.7 %collective-permute-start.8 = (bf16[192,256]{1,0:T(8,128)(2,1)S(1)}, bf16[192,256]{1,0:T(8,128)(2,1)S(1)}, u32[]{:S(2)}, u32[]{:S(2)}) collective-permute-start(bf16[192,256]{1,0:T(8,128)(2,1)S(1)} %u_rows.1.refs_5_), channel_id=1, source_target_pairs={{0,24},{8,16},{16,8},{24,0},{1,25},{9,17},{17,9},{25,1},{2,26},{10... | collective-permute-start | bytes 294920 | tf_op jit(solution)/shard_map/ppermute | solution.py:126
  19.9 1.3 %collective-permute-done.2.refs_3_ = bf16[208,256]{1,0:T(8,128)(2,1)S(1)} collective-permute-done((bf16[208,256]{1,0:T(8,128)(2,1)S(1)}, bf16[208,256]{1,0:T(8,128)(2,1)S(1)}, u32[]{:S(2)}, u32[]{:S(2)}) %collective-permute-start.2) | collective-permute-done | bytes 106528 | tf_op jit(solution)/shard_map/ppermute | solution.py:123
  21.7 1.1 %collective-permute-done.8.refs_8_ = bf16[192,256]{1,0:T(8,128)(2,1)S(1)} collective-permute-done((bf16[192,256]{1,0:T(8,128)(2,1)S(1)}, bf16[192,256]{1,0:T(8,128)(2,1)S(1)}, u32[]{:S(2)}, u32[]{:S(2)}) %collective-permute-start.8) | collective-permute-done | bytes 98336 | tf_op jit(solution)/shard_map/ppermute | solution.py:126
  23.8 1.5 %collective-permute-done.10.refs_6_.refs_1_ = bf16[512,256]{1,0:T(8,128)(2,1)S(1)} collective-permute-done((bf16[512,256]{1,0:T(8,128)(2,1)S(1)}, bf16[512,256]{1,0:T(8,128)(2,1)S(1)}, u32[]{:S(2)}, u32[]{:S(2)}) %collective-permute-start.10) | collective-permute-done | bytes 262176 | tf_op jit(solution)/shard_map/ppermute | solution.py:120
  25.3 1.5 %dense_grads.1 = (bf16[128,256]{1,0:T(8,128)(2,1)}, bf16[832,256]{1,0:T(8,128)(2,1)S(1)}, bf16[832,256]{1,0:T(8,128)(2,1)S(1)}) custom-call(s32[8,128]{1,0:T(8,128)S(1)} %broadcast_in_dim.32.spot_ref, bf16[512,256]{1,0:T(8,128)(2,1)S(1)} %get-tuple-element.64.refs_5_.refs_0_, bf16[512,256]{1,0:T(8,128)(2,1)S(1)} %collective-permute-done.10.refs_6_.refs_1_, ...), custom_call_target="tpu_custom_call" | custom-call | flops 100000000 | bytes 3301376 | tf_op jit(solution)/shard_map/dense_grads/pallas_call | solution.py:58
  28.7 1.4 %collective-permute-start.14 = (bf16[608,256]{1,0:T(8,128)(2,1)S(1)}, bf16[608,256]{1,0:T(8,128)(2,1)S(1)}, u32[]{:S(2)}, u32[]{:S(2)}) collective-permute-start(bf16[608,256]{1,0:T(8,128)(2,1)S(1)} %get-tuple-element.84), channel_id=1, source_target_pairs={{0,16},{8,24},{16,0},{24,8},{1,17},{9,25},{17,1},{25,9},{2,18},{10... | collective-permute-start | bytes 933896 | tf_op jit(solution)/shard_map/ppermute | solution.py:126
  31.1 7.8 %collective-permute-done.13.refs_1_ = bf16[576,256]{1,0:T(8,128)(2,1)S(1)} collective-permute-done((bf16[576,256]{1,0:T(8,128)(2,1)S(1)}, bf16[576,256]{1,0:T(8,128)(2,1)S(1)}, u32[]{:S(2)}, u32[]{:S(2)}) %collective-permute-start.13) | collective-permute-done | bytes 294944 | tf_op jit(solution)/shard_map/ppermute | solution.py:126
  39.0 1.0 %collective-permute-start.16 = (bf16[304,256]{1,0:T(8,128)(2,1)S(1)}, bf16[304,256]{1,0:T(8,128)(2,1)S(1)}, u32[]{:S(2)}, u32[]{:S(2)}) collective-permute-start(bf16[304,256]{1,0:T(8,128)(2,1)S(1)} %get-tuple-element.87), channel_id=1, source_target_pairs={{0,8},{8,0},{16,24},{24,16},{1,9},{9,1},{17,25},{25,17},{2,10},{10... | collective-permute-start | bytes 466952 | tf_op jit(solution)/shard_map/ppermute | solution.py:126
  40.8 4.4 %collective-permute-done.15.refs_1_ = bf16[288,256]{1,0:T(8,128)(2,1)S(1)} collective-permute-done((bf16[288,256]{1,0:T(8,128)(2,1)S(1)}, bf16[288,256]{1,0:T(8,128)(2,1)S(1)}, u32[]{:S(2)}, u32[]{:S(2)}) %collective-permute-start.15) | collective-permute-done | bytes 147488 | tf_op jit(solution)/shard_map/ppermute | solution.py:126
  45.9 5.2 %collective-permute-done.17.refs_1_ = bf16[400,256]{1,0:T(8,128)(2,1)S(1)} collective-permute-done((bf16[400,256]{1,0:T(8,128)(2,1)S(1)}, bf16[400,256]{1,0:T(8,128)(2,1)S(1)}, u32[]{:S(2)}, u32[]{:S(2)}) %collective-permute-start.17) | collective-permute-done | bytes 204832 | tf_op jit(solution)/shard_map/ppermute | solution.py:123
  51.1 2.1 %collective-permute-start.18 = (bf16[304,256]{1,0:T(8,128)(2,1)S(1)}, bf16[304,256]{1,0:T(8,128)(2,1)S(1)}, u32[]{:S(2)}, u32[]{:S(2)}) collective-permute-start(bf16[304,256]{1,0:T(8,128)(2,1)S(1)} %get-tuple-element.91), channel_id=1, source_target_pairs={{0,4},{2,6},{4,0},{6,2},{1,5},{3,7},{5,1},{7,3},{8,12},{10,14},{12... | collective-permute-start | bytes 466952 | tf_op jit(solution)/shard_map/ppermute | solution.py:123
  54.1 4.9 %collective-permute-done.18.refs_2_ = bf16[304,256]{1,0:T(8,128)(2,1)S(1)} collective-permute-done((bf16[304,256]{1,0:T(8,128)(2,1)S(1)}, bf16[304,256]{1,0:T(8,128)(2,1)S(1)}, u32[]{:S(2)}, u32[]{:S(2)}) %collective-permute-start.18) | collective-permute-done | bytes 155680 | tf_op jit(solution)/shard_map/ppermute | solution.py:123
  59.1 1.1 %collective-permute-start.19 = (bf16[304,256]{1,0:T(8,128)(2,1)S(1)}, bf16[304,256]{1,0:T(8,128)(2,1)S(1)}, u32[]{:S(2)}, u32[]{:S(2)}) collective-permute-start(bf16[304,256]{1,0:T(8,128)(2,1)S(1)} %z_sum.1.refs_0_), channel_id=1, source_target_pairs={{0,8},{8,0},{16,24},{24,16},{1,9},{9,1},{17,25},{25,17},{2,10},{10... | collective-permute-start | bytes 466952 | tf_op jit(solution)/shard_map/ppermute | solution.py:126
  60.9 1.7 %collective-permute-start.21 = (bf16[304,256]{1,0:T(8,128)(2,1)S(1)}, bf16[304,256]{1,0:T(8,128)(2,1)S(1)}, u32[]{:S(2)}, u32[]{:S(2)}) collective-permute-start(bf16[304,256]{1,0:T(8,128)(2,1)S(1)} %z_sum.1.refs_0_), channel_id=1, source_target_pairs={{0,24},{8,16},{16,8},{24,0},{1,25},{9,17},{17,9},{25,1},{2,26},{10... | collective-permute-start | bytes 466952 | tf_op jit(solution)/shard_map/ppermute | solution.py:126
  62.6 1.7 %collective-permute-done.19.refs_1_ = bf16[304,256]{1,0:T(8,128)(2,1)S(1)} collective-permute-done((bf16[304,256]{1,0:T(8,128)(2,1)S(1)}, bf16[304,256]{1,0:T(8,128)(2,1)S(1)}, u32[]{:S(2)}, u32[]{:S(2)}) %collective-permute-start.19) | collective-permute-done | bytes 155680 | tf_op jit(solution)/shard_map/ppermute | solution.py:126
  64.4 1.1 %collective-permute-done.20.refs_2_ = bf16[304,256]{1,0:T(8,128)(2,1)S(1)} collective-permute-done((bf16[304,256]{1,0:T(8,128)(2,1)S(1)}, bf16[304,256]{1,0:T(8,128)(2,1)S(1)}, u32[]{:S(2)}, u32[]{:S(2)}) %collective-permute-start.20) | collective-permute-done | bytes 155680 | tf_op jit(solution)/shard_map/ppermute | solution.py:126
  65.4 1.7 %collective-permute-done.21.refs_3_ = bf16[304,256]{1,0:T(8,128)(2,1)S(1)} collective-permute-done((bf16[304,256]{1,0:T(8,128)(2,1)S(1)}, bf16[304,256]{1,0:T(8,128)(2,1)S(1)}, u32[]{:S(2)}, u32[]{:S(2)}) %collective-permute-start.21) | collective-permute-done | bytes 155680 | tf_op jit(solution)/shard_map/ppermute | solution.py:126
  69.2 1.1 %last_rows.1 = (bf16[64,256]{1,0:T(8,128)(2,1)}, bf16[256,256]{1,0:T(8,128)(2,1)}, bf16[256,256]{1,0:T(8,128)(2,1)}, bf16[1024,256]{1,0:T(8,128)(2,1)}, bf16[256...) custom-call(s32[8,128]{1,0:T(8,128)S(1)} %broadcast_in_dim.32.spot_ref, bf16[304,256]{1,0:T(8,128)(2,1)S(1)} %z_sum.1.refs_0_, ...), custom_call_target="tpu_custom_call" | custom-call | flops 100000000 | bytes 2494464 | tf_op jit(solution)/shard_map/last_rows/pallas_call | solution.py:58
  (94 shorter events, 13.6 us)
Async XLA Ops:
  1.8 11.9 %collective-permute-start.3 = (bf16[64,256]{1,0:T(8,128)(2,1)S(1)}, bf16[64,256]{1,0:T(8,128)(2,1)S(1)}, u32[]{:S(2)}, u32[]{:S(2)}) collective-permute-start(bf16[64,256]{1,0:T(8,128)(2,1)S(1)} %u_cut.1), channel_id=1, source_target_pairs={{0,2},{2,0},{4,6},{6,4},{1,3},{3,1},{5,7},{7,5},{8,10},{10,8},{12,... | collective-permute-start | bytes 98312 | tf_op jit(solution)/shard_map/ppermute | solution.py:123
  4.9 9.1 %collective-permute-start.4 = (bf16[64,256]{1,0:T(8,128)(2,1)S(1)}, bf16[64,256]{1,0:T(8,128)(2,1)S(1)}, u32[]{:S(2)}, u32[]{:S(2)}) collective-permute-start(bf16[64,256]{1,0:T(8,128)(2,1)S(1)} %u_cut.1), channel_id=1, source_target_pairs={{0,4},{2,6},{4,0},{6,2},{1,5},{3,7},{5,1},{7,3},{8,12},{10,14},{12... | collective-permute-start | bytes 98312 | tf_op jit(solution)/shard_map/ppermute | solution.py:123
  7.5 6.6 %collective-permute-start.5 = (bf16[64,256]{1,0:T(8,128)(2,1)S(1)}, bf16[64,256]{1,0:T(8,128)(2,1)S(1)}, u32[]{:S(2)}, u32[]{:S(2)}) collective-permute-start(bf16[64,256]{1,0:T(8,128)(2,1)S(1)} %u_cut.1), channel_id=1, source_target_pairs={{0,6},{2,4},{4,2},{6,0},{1,7},{3,5},{5,3},{7,1},{8,14},{10,12},{12... | collective-permute-start | bytes 98312 | tf_op jit(solution)/shard_map/ppermute | solution.py:123
  7.7 8.1 %collective-permute-start = (bf16[208,256]{1,0:T(8,128)(2,1)S(1)}, bf16[208,256]{1,0:T(8,128)(2,1)S(1)}, u32[]{:S(2)}, u32[]{:S(2)}) collective-permute-start(bf16[208,256]{1,0:T(8,128)(2,1)S(1)} %get-tuple-element.58), channel_id=1, source_target_pairs={{0,2},{2,0},{4,6},{6,4},{1,3},{3,1},{5,7},{7,5},{8,10},{10,8},{12,... | collective-permute-start | bytes 319496 | tf_op jit(solution)/shard_map/ppermute | solution.py:123
  8.6 8.7 %collective-permute-start.1 = (bf16[208,256]{1,0:T(8,128)(2,1)S(1)}, bf16[208,256]{1,0:T(8,128)(2,1)S(1)}, u32[]{:S(2)}, u32[]{:S(2)}) collective-permute-start(bf16[208,256]{1,0:T(8,128)(2,1)S(1)} %get-tuple-element.59), channel_id=1, source_target_pairs={{0,4},{2,6},{4,0},{6,2},{1,5},{3,7},{5,1},{7,3},{8,12},{10,14},{12... | collective-permute-start | bytes 319496 | tf_op jit(solution)/shard_map/ppermute | solution.py:123
  13.7 9.1 %collective-permute-start.9 = (bf16[128,1024]{1,0:T(8,128)(2,1)S(1)}, bf16[128,1024]{1,0:T(8,128)(2,1)S(1)}, u32[]{:S(2)}, u32[]{:S(2)}) collective-permute-start(bf16[128,1024]{1,0:T(8,128)(2,1)S(1)} %cot_send.1), channel_id=1, source_target_pairs={{0,1},{1,0},{2,3},{3,2},{4,5},{5,4},{6,7},{7,6},{8,9},{9,8},{10,11... | collective-permute-start | bytes 786440 | tf_op jit(solution)/shard_map/ppermute | solution.py:120
  14.0 7.2 %collective-permute-start.2 = (bf16[208,256]{1,0:T(8,128)(2,1)S(1)}, bf16[208,256]{1,0:T(8,128)(2,1)S(1)}, u32[]{:S(2)}, u32[]{:S(2)}) collective-permute-start(bf16[208,256]{1,0:T(8,128)(2,1)S(1)} %get-tuple-element.60), channel_id=1, source_target_pairs={{0,6},{2,4},{4,2},{6,0},{1,7},{3,5},{5,3},{7,1},{8,14},{10,12},{12... | collective-permute-start | bytes 319496 | tf_op jit(solution)/shard_map/ppermute | solution.py:123
  14.1 7.1 %collective-permute-start.6 = (bf16[192,256]{1,0:T(8,128)(2,1)S(1)}, bf16[192,256]{1,0:T(8,128)(2,1)S(1)}, u32[]{:S(2)}, u32[]{:S(2)}) collective-permute-start(bf16[192,256]{1,0:T(8,128)(2,1)S(1)} %u_rows.1.refs_5_), channel_id=1, source_target_pairs={{0,8},{8,0},{16,24},{24,16},{1,9},{9,1},{17,25},{25,17},{2,10},{10... | collective-permute-start | bytes 294920 | tf_op jit(solution)/shard_map/ppermute | solution.py:126
  15.8 5.9 %collective-permute-start.7 = (bf16[192,256]{1,0:T(8,128)(2,1)S(1)}, bf16[192,256]{1,0:T(8,128)(2,1)S(1)}, u32[]{:S(2)}, u32[]{:S(2)}) collective-permute-start(bf16[192,256]{1,0:T(8,128)(2,1)S(1)} %u_rows.1.refs_5_), channel_id=1, source_target_pairs={{0,16},{8,24},{16,0},{24,8},{1,17},{9,25},{17,1},{25,9},{2,18},{10... | collective-permute-start | bytes 294920 | tf_op jit(solution)/shard_map/ppermute | solution.py:126
  17.3 5.5 %collective-permute-start.8 = (bf16[192,256]{1,0:T(8,128)(2,1)S(1)}, bf16[192,256]{1,0:T(8,128)(2,1)S(1)}, u32[]{:S(2)}, u32[]{:S(2)}) collective-permute-start(bf16[192,256]{1,0:T(8,128)(2,1)S(1)} %u_rows.1.refs_5_), channel_id=1, source_target_pairs={{0,24},{8,16},{16,8},{24,0},{1,25},{9,17},{17,9},{25,1},{2,26},{10... | collective-permute-start | bytes 294920 | tf_op jit(solution)/shard_map/ppermute | solution.py:126
  26.7 1.8 %collective-permute-start.12 = (bf16[832,256]{1,0:T(8,128)(2,1)S(1)}, bf16[832,256]{1,0:T(8,128)(2,1)S(1)}, u32[]{:S(2)}, u32[]{:S(2)}) collective-permute-start(bf16[832,256]{1,0:T(8,128)(2,1)S(1)} %get-tuple-element.78), channel_id=1, source_target_pairs={{0,1},{1,0},{2,3},{3,2},{4,5},{5,4},{6,7},{7,6},{8,9},{9,8},{10,11... | collective-permute-start | bytes 1277960 | tf_op jit(solution)/shard_map/ppermute | solution.py:120
  28.7 10.2 %collective-permute-start.14 = (bf16[608,256]{1,0:T(8,128)(2,1)S(1)}, bf16[608,256]{1,0:T(8,128)(2,1)S(1)}, u32[]{:S(2)}, u32[]{:S(2)}) collective-permute-start(bf16[608,256]{1,0:T(8,128)(2,1)S(1)} %get-tuple-element.84), channel_id=1, source_target_pairs={{0,16},{8,24},{16,0},{24,8},{1,17},{9,25},{17,1},{25,9},{2,18},{10... | collective-permute-start | bytes 933896 | tf_op jit(solution)/shard_map/ppermute | solution.py:126
  30.1 8.8 %collective-permute-start.13 = (bf16[576,256]{1,0:T(8,128)(2,1)S(1)}, bf16[576,256]{1,0:T(8,128)(2,1)S(1)}, u32[]{:S(2)}, u32[]{:S(2)}) collective-permute-start(bf16[576,256]{1,0:T(8,128)(2,1)S(1)} %get-tuple-element.82), channel_id=1, source_target_pairs={{0,8},{8,0},{16,24},{24,16},{1,9},{9,1},{17,25},{25,17},{2,10},{10... | collective-permute-start | bytes 884744 | tf_op jit(solution)/shard_map/ppermute | solution.py:126
  39.0 6.2 %collective-permute-start.16 = (bf16[304,256]{1,0:T(8,128)(2,1)S(1)}, bf16[304,256]{1,0:T(8,128)(2,1)S(1)}, u32[]{:S(2)}, u32[]{:S(2)}) collective-permute-start(bf16[304,256]{1,0:T(8,128)(2,1)S(1)} %get-tuple-element.87), channel_id=1, source_target_pairs={{0,8},{8,0},{16,24},{24,16},{1,9},{9,1},{17,25},{25,17},{2,10},{10... | collective-permute-start | bytes 466952 | tf_op jit(solution)/shard_map/ppermute | solution.py:126
  40.0 5.1 %collective-permute-start.15 = (bf16[288,256]{1,0:T(8,128)(2,1)S(1)}, bf16[288,256]{1,0:T(8,128)(2,1)S(1)}, u32[]{:S(2)}, u32[]{:S(2)}) collective-permute-start(bf16[288,256]{1,0:T(8,128)(2,1)S(1)} %get-tuple-element.86), channel_id=1, source_target_pairs={{0,16},{8,24},{16,0},{24,8},{1,17},{9,25},{17,1},{25,9},{2,18},{10... | collective-permute-start | bytes 442376 | tf_op jit(solution)/shard_map/ppermute | solution.py:126
  45.3 5.8 %collective-permute-start.17 = (bf16[400,256]{1,0:T(8,128)(2,1)S(1)}, bf16[400,256]{1,0:T(8,128)(2,1)S(1)}, u32[]{:S(2)}, u32[]{:S(2)}) collective-permute-start(bf16[400,256]{1,0:T(8,128)(2,1)S(1)} %get-tuple-element.89), channel_id=1, source_target_pairs={{0,2},{2,0},{4,6},{6,4},{1,3},{3,1},{5,7},{7,5},{8,10},{10,8},{12,... | collective-permute-start | bytes 614408 | tf_op jit(solution)/shard_map/ppermute | solution.py:123
  45.8 7.4 %collective-permute-start.11 = (bf16[128,1024]{1,0:T(8,128)(2,1)S(1)}, bf16[128,1024]{1,0:T(8,128)(2,1)S(1)}, u32[]{:S(2)}, u32[]{:S(2)}) collective-permute-start(bf16[128,1024]{1,0:T(8,128)(2,1)S(1)} %get-tuple-element.68), channel_id=1, source_target_pairs={{0,1},{1,0},{2,3},{3,2},{4,5},{5,4},{6,7},{7,6},{8,9},{9,8},{10,11... | collective-permute-start | bytes 786440 | tf_op jit(solution)/shard_map/ppermute | solution.py:120
  51.1 7.9 %collective-permute-start.18 = (bf16[304,256]{1,0:T(8,128)(2,1)S(1)}, bf16[304,256]{1,0:T(8,128)(2,1)S(1)}, u32[]{:S(2)}, u32[]{:S(2)}) collective-permute-start(bf16[304,256]{1,0:T(8,128)(2,1)S(1)} %get-tuple-element.91), channel_id=1, source_target_pairs={{0,4},{2,6},{4,0},{6,2},{1,5},{3,7},{5,1},{7,3},{8,12},{10,14},{12... | collective-permute-start | bytes 466952 | tf_op jit(solution)/shard_map/ppermute | solution.py:123
  59.1 5.3 %collective-permute-start.19 = (bf16[304,256]{1,0:T(8,128)(2,1)S(1)}, bf16[304,256]{1,0:T(8,128)(2,1)S(1)}, u32[]{:S(2)}, u32[]{:S(2)}) collective-permute-start(bf16[304,256]{1,0:T(8,128)(2,1)S(1)} %z_sum.1.refs_0_), channel_id=1, source_target_pairs={{0,8},{8,0},{16,24},{24,16},{1,9},{9,1},{17,25},{25,17},{2,10},{10... | collective-permute-start | bytes 466952 | tf_op jit(solution)/shard_map/ppermute | solution.py:126
  60.2 5.2 %collective-permute-start.20 = (bf16[304,256]{1,0:T(8,128)(2,1)S(1)}, bf16[304,256]{1,0:T(8,128)(2,1)S(1)}, u32[]{:S(2)}, u32[]{:S(2)}) collective-permute-start(bf16[304,256]{1,0:T(8,128)(2,1)S(1)} %z_sum.1.refs_0_), channel_id=1, source_target_pairs={{0,16},{8,24},{16,0},{24,8},{1,17},{9,25},{17,1},{25,9},{2,18},{10... | collective-permute-start | bytes 466952 | tf_op jit(solution)/shard_map/ppermute | solution.py:126
  60.9 6.2 %collective-permute-start.21 = (bf16[304,256]{1,0:T(8,128)(2,1)S(1)}, bf16[304,256]{1,0:T(8,128)(2,1)S(1)}, u32[]{:S(2)}, u32[]{:S(2)}) collective-permute-start(bf16[304,256]{1,0:T(8,128)(2,1)S(1)} %z_sum.1.refs_0_), channel_id=1, source_target_pairs={{0,24},{8,16},{16,8},{24,0},{1,25},{9,17},{17,9},{25,1},{2,26},{10... | collective-permute-start | bytes 466952 | tf_op jit(solution)/shard_map/ppermute | solution.py:126
  62.6 6.3 %collective-permute-start.22 = (bf16[304,256]{1,0:T(8,128)(2,1)S(1)}, bf16[304,256]{1,0:T(8,128)(2,1)S(1)}, u32[]{:S(2)}, u32[]{:S(2)}) collective-permute-start(bf16[304,256]{1,0:T(8,128)(2,1)S(1)} %z_sum.1.refs_0_), channel_id=1, source_target_pairs={{0,1},{1,0},{2,3},{3,2},{4,5},{5,4},{6,7},{7,6},{8,9},{9,8},{10,11... | collective-permute-start | bytes 466952 | tf_op jit(solution)/shard_map/ppermute | solution.py:120
  64.4 4.6 %collective-permute-start.23 = (bf16[304,256]{1,0:T(8,128)(2,1)S(1)}, bf16[304,256]{1,0:T(8,128)(2,1)S(1)}, u32[]{:S(2)}, u32[]{:S(2)}) collective-permute-start(bf16[304,256]{1,0:T(8,128)(2,1)S(1)} %collective-permute-done.19.refs_1_), channel_id=1, source_target_pairs={{0,1},{1,0},{2,3},{3,2},{4,5},{5,4},{6,7},{7,6},{8,9},{9,8},{10,11... | collective-permute-start | bytes 466952 | tf_op jit(solution)/shard_map/ppermute | solution.py:120
  65.4 3.5 %collective-permute-start.24 = (bf16[304,256]{1,0:T(8,128)(2,1)S(1)}, bf16[304,256]{1,0:T(8,128)(2,1)S(1)}, u32[]{:S(2)}, u32[]{:S(2)}) collective-permute-start(bf16[304,256]{1,0:T(8,128)(2,1)S(1)} %collective-permute-done.20.refs_2_), channel_id=1, source_target_pairs={{0,1},{1,0},{2,3},{3,2},{4,5},{5,4},{6,7},{7,6},{8,9},{9,8},{10,11... | collective-permute-start | bytes 466952 | tf_op jit(solution)/shard_map/ppermute | solution.py:120
  (18 other events, 90.9 us)
